TPU v7x, 32 devices: a whole 2x2x4 slice. The times are simulated.
32 devices in a mesh: tok: 8 (over z, x), head: 4 (over y, core).
Axes of the slice: x: 2, y: 2, z: 4, core: 2. Of those that a mesh axis runs over, the one named last changes fastest.
Arguments:
- tokens: bfloat16 [2048, 2880], P(('tok', 'head')), may hold values from -6 to 6
- lengths: int32 [4], replicated, may hold values from 1 to 1024, 1920 in all
- norm_gain_attn: float32 [2880], replicated, may hold values from 0.1 to 1.9
- query_key_value_weight: bfloat16 [2880, 5120], P(None, 'head'), may hold values from -0.109375 to 0.109375
- sinks: float32 [64], P('head'), may hold values from 1 to 6
- w_out_attn: bfloat16 [4096, 2880], P('head'), may hold values from -0.09375 to 0.09375
- norm_gain_moe: float32 [2880], replicated, may hold values from 0.1 to 1.9
- routes: int32 [2048, 4], P(('tok', 'head')), may hold values from 0 to 31, all different within a row; in each aligned block of 64 rows (0 to 63, 64 to 127, ...) at most 10 rows name the same one
- gates: float32 [2048, 4], P(('tok', 'head')), may hold values from 0.1 to 1
- w_in: bfloat16 [32, 2880, 5760], P(('tok', 'head')), may hold values from -0.109375 to 0.109375
- w_down: bfloat16 [32, 2880, 2880], P(('tok', 'head')), may hold values from -0.109375 to 0.109375
- page_table: int32 [128], replicated, may hold values from 0 to 127, as said below
Outputs:
- hidden_out: bfloat16 [2048, 2880], P(('tok', 'head'))
- kv_cache: bfloat16 [8, 128, 16, 128], P('head', 'tok')
Inputs may be any that keep to these rules, and one draw needn't show every extreme that they name: `routes`: every row names 4 different experts. In each aligned block of 64 rows no expert is named by more than 10 rows, and in every draw some block has an expert named by exactly 10 rows. `lengths`: they sum to 1920, and the longest is exactly 1024. `page_table`: A permutation. Of the 16 logical pages in each aligned block of 16, exactly 2 map into each aligned block of 16 physical pages.
All inputs are finite; a program needn't handle non-finite values.
Results may differ from a plain program's by a relative error of at most 0.018.
Values may be sent and summed in bfloat16 or wider, within the bound.
No kernel may reach another device: no remote copies, remote signals or barrier semaphores. Data moves between devices by JAX's collectives and lax.ppermute only.
A program may use at most 128 MiB of HBM per device.

v0:
```python
import math

import jax
import jax.numpy as jnp
from jax import lax
from jax.sharding import PartitionSpec as P

MODEL_WIDTH = 2880
HEAD_SIZE = 64
EXPERTS = 32
ATTEND_WINDOW = 128
NSEQ = 4
PAGE_TOKENS = 16
QUERY_PER_KEY = 8


EPSILON = 1e-05
ROPE_BASE = 150000.0
GLU_ALPHA = 1.702


def passed_along(array, axis, by):
    peers = lax.axis_size(axis)
    pairs = [(i, i + by) for i in range(peers) if 0 <= i + by < peers]
    return lax.ppermute(array, axis, pairs)


def normalize(values, gain_vec):
    wide = values.astype(jnp.float32)
    inv_rms = lax.rsqrt(jnp.mean(wide * wide, axis=-1, keepdims=True) + EPSILON)
    return wide * inv_rms * gain_vec


def segment_table(lengths, row_index):
    seq_ends = jnp.cumsum(lengths)
    starts = jnp.concatenate([jnp.zeros((1,), jnp.int32), seq_ends])
    segment = jnp.sum((row_index[:, None] >= seq_ends[None, :]).astype(jnp.int32), axis=1)
    onehot = segment[:, None] == jnp.arange(starts.shape[0], dtype=jnp.int32)[None, :]
    seg_start = jnp.sum(jnp.where(onehot, starts[None, :], 0), axis=1)
    return (segment, row_index - seg_start)


def rotate(values, positions):
    half_dim = values.shape[-1] // 2
    inv_freq = jnp.exp(
        jnp.arange(half_dim, dtype=jnp.float32) * (-2.0 * math.log(ROPE_BASE) / values.shape[-1])
    )
    angles = positions.astype(jnp.float32)[:, None] * inv_freq[None, :]
    view_shape = (angles.shape[0],) + (1,) * (values.ndim - 2) + (half_dim,)
    cos_table = jnp.cos(angles).reshape(view_shape)
    sin_table = jnp.sin(angles).reshape(view_shape)
    lower_half = values[..., :half_dim]
    upper_half = values[..., half_dim:]
    return jnp.concatenate(
        [
            lower_half * cos_table - upper_half * sin_table,
            upper_half * cos_table + lower_half * sin_table,
        ],
        axis=-1,
    )


def band_mask(query_index, key_index, query_segs, key_segs, window):
    nblocks = query_index.shape[0] // window
    query_pos = query_index.reshape(nblocks, window)
    query_seg = query_segs.reshape(nblocks, window)
    key_grid = key_index.reshape(nblocks + 1, window)
    seg_grid = key_segs.reshape(nblocks + 1, window)
    key_pos = jnp.concatenate([key_grid[:-1], key_grid[1:]], axis=1)
    key_seg = jnp.concatenate([seg_grid[:-1], seg_grid[1:]], axis=1)
    distance = query_pos[:, :, None] - key_pos[:, None, :]
    allowed = (query_seg[:, :, None] == key_seg[:, None, :]) & (query_seg < NSEQ)[:, :, None]
    allowed = allowed & (key_pos >= 0)[:, None, :] & (distance >= 0) & (distance < window)
    return allowed


def band_attention(query_rows, extended, sink_table, allowed):
    nblocks = allowed.shape[0]
    groups = sink_table.shape[0]
    query_blocks = query_rows.reshape(nblocks, ATTEND_WINDOW, groups, QUERY_PER_KEY, HEAD_SIZE)
    pair_grid = extended.reshape(nblocks + 1, ATTEND_WINDOW, groups, 2 * HEAD_SIZE)
    key_band = jnp.concatenate([pair_grid[:-1], pair_grid[1:]], axis=1)
    scores = jnp.einsum(
        "bqgnh,bkgh->bgnqk",
        query_blocks,
        key_band[..., :HEAD_SIZE],
        preferred_element_type=jnp.float32,
    )
    weights = jnp.where(allowed[:, None, None], jnp.exp(scores), 0.0)
    totals = jnp.sum(weights, axis=-1, keepdims=True) + jnp.exp(sink_table)[None, :, :, None, None]
    probs_bf = (weights / totals).astype(jnp.bfloat16)
    outputs = jnp.einsum(
        "bgnqk,bkgh->bqgnh", probs_bf, key_band[..., HEAD_SIZE:], preferred_element_type=jnp.float32
    )
    return outputs.astype(jnp.bfloat16).reshape(
        nblocks * ATTEND_WINDOW, groups * QUERY_PER_KEY * HEAD_SIZE
    )


def expert_mlp(rows_in, w_in_local, w_down_local):
    ffs_local = w_down_local.shape[0]
    gate_up = jnp.dot(rows_in, w_in_local, preferred_element_type=jnp.float32)
    gate_part = gate_up[:, :ffs_local]
    up_part = gate_up[:, ffs_local:]
    activated = ((up_part + 1.0) * gate_part * jax.nn.sigmoid(GLU_ALPHA * gate_part)).astype(
        jnp.bfloat16
    )
    return jnp.dot(activated, w_down_local, preferred_element_type=jnp.float32).astype(jnp.bfloat16)


def copied_route(outgoing, route, width_split, slots, w_in_local, w_down_local):
    spread = jnp.broadcast_to(
        outgoing[:, None], (EXPERTS, width_split, slots, MODEL_WIDTH)
    ).reshape(EXPERTS * width_split, slots, MODEL_WIDTH)
    incoming = route(spread)
    produced = expert_mlp(incoming.reshape(-1, MODEL_WIDTH), w_in_local, w_down_local).reshape(
        spread.shape
    )
    returned = route(produced)
    return jnp.sum(
        returned.astype(jnp.float32).reshape(EXPERTS, width_split, slots, MODEL_WIDTH), axis=1
    ).reshape(EXPERTS * slots, MODEL_WIDTH)


def page_order(page_table, n_tok, pages_dev):
    page_grid = page_table.reshape(n_tok, pages_dev)
    target = page_grid // pages_dev
    page_ids = jnp.arange(pages_dev, dtype=jnp.int32)
    earlier = page_ids[:, None] > page_ids[None, :]
    same_dest = target[:, :, None] == target[:, None, :]
    order_rank = jnp.sum((same_dest & earlier[None]).astype(jnp.int32), axis=2)
    return (target, order_rank, page_grid % pages_dev)


def per_device(
    tokens,
    lengths,
    norm_gain_attn,
    query_key_value_weight,
    sinks,
    w_out_attn,
    norm_gain_moe,
    routes,
    gates,
    w_in,
    w_down,
    page_table,
):
    n_tok = lax.axis_size("tok")
    n_head = lax.axis_size("head")
    tok_id = lax.axis_index("tok")
    head_id = lax.axis_index("head")
    row_count = tokens.shape[0]
    tok_dev = row_count * n_head
    groups = sinks.shape[0] // QUERY_PER_KEY
    normed_input = normalize(tokens, norm_gain_attn).astype(jnp.bfloat16)
    projected_rows = jnp.dot(
        lax.all_gather(normed_input, "head", axis=0, tiled=True),
        query_key_value_weight,
        preferred_element_type=jnp.float32,
    ).reshape(tok_dev, groups, QUERY_PER_KEY + 2, HEAD_SIZE)
    row_base = tok_id * tok_dev
    query_index = row_base + jnp.arange(tok_dev, dtype=jnp.int32)
    query_segs, positions = segment_table(lengths, query_index)
    query_rows = (
        rotate(projected_rows[:, :, :QUERY_PER_KEY], positions) * HEAD_SIZE ** (-0.5)
    ).astype(jnp.bfloat16)
    key_rot = rotate(projected_rows[:, :, QUERY_PER_KEY], positions)
    key_value_pairs = jnp.concatenate(
        [key_rot, projected_rows[:, :, QUERY_PER_KEY + 1]], axis=-1
    ).astype(jnp.bfloat16)
    rim_rows = passed_along(key_value_pairs[tok_dev - ATTEND_WINDOW :], "tok", 1)
    key_index = row_base - ATTEND_WINDOW + jnp.arange(tok_dev + ATTEND_WINDOW, dtype=jnp.int32)
    key_segs, _ = segment_table(lengths, key_index)
    allowed = band_mask(query_index, key_index, query_segs, key_segs, ATTEND_WINDOW)
    attended = band_attention(
        query_rows,
        jnp.concatenate([rim_rows, key_value_pairs], axis=0),
        sinks.reshape(groups, QUERY_PER_KEY),
        allowed,
    )
    attn_sum = lax.psum_scatter(
        jnp.dot(attended, w_out_attn, preferred_element_type=jnp.float32).astype(jnp.bfloat16),
        "head",
        scatter_dimension=0,
        tiled=True,
    ).astype(jnp.float32)
    resid = tokens.astype(jnp.float32) + attn_sum
    moe_in = normalize(resid, norm_gain_moe).astype(jnp.bfloat16)
    own_index = row_base + head_id * row_count + jnp.arange(row_count, dtype=jnp.int32)
    own_segs, _ = segment_table(lengths, own_index)
    is_live = own_segs < NSEQ
    capacity = row_count // 8 + 2
    width_split = n_tok * n_head // EXPERTS
    expert_ids = jnp.arange(EXPERTS, dtype=jnp.int32)
    naming = routes[:, :, None] == expert_ids[None, None, :]
    routed = (jnp.any(naming, axis=1) & is_live[:, None]).astype(jnp.int32)
    slot_rank = jnp.cumsum(routed, axis=0) - 1
    slot_ids = jnp.arange(capacity, dtype=jnp.int32)
    placed = (routed == 1)[:, :, None] & (slot_rank[:, :, None] == slot_ids[None, None, :])
    local_ids = jnp.arange(row_count, dtype=jnp.int32)
    source_row = jnp.sum(jnp.where(placed, local_ids[:, None, None], 0), axis=0)
    filled = jnp.any(placed, axis=0)
    outgoing = jnp.where(filled[:, :, None], moe_in[source_row], jnp.zeros((), jnp.bfloat16))

    def flat_route(blocks):
        return lax.all_to_all(blocks, ("tok", "head"), split_axis=0, concat_axis=0, tiled=True)

    summed = copied_route(outgoing, flat_route, width_split, capacity, w_in[0], w_down[0])
    chosen_rank = jnp.sum(jnp.where(naming, slot_rank[:, None, :], 0), axis=2)
    pick_rows = routes * capacity + jnp.clip(chosen_rank, 0, capacity - 1)
    weighted = jnp.where(is_live[:, None], gates, 0.0)
    expert_sum = jnp.sum(summed[pick_rows] * weighted[:, :, None], axis=1)
    hidden_out = (resid + expert_sum).astype(jnp.bfloat16)
    pages_dev = tok_dev // PAGE_TOKENS
    share_count = pages_dev // n_tok
    paged = key_value_pairs.reshape(pages_dev, PAGE_TOKENS, groups, 2 * HEAD_SIZE)
    target, order_rank, slot_grid = page_order(page_table, n_tok, pages_dev)
    dest_ids = jnp.arange(n_tok, dtype=jnp.int32)
    share_ids = jnp.arange(share_count, dtype=jnp.int32)
    page_ids = jnp.arange(pages_dev, dtype=jnp.int32)
    my_target = target[tok_id]
    my_rank = order_rank[tok_id]
    matched = (my_target[:, None, None] == dest_ids[None, :, None]) & (
        my_rank[:, None, None] == share_ids[None, None, :]
    )
    pick_page = jnp.sum(jnp.where(matched, page_ids[:, None, None], 0), axis=0)
    arrived = lax.all_to_all(paged[pick_page], "tok", split_axis=0, concat_axis=0, tiled=True)
    to_here = (target == tok_id)[:, :, None] & (order_rank[:, :, None] == share_ids[None, None, :])
    landing = jnp.sum(jnp.where(to_here, slot_grid[:, :, None], 0), axis=1)
    stored = jnp.zeros_like(paged).at[landing.reshape(-1)].set(arrived.reshape(paged.shape))
    kv_cache = jnp.transpose(stored, (2, 0, 1, 3))
    return (hidden_out, kv_cache)


def solution(mesh):
    return jax.shard_map(
        per_device,
        mesh=mesh,
        in_specs=(
            P(("tok", "head"), None),
            P(),
            P(),
            P(None, "head"),
            P("head"),
            P("head", None),
            P(),
            P(("tok", "head"), None),
            P(("tok", "head"), None),
            P(("tok", "head"), None, None),
            P(("tok", "head"), None, None),
            P(),
        ),
        out_specs=(P(("tok", "head"), None), P("head", "tok", None, None)),
        check_vma=False,
    )
```

profile of v0, /device:TPU:0, one launch (start us, length us, event | category | flops | bytes accessed | tf_op | source)
XLA Modules:
  0.0 305.4 jit_solution(13379243260324787856)
XLA Ops:
  7.2 1.2 fusion.18
  8.4 1.9 fusion.20
  10.4 0.7 exp.30
  11.2 0.8 reduce-window.8
  12.9 19.6 %all-gather.2.cloned.1.call-done = bf16[256,2880]{1,0:T(8,128)(2,1)} async-done(((bf16[64,2880]{1,0:T(8,128)(2,1)}), bf16[256,2880]{1,0:T(8,128)(2,1)}) %all-gather.2.cloned.1.call-update) | async-done | bytes 1474576 | tf_op jit(solution)/shard_map/all_gather | solution.py:158
  32.5 6.7 %fusion.41 = f32[256,1280]{0,1:T(8,128)S(1)} fusion(bf16[256,2880]{1,0:T(8,128)(2,1)} %all-gather.2.cloned.1.call-done, bf16[2880,1280]{1,0:T(8,128)(2,1)} %param.15), kind=kOutput, calls=%fused_computation.132 | convolution fusion | flops 1887436800 | bytes 10158080 | tf_op jit(solution)/shard_map/dot_general | solution.py:157
  39.4 3.4 %collective-permute-start = (bf16[128,2,128]{0,2,1:T(8,128)(2,1)S(1)}, bf16[128,2,128]{0,2,1:T(8,128)(2,1)S(1)}, u32[]{:S(2)}, u32[]{:S(2)}) collective-permute-start(bf16[128,2,128]{0,2,1:T(8,128)(2,1)S(1)} %pad_maximum_fusion.4), channel_id=1, source_target_pairs={{0,4},{4,8},{8,12},{12,16},{16,20},{20,24},{24,28},{1,5},{5,9},{9,... | collective-permute-start | bytes 196616 | tf_op jit(solution)/shard_map/ppermute | solution.py:25
  43.0 1.7 collective-permute-done
  45.0 0.9 fusion.10
  46.0 0.9 fusion.16
  48.0 3.1 %convolution_convert_fusion = bf16[256,2880]{1,0:T(8,128)(2,1)} fusion(bf16[1024,2880]{0,1:T(8,128)(2,1)S(1)} %bitcast.118, bf16[128,8,2,128]{3,2,1,0:T(2,128)(2,1)S(1)} %bitcast.105), kind=kOutput, calls=%fused_computation.11 | convolution fusion | flops 1510686720 | bytes 7897088 | tf_op jit(solution)/shard_map/dot_general | solution.py:183
  52.8 27.0 %reduce-scatter.2.cloned.1.call-done = bf16[64,2880]{1,0:T(8,128)(2,1)} async-done(((bf16[256,2880]{1,0:T(8,128)(2,1)}), bf16[64,2880]{1,0:T(8,128)(2,1)}) %reduce-scatter.2.cloned.1.call-update) | async-done | bytes 368656 | tf_op jit(solution)/shard_map/reduce_scatter | solution.py:182
  79.8 1.2 multiply_reduce_fusion.1
  81.1 1.1 multiply_convert_fusion
  82.2 2.8 gather_fusion
  85.0 2.4 reshape.547
  87.5 3.8 %broadcast_select_fusion = bf16[32,10,2880]{2,1,0:T(8,128)(2,1)} fusion(bf16[32,10,2880]{2,1,0:T(8,128)(2,1)} %reshape.547, pred[32,10]{1,0:T(8,128)(4,1)S(1)} %copy.69), kind=kLoop, calls=%fused_computation.18 | loop fusion | flops 921600 | bytes 3686720 | tf_op jit(solution)/shard_map/jit(_where)/select_n | solution.py:204
  91.3 4.8 %all-to-all-start = ((bf16[32,10,2880]{2,1,0:T(8,128)(2,1)}), bf16[32,10,2880]{2,1,0:T(8,128)(2,1)S(1)}, u32[]{:S(2)}, u32[]{:S(2)}) async-start(bf16[32,10,2880]{2,1,0:T(8,128)(2,1)} %broadcast_select_fusion), calls=%async_computation.1 | async-start | bytes 6029312 | tf_op jit(solution)/shard_map/all_to_all | solution.py:207
  96.2 0.6 broadcast_compare_fusion.1
  97.0 0.6 copy-done.5
  98.0 0.8 copy.75
  98.7 0.8 copy.76
  99.5 0.8 copy.77
  100.2 1.2 pad_maximum_fusion.3
  101.4 1.2 gather_fusion.2
  102.7 62.1 %all-to-all-done = bf16[32,10,2880]{2,1,0:T(8,128)(2,1)S(1)} async-done(((bf16[32,10,2880]{2,1,0:T(8,128)(2,1)}), bf16[32,10,2880]{2,1,0:T(8,128)(2,1)S(1)}, u32[]{:S(2)}, u32[]{:S(2)}) %all-to-all-start) | async-done | bytes 1843232 | tf_op jit(solution)/shard_map/all_to_all | solution.py:207
  164.8 3.4 %all-to-all-start.2 = ((bf16[8,2,16,2,128]{4,2,3,1,0:T(8,128)(2,1)}), bf16[8,2,16,2,128]{4,2,3,1,0:T(8,128)(2,1)S(1)}, u32[]{:S(2)}, u32[]{:S(2)}) async-start(bf16[8,2,16,2,128]{4,2,3,1,0:T(8,128)(2,1)} %bitcast.107), calls=%async_computation.3 | async-start | bytes 262144 | tf_op jit(solution)/shard_map/all_to_all | solution.py:228
  168.2 2.5 reshape.537
  170.6 20.8 %fusion = f32[320,5760]{1,0:T(8,128)} fusion(bf16[320,2880]{1,0:T(8,128)(2,1)} %reshape.537, bf16[1,2880,5760]{2,1,0:T(8,128)(2,1)} %param.21), kind=kOutput, calls=%fused_computation.4 | convolution fusion | flops 10616832000 | bytes 42393600 | tf_op jit(solution)/shard_map/dot_general | solution.py:102
  191.4 13.9 %fusion.4 = bf16[320,2880]{1,0:T(8,128)(2,1)S(1)} fusion(bf16[1,2880,2880]{2,1,0:T(8,128)(2,1)} %param.22, f32[320,5760]{1,0:T(8,128)} %fusion), kind=kOutput, calls=%fused_computation.10 | convolution fusion | flops 5316710400 | bytes 26337280 | tf_op jit(solution)/shard_map/dot_general | solution.py:108
  205.3 2.4 reshape.538
  207.7 7.3 %all-to-all-start.1 = ((bf16[32,10,2880]{2,1,0:T(8,128)(2,1)}), bf16[32,10,2880]{2,1,0:T(8,128)(2,1)S(1)}, u32[]{:S(2)}, u32[]{:S(2)}) async-start(bf16[32,10,2880]{2,1,0:T(8,128)(2,1)} %reshape.538), calls=%async_computation.2 | async-start | bytes 6029312 | tf_op jit(solution)/shard_map/all_to_all | solution.py:207
  215.1 0.6 compare_select_fusion.1
  215.6 0.8 copy.72
  216.4 0.7 reshape.556
  217.1 0.7 broadcast_select_fusion.1
  217.8 0.7 copy.73
  218.5 0.7 add_select_fusion
  219.2 0.8 select_reduce_fusion.3
  220.2 0.7 pad_clamp_fusion.1
  220.9 1.7 scatter_fusion
  222.6 0.7 copy.79
  223.2 60.5 %all-to-all-done.1 = bf16[32,10,2880]{2,1,0:T(8,128)(2,1)S(1)} async-done(((bf16[32,10,2880]{2,1,0:T(8,128)(2,1)}), bf16[32,10,2880]{2,1,0:T(8,128)(2,1)S(1)}, u32[]{:S(2)}, u32[]{:S(2)}) %all-to-all-start.1) | async-done | bytes 1843232 | tf_op jit(solution)/shard_map/all_to_all | solution.py:207
  283.7 2.7 reshape.545
  286.4 5.1 %gather_fusion.1 = f32[256,2880]{1,0:T(8,128)S(1)} fusion(f32[320,2880]{1,0:T(8,128)} %reshape.545, s32[1024]{0:T(1024)S(1)} %pad_clamp_fusion.1), kind=kCustom, calls=%fused_computation.1 | custom fusion | bytes 5899264 | tf_op jit(solution)/shard_map/gather | solution.py:213
  291.6 2.1 reshape.555
  293.7 4.0 %multiply_reduce_fusion = f32[64,2880]{1,0:T(8,128)S(1)} fusion(f32[64,4,2880]{2,1,0:T(4,128)} %reshape.555, f32[64,4]{1,0:T(8,128)S(1)} %copy-done.3), kind=kLoop, calls=%fused_computation.17 | loop fusion | flops 1290240 | bytes 3687424 | tf_op jit(solution)/shard_map/reduce_sum | solution.py:213
  297.7 0.9 add_convert_fusion
  (97 shorter events, 5.6 us)
Async XLA Ops:
  7.2 25.3 %all-gather.2.cloned.1.call-start = ((), (), s32[]{:S(2)}) async-start(), calls=%async_computation.4 | async-start | bytes 1884160 | tf_op jit(solution)/shard_map/all_gather | solution.py:158
  10.3 69.5 %reduce-scatter.2.cloned.1.call-start = ((), (), s32[]{:S(2)}) async-start(), calls=%async_computation.5 | async-start | bytes 1884160 | tf_op jit(solution)/shard_map/reduce_scatter | solution.py:182
  39.4 5.3 %collective-permute-start = (bf16[128,2,128]{0,2,1:T(8,128)(2,1)S(1)}, bf16[128,2,128]{0,2,1:T(8,128)(2,1)S(1)}, u32[]{:S(2)}, u32[]{:S(2)}) collective-permute-start(bf16[128,2,128]{0,2,1:T(8,128)(2,1)S(1)} %pad_maximum_fusion.4), channel_id=1, source_target_pairs={{0,4},{4,8},{8,12},{12,16},{16,20},{20,24},{24,28},{1,5},{5,9},{9,... | collective-permute-start | bytes 196616 | tf_op jit(solution)/shard_map/ppermute | solution.py:25
  45.0 2.5 slice-start
  46.0 1.9 slice-start.1
  48.0 3.1 %copy-start.6 = (s32[64,4]{0,1:T(4,128)S(1)}, s32[64,4]{0,1:T(4,128)}, u32[]{:S(2)}) copy-start(s32[64,4]{0,1:T(4,128)} %param.19) | copy-start | bytes 3076
  48.0 31.9 %copy-start = (bf16[64,2880]{1,0:T(8,128)(2,1)S(1)}, bf16[64,2880]{1,0:T(8,128)(2,1)}, u32[]{:S(2)}) copy-start(bf16[64,2880]{1,0:T(8,128)(2,1)} %param.12) | copy-start | bytes 1105924
  48.0 33.1 %copy-start.7 = (f32[2880]{0:T(1024)S(1)}, f32[2880]{0:T(1024)}, u32[]{:S(2)}) copy-start(f32[2880]{0:T(1024)} %param.18) | copy-start | bytes 34564
  51.2 0.5 copy-start.8
  91.3 4.8 %copy-start.9 = (s32[128]{0:T(128)S(1)}, s32[128]{0:T(128)}, u32[]{:S(2)}) copy-start(s32[128]{0:T(128)} %param.23) | copy-start | bytes 1540
  91.3 73.5 %all-to-all-start = ((bf16[32,10,2880]{2,1,0:T(8,128)(2,1)}), bf16[32,10,2880]{2,1,0:T(8,128)(2,1)S(1)}, u32[]{:S(2)}, u32[]{:S(2)}) async-start(bf16[32,10,2880]{2,1,0:T(8,128)(2,1)} %broadcast_select_fusion), calls=%async_computation.1 | async-start | bytes 6029312 | tf_op jit(solution)/shard_map/all_to_all | solution.py:207
  96.1 95.3 %copy-start.4 = (s32[8,16]{1,0:T(8,128)}, s32[8,16]{1,0:T(8,128)S(1)}, u32[]{:S(2)}) copy-start(s32[8,16]{1,0:T(8,128)S(1)} %reshape.541) | copy-start | bytes 1540
  97.0 0.6 copy-start.5
  164.8 43.0 %all-to-all-start.2 = ((bf16[8,2,16,2,128]{4,2,3,1,0:T(8,128)(2,1)}), bf16[8,2,16,2,128]{4,2,3,1,0:T(8,128)(2,1)S(1)}, u32[]{:S(2)}, u32[]{:S(2)}) async-start(bf16[8,2,16,2,128]{4,2,3,1,0:T(8,128)(2,1)} %bitcast.107), calls=%async_computation.3 | async-start | bytes 262144 | tf_op jit(solution)/shard_map/all_to_all | solution.py:228
  207.7 13.1 %copy-start.2 = (bf16[8,2,16,2,128]{4,2,3,1,0:T(8,128)(2,1)}, bf16[8,2,16,2,128]{4,2,3,1,0:T(8,128)(2,1)S(1)}, u32[]{:S(2)}) copy-start(bf16[8,2,16,2,128]{4,2,3,1,0:T(8,128)(2,1)S(1)} %all-to-all-done.2) | copy-start | bytes 393220
  207.7 76.0 %all-to-all-start.1 = ((bf16[32,10,2880]{2,1,0:T(8,128)(2,1)}), bf16[32,10,2880]{2,1,0:T(8,128)(2,1)S(1)}, u32[]{:S(2)}, u32[]{:S(2)}) async-start(bf16[32,10,2880]{2,1,0:T(8,128)(2,1)} %reshape.538), calls=%async_computation.2 | async-start | bytes 6029312 | tf_op jit(solution)/shard_map/all_to_all | solution.py:207
  291.6 2.1 copy-start.3
  293.7 4.0 %copy-start.1 = (bf16[64,2880]{1,0:T(8,128)(2,1)S(1)}, bf16[64,2880]{1,0:T(8,128)(2,1)}, u32[]{:S(2)}) copy-start(bf16[64,2880]{1,0:T(8,128)(2,1)} %reduce-scatter.2.cloned.1.call-done) | copy-start | bytes 1105924
Sparse Core Ops, SparseCore 0:
  10.4 21.9 all-gather.1
  51.2 28.6 reduce-scatter.1
where the time goes:
time: 306 us; the launch traced here: 305 us
  waiting for transfers between devices  171 us (56%)
  matrix products  46.3 us (15%)
  local copies, waits for them, and re-layouts  32.3 us (11%)
  other arithmetic  22.6 us (7%)
  starting transfers between devices  18.9 us (6%)
  between operations  14.5 us (5%)
    all_to_all x2, waiting for transfers between devices, flat_route(): lax.all_to_all(blocks, ('tok', 'head'), split_axis=0, concat_axis=0, tile...  123 us
    reduce_scatter x1, waiting for transfers between devices, per_device(): lax.psum_scatter(jnp.dot(attended, w_out_attn, preferred_element_type=jnp...  27 us
    dot_general x1, matrix products, expert_mlp(): gate_up = jnp.dot(rows_in, w_in_local, preferred_element_type=jnp.float32)  20.8 us
    all_gather x1, waiting for transfers between devices, per_device(): lax.all_gather(normed_input, 'head', axis=0, tiled=True)  19.6 us
    dot_general x1, matrix products, expert_mlp(): jnp.dot(activated, w_down_local, preferred_element_type=jnp.float32)  13.9 us
    all_to_all x2, starting transfers between devices, flat_route(): lax.all_to_all(blocks, ('tok', 'head'), split_axis=0, concat_axis=0, tile...  12 us
    gather x2, local copies, waits for them, and re-layouts, per_device(): expert_sum = jnp.sum(summed[pick_rows] * weighted[:, :, None], axis=1)  7.21 us
    dot_general x1, matrix products, per_device(): jnp.dot(lax.all_gather(normed_input, 'head', axis=0, tiled=True), query_k...  6.69 us
  transfers between devices with their start and end apart: 6, of which 5 were waited for; matrix products, arithmetic and copies ran while one was open for 19% of the time, Pallas kernels for 0%

commit v1 on v0

v1 whole, which is shorter than its diff:
```python
import functools
import math

import jax
import jax.numpy as jnp
from jax import lax
from jax.experimental import pallas as pl
from jax.experimental.pallas import tpu as pltpu
from jax.sharding import PartitionSpec as P

MODEL_WIDTH = 2880
HEAD_SIZE = 64
EXPERTS = 32
ATTEND_WINDOW = 128
NSEQ = 4
PAGE_TOKENS = 16
QUERY_PER_KEY = 8


EPSILON = 1e-05
ROPE_BASE = 150000.0
GLU_ALPHA = 1.702

LANES = 128
MAIN_SLOTS = 8
PIECE = 768
PIECES = 4
EXTRA_AT = 2944
IN_TILE = 1152
MIB = 1 << 20


def passed_along(array, axis, by):
    peers = lax.axis_size(axis)
    pairs = [(i, i + by) for i in range(peers) if 0 <= i + by < peers]
    return lax.ppermute(array, axis, pairs)


def segment_ends(lengths_ref):
    ends, end = [], 0
    for k in range(NSEQ):
        end = end + lengths_ref[k]
        ends.append(end)
    return ends


def segment_of(index, ends):
    segment = jnp.zeros_like(index)
    for end in ends:
        segment = segment + jnp.where(index >= end, 1, 0)
    return segment


def rope_tables(index, ends):
    start = jnp.zeros_like(index)
    for end in ends:
        start = jnp.where(index >= end, end, start)
    half = HEAD_SIZE // 2
    lane = lax.broadcasted_iota(jnp.int32, index.shape, 1)
    inv_freq = jnp.exp(
        (lane % half).astype(jnp.float32) * (-2.0 * math.log(ROPE_BASE) / HEAD_SIZE)
    )
    angles = (index - start).astype(jnp.float32) * inv_freq
    low = lane % HEAD_SIZE < half
    sin = jnp.sin(angles)
    return jnp.cos(angles), jnp.where(low, -sin, sin), low, lane


def qkv_kernel(step, chips, ids_ref, lengths_ref, own_ref, other_ref, gain_ref, w_ref, *refs):
    q_ref, kv_ref, xn_ref, cos_ref, sin_ref = refs[-5:]
    rows = own_ref.shape[0]
    core, chip, shard = ids_ref[0], (ids_ref[1] + chips - step) % chips, ids_ref[2]

    @pl.when(pl.program_id(0) == 0)
    def _():
        for at, ref in ((core, own_ref), (1 - core, other_ref)):
            wide = ref[...].astype(jnp.float32)
            inv_rms = lax.rsqrt(jnp.mean(wide * wide, axis=-1, keepdims=True) + EPSILON)
            normed = (wide * inv_rms * gain_ref[...][None]).astype(jnp.bfloat16)
            xn_ref[pl.ds(pl.multiple_of(at * rows, 16), rows), :] = normed
        first = (shard * chips + chip) * 2 * rows
        index = first + lax.broadcasted_iota(jnp.int32, cos_ref.shape, 0)
        cos, sin, _, _ = rope_tables(index, segment_ends(lengths_ref))
        cos_ref[...] = cos
        sin_ref[...] = sin

    projected = jnp.dot(xn_ref[...], w_ref[...], preferred_element_type=jnp.float32)
    cos, sin = cos_ref[...], sin_ref[...]
    lane = lax.broadcasted_iota(jnp.int32, cos.shape, 1)
    low = lane % HEAD_SIZE < HEAD_SIZE // 2

    def turned(u):
        return jnp.where(low, pltpu.roll(u, LANES - 32, 1), pltpu.roll(u, 32, 1))

    for b in range(QUERY_PER_KEY // 2):
        u = projected[:, b * LANES : (b + 1) * LANES]
        q_ref[:, b * LANES : (b + 1) * LANES] = (
            (u * cos + turned(u) * sin) * HEAD_SIZE ** (-0.5)
        ).astype(jnp.bfloat16)
    u = projected[:, QUERY_PER_KEY * HEAD_SIZE :]
    rotated = u * cos + turned(u) * sin
    kv_ref[...] = jnp.where(lane < HEAD_SIZE, rotated, u).astype(jnp.bfloat16)


def project(ids, lengths, step, chips, own, other, gain, weight, earlier):
    rows, width = own.shape
    columns = weight.shape[1]
    group = (QUERY_PER_KEY + 2) * HEAD_SIZE
    qs, kvs = QUERY_PER_KEY * HEAD_SIZE, 2 * HEAD_SIZE
    groups = columns // group
    whole = lambda g, ids: (0, 0)
    by_group = lambda g, ids: ((ids[1] + chips - step) % chips, g)
    return pl.pallas_call(
        functools.partial(qkv_kernel, step, chips),
        grid_spec=pltpu.PrefetchScalarGridSpec(
            num_scalar_prefetch=1,
            grid=(groups,),
            in_specs=[
                pl.BlockSpec(memory_space=pltpu.SMEM),
                pl.BlockSpec((rows, width), whole),
                pl.BlockSpec((rows, width), whole),
                pl.BlockSpec((width,), lambda g, ids: (0,)),
                pl.BlockSpec((width, group), lambda g, ids: (0, g)),
            ]
            + [pl.BlockSpec(memory_space=pl.ANY)] * len(earlier),
            out_specs=[
                pl.BlockSpec((2 * rows, qs), by_group),
                pl.BlockSpec((2 * rows, kvs), by_group),
            ],
            scratch_shapes=[
                pltpu.VMEM((2 * rows, width), jnp.bfloat16),
                pltpu.VMEM((2 * rows, LANES), jnp.float32),
                pltpu.VMEM((2 * rows, LANES), jnp.float32),
            ],
        ),
        out_shape=[
            jax.ShapeDtypeStruct((2 * rows * chips, groups * qs), jnp.bfloat16),
            jax.ShapeDtypeStruct((2 * rows * chips, groups * kvs), jnp.bfloat16),
        ],
        input_output_aliases={6: 0, 7: 1} if earlier else {},
        compiler_params=pltpu.CompilerParams(vmem_limit_bytes=60 * MIB),
        cost_estimate=pl.CostEstimate(
            flops=4 * rows * width * columns, bytes_accessed=2 * width * columns, transcendentals=0
        ),
        name="project",
    )(ids, lengths, own, other, gain, weight, *earlier)


def pack_rows(values_ref, pick_ref, packed_ref):
    packed_ref[:, :EXTRA_AT] = jnp.dot(
        pick_ref[0], values_ref[:, :EXTRA_AT], preferred_element_type=jnp.float32
    ).astype(jnp.bfloat16)
    pieces = jnp.zeros((packed_ref.shape[0], packed_ref.shape[1] - EXTRA_AT), jnp.float32)
    for p in range(pick_ref.shape[0] - 1):
        pieces = pieces + jnp.dot(
            pick_ref[1 + p],
            values_ref[:, p * PIECE : (p + 1) * PIECE],
            preferred_element_type=jnp.float32,
        )
    packed_ref[:, EXTRA_AT:] = pieces.astype(jnp.bfloat16)


def resid_kernel(tokens_ref, own_ref, others_ref, gain_ref, resid_ref, moe_ref):
    resid = tokens_ref[...].astype(jnp.float32) + own_ref[...].astype(jnp.float32)
    for k in range(others_ref.shape[0]):
        resid = resid + others_ref[k].astype(jnp.float32)
    resid_ref[...] = resid
    inv_rms = lax.rsqrt(jnp.mean(resid * resid, axis=-1, keepdims=True) + EPSILON)
    moe_ref[...] = (resid * inv_rms * gain_ref[...][None]).astype(jnp.bfloat16)


def pack_kernel(moe_ref, pick_ref, packed_ref, values_ref):
    width = moe_ref.shape[1]
    values_ref[:, width:] = jnp.zeros_like(values_ref[:, width:])
    values_ref[:, :width] = moe_ref[...]
    pack_rows(values_ref, pick_ref, packed_ref)


def packed_width(extras):
    return EXTRA_AT + PIECE if extras else PIECES * PIECE


def finish_attention(tokens, own, others, gain):
    rows, width = tokens.shape
    return pl.pallas_call(
        resid_kernel,
        out_shape=[
            jax.ShapeDtypeStruct((rows, width), jnp.float32),
            jax.ShapeDtypeStruct((rows, width), jnp.bfloat16),
        ],
        compiler_params=pltpu.CompilerParams(vmem_limit_bytes=32 * MIB),
        name="finish_attention",
    )(tokens, own, others, gain)


def pack(moe_in, picks, beside):
    rows, width = moe_in.shape
    kinds, slots, _ = picks.shape
    return pl.pallas_call(
        pack_kernel,
        out_shape=jax.ShapeDtypeStruct((slots, packed_width(kinds > 1)), jnp.bfloat16),
        scratch_shapes=[pltpu.VMEM((rows, PIECES * PIECE), jnp.bfloat16)],
        compiler_params=pltpu.CompilerParams(vmem_limit_bytes=32 * MIB),
        cost_estimate=pl.CostEstimate(
            flops=2 * slots * rows * 2 * width, bytes_accessed=beside, transcendentals=0
        ),
        name="pack",
    )(moe_in, picks)


def piece_of(count, slots, piece):
    t = lax.broadcasted_iota(jnp.int32, (count, slots), 0)
    r = lax.broadcasted_iota(jnp.int32, (count, slots), 1)
    return jnp.where(r == PIECES * t + piece, 1.0, 0.0).astype(jnp.bfloat16)


def fill_rows(packed_ref, x_ref, extras):
    slots, width = packed_ref.shape[0], x_ref.shape[1]
    x_ref[:slots, :] = packed_ref[:, :width]
    if extras:
        further = slots // PIECES
        for p in range(PIECES):
            extent = min(PIECE, width - p * PIECE)
            x_ref[slots:, p * PIECE : p * PIECE + extent] = jnp.dot(
                piece_of(further, slots, p),
                packed_ref[:, EXTRA_AT : EXTRA_AT + extent],
                preferred_element_type=jnp.float32,
            ).astype(jnp.bfloat16)


def activate(gate_up_ref, act_ref):
    rows, ffs = act_ref.shape
    base = ffs // LANES * LANES
    chunk = 32
    for r in range(0, rows, chunk):
        gate = gate_up_ref[r : r + chunk, :ffs]
        up = gate_up_ref[r : r + chunk, base:]
        if ffs > base:
            up = pltpu.roll(up, up.shape[1] - (ffs - base), 1)
        up = up[:, :ffs]
        act_ref[r : r + chunk, :] = (
            (up + 1.0) * gate * jax.nn.sigmoid(GLU_ALPHA * gate)
        ).astype(jnp.bfloat16)


def put_piece(piece, act_ref, w_down_ref, out_ref, width, piece_ref):
    slots = out_ref.shape[0]
    made = jnp.dot(act_ref[...], w_down_ref[0], preferred_element_type=jnp.float32)
    column = lax.broadcasted_iota(jnp.int32, made.shape, 1) + piece * PIECE
    made = jnp.where(column < width, made, 0.0).astype(jnp.bfloat16)
    out_ref[:, pl.ds(pl.multiple_of(piece * PIECE, LANES), PIECE)] = made[:slots]
    if piece_ref is not None:
        further = slots // PIECES
        t = lax.broadcasted_iota(jnp.int32, (slots, further), 1)
        r = lax.broadcasted_iota(jnp.int32, (slots, further), 0)
        spread = jnp.where(r == PIECES * t + piece, 1.0, 0.0).astype(jnp.bfloat16)
        part = jnp.dot(spread, made[slots:], preferred_element_type=jnp.float32).astype(
            jnp.bfloat16
        )

        @pl.when(piece == 0)
        def _():
            piece_ref[...] = part

        @pl.when(piece > 0)
        def _():
            piece_ref[...] = piece_ref[...] + part

        @pl.when(piece == PIECES - 1)
        def _():
            out_ref[:, EXTRA_AT:] = piece_ref[...]


def expert_kernel(extras, in_tiles, down, *refs):
    packed_ref, w_in_ref = refs[:2]
    scratch = refs[4:] if down else refs[3:]
    x_ref, gate_up_ref = scratch[:2]
    act_ref = scratch[2] if down else refs[2]
    step = pl.program_id(0)

    @pl.when(step == 0)
    def _():
        fill_rows(packed_ref, x_ref, extras)

    @pl.when(step < in_tiles)
    def _():
        gate_up_ref[:, pl.ds(pl.multiple_of(step * IN_TILE, LANES), IN_TILE)] = jnp.dot(
            x_ref[...], w_in_ref[0], preferred_element_type=jnp.float32
        )

    @pl.when(step == (in_tiles if down else in_tiles - 1))
    def _():
        activate(gate_up_ref, act_ref)

    if down:
        w_down_ref, out_ref = refs[2:4]

        @pl.when(step >= in_tiles)
        def _():
            piece_ref = scratch[3] if extras else None
            put_piece(step - in_tiles, act_ref, w_down_ref, out_ref, x_ref.shape[1], piece_ref)


def down_kernel(extras, width, act_ref, w_down_ref, out_ref, *scratch):
    put_piece(
        pl.program_id(0), act_ref, w_down_ref, out_ref, width, scratch[0] if extras else None
    )


def expert(packed, w_in, w_down, extras, down=True):
    slots, held = packed.shape
    width = w_in.shape[1]
    ffs = w_down.shape[1]
    rows = slots + (slots // PIECES if extras else 0)
    in_tiles = pl.cdiv(2 * ffs, IN_TILE)
    whole = lambda i: (0, 0)
    in_specs = [
        pl.BlockSpec((slots, held), whole),
        pl.BlockSpec((1, width, IN_TILE), lambda i: (0, 0, jnp.minimum(i, in_tiles - 1))),
    ]
    scratch = [
        pltpu.VMEM((rows, width), jnp.bfloat16),
        pltpu.VMEM((rows, in_tiles * IN_TILE), jnp.float32),
    ]
    args = (packed, w_in)
    out = (rows, ffs)
    if down:
        in_specs += [
            pl.BlockSpec((1, ffs, PIECE), lambda i: (0, 0, jnp.maximum(i - in_tiles, 0)))
        ]
        scratch += [pltpu.VMEM((rows, ffs), jnp.bfloat16)]
        scratch += [pltpu.VMEM((slots, PIECE), jnp.bfloat16)] if extras else []
        args += (w_down,)
        out = (slots, held)
    parts = 6 if down else 4
    return pl.pallas_call(
        functools.partial(expert_kernel, extras, in_tiles, down),
        grid=(in_tiles + (PIECES if down else 0),),
        in_specs=in_specs,
        out_specs=pl.BlockSpec(out, whole),
        out_shape=jax.ShapeDtypeStruct(out, jnp.bfloat16),
        scratch_shapes=scratch,
        compiler_params=pltpu.CompilerParams(vmem_limit_bytes=56 * MIB),
        cost_estimate=pl.CostEstimate(
            flops=parts * rows * width * ffs,
            bytes_accessed=parts * width * ffs,
            transcendentals=rows * ffs,
        ),
        name="expert" if down else "expert_up",
    )(*args)


def expert_down(act, w_down, slots, held, extras):
    rows, ffs = act.shape
    width = w_down.shape[2]
    whole = lambda i: (0, 0)
    return pl.pallas_call(
        functools.partial(down_kernel, extras, width),
        grid=(PIECES,),
        in_specs=[
            pl.BlockSpec((rows, ffs), whole),
            pl.BlockSpec((1, ffs, PIECE), lambda i: (0, 0, i)),
        ],
        out_specs=pl.BlockSpec((slots, held), whole),
        out_shape=jax.ShapeDtypeStruct((slots, held), jnp.bfloat16),
        scratch_shapes=[pltpu.VMEM((slots, PIECE), jnp.bfloat16)] if extras else [],
        compiler_params=pltpu.CompilerParams(vmem_limit_bytes=56 * MIB),
        cost_estimate=pl.CostEstimate(
            flops=2 * rows * width * ffs, bytes_accessed=2 * width * ffs, transcendentals=0
        ),
        name="expert_down",
    )(act, w_down)


def weighted_sum(made_ref, weight_ref, total_ref):
    width = total_ref.shape[1]
    for term in range(2):
        made = jnp.dot(
            weight_ref[term, 0], made_ref[:, :width], preferred_element_type=jnp.float32
        )
        total_ref[...] = made if term == 0 else total_ref[...] + made
        for p in range(weight_ref.shape[1] - 1):
            extent = min(PIECE, width - p * PIECE)
            at = slice(p * PIECE, p * PIECE + extent)
            total_ref[:, at] = total_ref[:, at] + jnp.dot(
                weight_ref[term, 1 + p],
                made_ref[:, EXTRA_AT : EXTRA_AT + extent],
                preferred_element_type=jnp.float32,
            )


def partial_kernel(made_ref, weight_ref, out_ref, total_ref):
    weighted_sum(made_ref, weight_ref, total_ref)
    out_ref[...] = total_ref[...].astype(jnp.bfloat16)


def total_kernel(made_ref, weight_ref, resid_ref, far_ref, out_ref, total_ref):
    weighted_sum(made_ref, weight_ref, total_ref)
    out_ref[...] = (
        resid_ref[...] + (total_ref[...] + far_ref[...].astype(jnp.float32))
    ).astype(jnp.bfloat16)


def combine(made, weights, resid=None, far=None):
    rows = weights.shape[2]
    kernel, more = (partial_kernel, ()) if resid is None else (total_kernel, (resid, far))
    return pl.pallas_call(
        kernel,
        out_shape=jax.ShapeDtypeStruct((rows, MODEL_WIDTH), jnp.bfloat16),
        scratch_shapes=[pltpu.VMEM((rows, MODEL_WIDTH), jnp.float32)],
        compiler_params=pltpu.CompilerParams(vmem_limit_bytes=32 * MIB),
        name="combine",
    )(made, weights, *more)


def slots_kernel(extras, far, half, experts, shards, topk, ids_ref, lengths_ref, choice_ref, *out_refs):
    pick_ref, weight_ref = out_refs
    device = ids_ref[3]
    first_expert = device // half * experts
    _, slots, rows = pick_ref.shape
    source = (device + half) % (2 * half) if far else device
    r = lax.broadcasted_iota(jnp.int32, (slots, rows), 0)
    index = source * rows + lax.broadcasted_iota(jnp.int32, (slots, rows), 1)
    slot = r % MAIN_SLOTS
    own_expert = (first_expert + r // (MAIN_SLOTS * shards)).astype(jnp.float32)
    named = jnp.zeros((slots, rows), jnp.float32)
    gate = jnp.zeros((slots, rows), jnp.float32)
    for k in range(topk):
        here = choice_ref[k : k + 1, :] == own_expert
        named = jnp.where(here, 1.0, named)
        gate = gate + jnp.where(here, choice_ref[topk + k : topk + k + 1, :], 0.0)
    named = jnp.where(index < segment_ends(lengths_ref)[-1], named, 0.0)
    i = lax.broadcasted_iota(jnp.int32, (rows, rows), 0)
    j = lax.broadcasted_iota(jnp.int32, (rows, rows), 1)
    earlier = jnp.where(i < j, 1.0, 0.0).astype(jnp.bfloat16)
    same = jnp.where(i == j, 1.0, 0.0).astype(jnp.bfloat16)
    rank = jnp.dot(named.astype(jnp.bfloat16), earlier, preferred_element_type=jnp.float32)
    rank = jnp.where(named > 0.0, rank, -1.0).astype(jnp.int32)
    high = gate.astype(jnp.bfloat16).astype(jnp.float32)

    def put(hit, pick_at, high_at, low_at):
        pick_at[...] = jnp.where(hit, 1.0, 0.0).astype(jnp.bfloat16)
        for values, at in ((high, high_at), (gate - high, low_at)):
            kept = jnp.where(hit, values, 0.0).astype(jnp.bfloat16)
            at[...] = lax.dot_general(
                same, kept, (((1,), (1,)), ((), ())), preferred_element_type=jnp.float32
            ).astype(jnp.bfloat16)

    put(rank == slot, pick_ref.at[0], weight_ref.at[0, 0], weight_ref.at[1, 0])
    if extras:
        for p in range(PIECES):
            hit = jnp.where(slot % PIECES == p, rank, -2) == MAIN_SLOTS + slot // PIECES
            put(hit, pick_ref.at[1 + p], weight_ref.at[0, 1 + p], weight_ref.at[1, 1 + p])


def slot_tables(ids, lengths, choice, far, half, experts, shards, extras):
    topk, rows = choice.shape[0] // 2, choice.shape[1]
    slots = experts * shards * MAIN_SLOTS
    kinds = 1 + PIECES if extras else 1
    shapes = [(kinds, slots, rows), (2, kinds, rows, slots)]
    smem = pl.BlockSpec(memory_space=pltpu.SMEM)
    return pl.pallas_call(
        functools.partial(slots_kernel, extras, far, half, experts, shards, topk),
        in_specs=[smem, smem, pl.BlockSpec(memory_space=pltpu.VMEM)],
        out_shape=[jax.ShapeDtypeStruct(shape, jnp.bfloat16) for shape in shapes],
        compiler_params=pltpu.CompilerParams(vmem_limit_bytes=32 * MIB),
        name="slots",
    )(ids, lengths, choice)


def attend_kernel(row_count, chips, ids_ref, lengths_ref, q_ref, rim_ref, pair_ref, sink_ref, w_ref, kept_ref, sent_ref, attended_ref):
    def attend_block(block):
        window = rim_ref.shape[0]
        rows = slice(block * window, (block + 1) * window)
        groups = pair_ref.shape[1] // LANES
        core = ids_ref[0]
        ends = segment_ends(lengths_ref)
        first = ids_ref[2] * (chips * 2 * row_count) + block * window
        query = first + lax.broadcasted_iota(jnp.int32, (window, 2 * window), 0)
        key = first - window + lax.broadcasted_iota(jnp.int32, (window, 2 * window), 1)
        query_segment = segment_of(query, ends)
        seen = (query_segment == segment_of(key, ends)) & (query_segment < NSEQ)
        seen = seen & (key >= 0) & (query >= key) & (query - key < window)
        lane = lax.broadcasted_iota(jnp.int32, (2 * window, LANES), 1)
        twos = QUERY_PER_KEY // 2
        for g in range(groups):
            at = slice(g * LANES, (g + 1) * LANES)
            before = pair_ref[(block - 1) * window : block * window, at] if block else rim_ref[:, at]
            pairs = jnp.concatenate([before, pair_ref[rows, at]], axis=0).astype(jnp.float32)
            keys = jnp.where(lane < HEAD_SIZE, pairs, 0.0)
            values = jnp.where(lane < HEAD_SIZE, 0.0, pairs)
            keys = [x.astype(jnp.bfloat16) for x in (keys, pltpu.roll(keys, HEAD_SIZE, 1))]
            values = [x.astype(jnp.bfloat16) for x in (pltpu.roll(values, HEAD_SIZE, 1), values)]
            start = g * twos * LANES
            queries = jnp.concatenate(
                [q_ref[rows, start + two * LANES : start + (two + 1) * LANES] for two in range(twos)],
                axis=0,
            )
            made = jnp.zeros((twos * window, LANES), jnp.float32)
            for side in range(2):
                scores = lax.dot_general(
                    queries, keys[side], (((1,), (1,)), ((), ())), preferred_element_type=jnp.float32
                )
                probs = []
                for two in range(twos):
                    sink = sink_ref[g * QUERY_PER_KEY + 2 * two + side]
                    weights = jnp.where(
                        seen, jnp.exp(scores[two * window : (two + 1) * window]), 0.0
                    )
                    totals = jnp.sum(weights, axis=-1, keepdims=True)
                    totals = totals + jnp.exp(jnp.full_like(totals, sink))
                    probs.append((weights * (1.0 / totals)).astype(jnp.bfloat16))
                made = made + jnp.dot(
                    jnp.concatenate(probs, axis=0), values[side], preferred_element_type=jnp.float32
                )
            made = made.astype(jnp.bfloat16)
            for two in range(twos):
                columns = slice(start + two * LANES, start + (two + 1) * LANES)
                for part in range(window // row_count):
                    head = block * (window // row_count) + part
                    place = (head % 2 + core) % 2 * chips + head // 2
                    row = two * window + part * row_count
                    attended_ref[
                        pl.ds(pl.multiple_of(place * row_count, 16), row_count), columns
                    ] = made[row : row + row_count]

    @pl.when(pl.program_id(0) == 0)
    def _():
        window = rim_ref.shape[0]
        for block in range(q_ref.shape[0] // window):
            attend_block(block)

    product = lax.dot_general(
        attended_ref[...],
        w_ref[...],
        (((1,), (1,)), ((), ())),
        preferred_element_type=jnp.float32,
    )
    for chip in range(chips):
        at, then = chip * row_count, (chips + chip) * row_count
        kept_ref[chip] = product[at : at + row_count]
        sent_ref[chip] = product[then : then + row_count].astype(jnp.bfloat16)


def attend(ids, lengths, queries, rim, pairs, sinks, w_out, row_count):
    total, columns = queries.shape
    width = w_out.shape[0]
    chips = total // (2 * row_count)
    tile = PIECE
    whole = lambda i, ids: (0, 0)
    smem = pl.BlockSpec(memory_space=pltpu.SMEM)
    return pl.pallas_call(
        functools.partial(attend_kernel, row_count, chips),
        grid_spec=pltpu.PrefetchScalarGridSpec(
            num_scalar_prefetch=1,
            grid=(pl.cdiv(width, tile),),
            in_specs=[
                smem,
                pl.BlockSpec(queries.shape, whole),
                pl.BlockSpec(rim.shape, whole),
                pl.BlockSpec(pairs.shape, whole),
                smem,
                pl.BlockSpec((tile, columns), lambda i, ids: (i, 0)),
            ],
            out_specs=[pl.BlockSpec((chips, row_count, tile), lambda i, ids: (0, 0, i))] * 2,
            scratch_shapes=[pltpu.VMEM(queries.shape, jnp.bfloat16)],
        ),
        out_shape=[
            jax.ShapeDtypeStruct((chips, row_count, width), jnp.float32),
            jax.ShapeDtypeStruct((chips, row_count, width), jnp.bfloat16),
        ],
        compiler_params=pltpu.CompilerParams(vmem_limit_bytes=60 * MIB),
        cost_estimate=pl.CostEstimate(
            flops=2 * total * columns * width, bytes_accessed=2 * columns * width, transcendentals=0
        ),
        name="attend",
    )(ids, lengths, queries, rim, pairs, sinks, w_out)


def page_order(page_table, n_tok, pages_dev):
    page_grid = page_table.reshape(n_tok, pages_dev)
    target = page_grid // pages_dev
    page_ids = jnp.arange(pages_dev, dtype=jnp.int32)
    earlier = page_ids[:, None] > page_ids[None, :]
    same_dest = target[:, :, None] == target[:, None, :]
    order_rank = jnp.sum((same_dest & earlier[None]).astype(jnp.int32), axis=2)
    return (target, order_rank, page_grid % pages_dev)


def exchanged_pages(pairs, page_table, tok_id, n_tok):
    rows = pairs.shape[0]
    groups = pairs.shape[1] // (2 * HEAD_SIZE)
    pages_dev = rows // PAGE_TOKENS
    share_count = pages_dev // n_tok
    paged = pairs.reshape(pages_dev, PAGE_TOKENS, groups, 2 * HEAD_SIZE).transpose(0, 2, 1, 3)
    target, order_rank, _ = page_order(page_table, n_tok, pages_dev)
    dest_ids = jnp.arange(n_tok, dtype=jnp.int32)
    share_ids = jnp.arange(share_count, dtype=jnp.int32)
    page_ids = jnp.arange(pages_dev, dtype=jnp.int32)
    matched = (target[tok_id][:, None, None] == dest_ids[None, :, None]) & (
        order_rank[tok_id][:, None, None] == share_ids[None, None, :]
    )
    pick_page = jnp.sum(jnp.where(matched, page_ids[:, None, None], 0), axis=0).reshape(-1)
    sent = paged[pick_page].reshape(n_tok, share_count * groups * PAGE_TOKENS, 2 * HEAD_SIZE)
    return lax.all_to_all(sent, "tok", split_axis=0, concat_axis=0, tiled=True)


def landed_pages(arrived, page_table, tok_id, n_tok, groups):
    share_count = arrived.shape[1] // (groups * PAGE_TOKENS)
    pages_dev = n_tok * share_count
    arrived = arrived.reshape(pages_dev, groups, PAGE_TOKENS, 2 * HEAD_SIZE)
    target, order_rank, slot_grid = page_order(page_table, n_tok, pages_dev)
    share_ids = jnp.arange(share_count, dtype=jnp.int32)
    page_ids = jnp.arange(pages_dev, dtype=jnp.int32)
    to_here = (target == tok_id)[:, :, None] & (order_rank[:, :, None] == share_ids[None, None, :])
    landing = jnp.sum(jnp.where(to_here, slot_grid[:, :, None], 0), axis=1).reshape(-1)
    source = jnp.sum(
        jnp.where(landing[None, :] == page_ids[:, None], page_ids[None, :], 0), axis=1
    )
    return arrived[source].transpose(1, 0, 2, 3)


def per_device(
    tokens,
    lengths,
    norm_gain_attn,
    query_key_value_weight,
    sinks,
    w_out_attn,
    norm_gain_moe,
    routes,
    gates,
    w_in,
    w_down,
    page_table,
):
    n_tok = lax.axis_size("tok")
    n_head = lax.axis_size("head")
    tok_id = lax.axis_index("tok")
    head_id = lax.axis_index("head")
    row_count, width = tokens.shape
    tok_dev = row_count * n_head
    groups = sinks.shape[0] // QUERY_PER_KEY
    n_y = n_head // 2
    y_id, core = head_id // 2, head_id % 2

    def to_core(array):
        return lax.ppermute(array, "head", [(h, h ^ 1) for h in range(n_head)])

    def along_y(array, by):
        return lax.ppermute(
            array, "head", [(h, (h // 2 + by) % n_y * 2 + h % 2) for h in range(n_head)]
        )

    n_dev = n_tok * n_head
    half = n_dev // 2

    def across(array):
        return lax.ppermute(array, ("tok", "head"), [(d, d ^ half) for d in range(n_dev)])

    def in_half(array):
        return lax.all_to_all(
            array,
            ("tok", "head"),
            split_axis=0,
            concat_axis=0,
            tiled=True,
            axis_index_groups=[list(range(half)), list(range(half, n_dev))],
        )

    flat_id = tok_id * n_head + head_id
    ids = jnp.stack([core, y_id, tok_id, flat_id]).astype(jnp.int32)
    choice = jnp.concatenate([routes.T.astype(jnp.float32), gates.T], axis=0)
    far_choice = across(choice)

    capacity = row_count // 8 + 2
    shards = n_dev // EXPERTS
    extras = capacity > MAIN_SLOTS
    tables = functools.partial(slot_tables, ids, lengths)
    sizes = (half, EXPERTS // 2, shards, extras)
    slots = tables(choice, False, *sizes), tables(far_choice, True, *sizes)

    placed, block = [], tokens
    for k in range(n_y):
        if k:
            block, slots = lax.optimization_barrier((along_y(tokens, k), slots))
        placed = project(
            ids,
            lengths,
            k,
            n_y,
            block,
            to_core(block),
            norm_gain_attn,
            query_key_value_weight,
            placed,
        )
    (own_picks, own_weights), (far_picks, far_weights) = slots
    query_rows, key_value_pairs = placed
    rim_rows = passed_along(key_value_pairs[tok_dev - ATTEND_WINDOW :], "tok", 1)
    kept, sent = attend(
        ids, lengths, query_rows, rim_rows, key_value_pairs, sinks, w_out_attn.T, row_count
    )
    sent = to_core(sent)

    def chip_sum(chip):
        here = lax.dynamic_index_in_dim(kept, chip, 0, keepdims=False)
        there = lax.dynamic_index_in_dim(sent, chip, 0, keepdims=False)
        return here + there.astype(jnp.float32)

    own_sum = chip_sum(y_id)
    leaving = [chip_sum((y_id + k) % n_y).astype(jnp.bfloat16) for k in range(1, n_y)]
    leaving, key_value_pairs = lax.optimization_barrier((leaving, key_value_pairs))
    other_sums = jnp.stack([along_y(part, k + 1) for k, part in enumerate(leaving)])
    pages = exchanged_pages(key_value_pairs, page_table, tok_id, n_tok)
    other_sums, pages = lax.optimization_barrier((other_sums, pages))

    resid, moe_in = finish_attention(
        tokens, own_sum, other_sums, norm_gain_moe
    )
    far_moe_in = across(moe_in)
    own_packed = pack(moe_in, own_picks, 64 * MIB)

    def exchanged(packed):
        slots, held = packed.shape
        return in_half(packed.reshape(half, MAIN_SLOTS, held)).reshape(slots, held)

    far_packed = pack(far_moe_in, far_picks, MIB)
    far_arrived = exchanged(far_packed)
    far_arrived, own_packed = lax.optimization_barrier((far_arrived, own_packed))
    own_arrived = exchanged(own_packed)
    far_made = expert(far_arrived, w_in, w_down, extras)
    far_made, own_arrived = lax.optimization_barrier((far_made, own_arrived))
    far_returned = exchanged(far_made)
    own_act = expert(own_arrived, w_in, w_down, extras, down=False)
    far_returned, own_act = lax.optimization_barrier((far_returned, own_act))
    far_part, own_act = lax.optimization_barrier((combine(far_returned, far_weights), own_act))
    far_sum = across(far_part)
    own_returned = lax.fori_loop(
        0,
        jnp.minimum(lengths[0], 1),
        lambda _, held: exchanged(expert_down(own_act, w_down, *held.shape, extras)),
        own_packed,
    )
    hidden_out = combine(own_returned, own_weights, resid, far_sum)
    kv_cache = landed_pages(pages, page_table, tok_id, n_tok, groups)
    return (hidden_out, kv_cache)


def solution(mesh):
    return jax.shard_map(
        per_device,
        mesh=mesh,
        in_specs=(
            P(("tok", "head"), None),
            P(),
            P(),
            P(None, "head"),
            P("head"),
            P("head", None),
            P(),
            P(("tok", "head"), None),
            P(("tok", "head"), None),
            P(("tok", "head"), None, None),
            P(("tok", "head"), None, None),
            P(),
        ),
        out_specs=(P(("tok", "head"), None), P("head", "tok", None, None)),
        check_vma=False,
    )
```

time: 306 us -> 193 us (0.63)
  waiting for transfers between devices: 171 us -> 55.8 us
  Pallas kernels: 0 us -> 77.3 us
  matrix products: 46.3 us -> 0 us
  local copies, waits for them, and re-layouts: 32.3 us -> 9.54 us
  other arithmetic: 22.6 us -> 3.72 us
  blocking collectives: 0 us -> 13.9 us
  between operations: 14.5 us -> 0.98 us
  starting transfers between devices: 18.9 us -> 30.3 us
    all_to_all x3 -> x4, waiting for transfers between devices: 123 us -> 34.6 us  [in_half(): lax.all_to_all(array, ('tok', 'head'), split_axis=0, concat_axis=0, tiled...]
    pallas_call x0 -> x13, Pallas kernels: none -> 77.3 us  [the longest x2 38.4 us: expert(): pl.pallas_call(functools.partial(expert_kernel, extras, in_tiles, down),...]
    dot_general x6 -> x0, matrix products: 46.3 us -> none  [the longest x1 20.8 us: expert_mlp(): gate_up = jnp.dot(rows_in, w_in_local, preferred_element_type=jnp.float32)]
    reduce_scatter x1 -> x0, waiting for transfers between devices: 27 us -> none  [per_device(): lax.psum_scatter(jnp.dot(attended, w_out_attn, preferred_element_type=jnp...]
    all_gather x1 -> x0, waiting for transfers between devices: 19.6 us -> none  [per_device(): lax.all_gather(normed_input, 'head', axis=0, tiled=True)]
    ppermute x0 -> x8, waiting for transfers between devices: none -> 19.2 us  [the longest x3 17.1 us: across(): lax.ppermute(array, ('tok', 'head'), [(d, d ^ half) for d in range(n_dev)])]
    all_to_all x0 -> x1, blocking collectives: none -> 13.9 us  [exchanged_pages(): return lax.all_to_all(sent, 'tok', split_axis=0, concat_axis=0, tiled=True)]
    gather x5 -> x2, local copies, waits for them, and re-layouts: 13.7 us -> 1.15 us  [the longest x1 0.58 us: exchanged_pages(): paged[pick_page]]
  transfers between devices with their start and end apart: 6 -> 13, of which waited for: 5 -> 6; matrix products, arithmetic and copies ran while one was open for 19% -> 4% of each run, Pallas kernels for 0% -> 25%
where the time goes in v1:
time: 193 us; the launch traced here: 192 us
  Pallas kernels  77.3 us (40%)
  waiting for transfers between devices  55.8 us (29%)
  starting transfers between devices  30.3 us (16%)
  blocking collectives  13.9 us (7%)
  local copies, waits for them, and re-layouts  9.54 us (5%)
  other arithmetic  3.72 us (2%)
    pallas_call x2, Pallas kernels, expert(): pl.pallas_call(functools.partial(expert_kernel, extras, in_tiles, down),...  38.4 us
    all_to_all x4, waiting for transfers between devices, in_half(): lax.all_to_all(array, ('tok', 'head'), split_axis=0, concat_axis=0, tiled...  34.6 us
    all_to_all x4, starting transfers between devices, in_half(): lax.all_to_all(array, ('tok', 'head'), split_axis=0, concat_axis=0, tiled...  18.1 us
    ppermute x3, waiting for transfers between devices, across(): lax.ppermute(array, ('tok', 'head'), [(d, d ^ half) for d in range(n_dev)])  17.1 us
    all_to_all x1, blocking collectives, exchanged_pages(): return lax.all_to_all(sent, 'tok', split_axis=0, concat_axis=0, tiled=True)  13.9 us
    pallas_call x2, Pallas kernels, project(): pl.pallas_call(functools.partial(qkv_kernel, step, chips), grid_spec=pltp...  11.9 us
    pallas_call x1, Pallas kernels, expert_down(): pl.pallas_call(functools.partial(down_kernel, extras, width), grid=(PIECE...  9.49 us
    pallas_call x1, Pallas kernels, attend(): pl.pallas_call(functools.partial(attend_kernel, row_count, chips), grid_s...  9.06 us
  transfers between devices with their start and end apart: 13, of which 6 were waited for; matrix products, arithmetic and copies ran while one was open for 4% of the time, Pallas kernels for 25%

profile of v1, /device:TPU:0, one launch (start us, length us, event | category | flops | bytes accessed | tf_op | source)
XLA Modules:
  0.0 191.6 jit_solution(12442351769478206365)
XLA Ops:
  0.6 3.0 %collective-permute-start = (bf16[64,2880]{1,0:T(8,128)(2,1)}, bf16[64,2880]{1,0:T(8,128)(2,1)S(1)}, u32[]{:S(2)}, u32[]{:S(2)}) collective-permute-start(bf16[64,2880]{1,0:T(8,128)(2,1)} %tokens_ref.1), channel_id=1, source_target_pairs={{0,2},{1,3},{2,0},{3,1},{4,6},{5,7},{6,4},{7,5},{8,10},{9,11},{10,... | collective-permute-start | bytes 1105928 | tf_op jit(solution)/shard_map/ppermute | solution.py:651
  3.7 0.7 convert_bitcast_fusion
  4.3 0.7 pad_maximum_fusion.choice_ref
  5.0 2.6 %collective-permute-start.1 = (f32[8,64]{1,0:T(8,128)S(1)}, f32[8,64]{1,0:T(8,128)S(1)}, u32[]{:S(2)}, u32[]{:S(2)}) collective-permute-start(f32[8,64]{1,0:T(8,128)S(1)} %pad_maximum_fusion.choice_ref), channel_id=1, source_target_pairs={{0,16},{1,17},{2,18},{3,19},{4,20},{5,21},{6,22},{7,23},{8,24},{9,... | collective-permute-start | bytes 6152 | tf_op jit(solution)/shard_map/ppermute | solution.py:659
  7.6 0.7 reshape.250
  8.4 0.3 convert_reduce_fusion
  8.8 0.7 copy-done.2
  9.4 1.0 slots.2
  10.5 0.6 copy-done.3
  11.2 1.0 slots.3
  12.2 0.4 collective-permute-done.own_ref
  12.7 0.8 copy-done.9
  13.5 6.0 %project.2 = (bf16[256,1024]{1,0:T(8,128)(2,1)}, bf16[256,256]{1,0:T(8,128)(2,1)}) custom-call(s32[4]{0:T(128)} %copy-done.1, s32[4]{0:T(128)} %lengths_ref.9, bf16[64,2880]{1,0:T(8,128)(2,1)} %tokens_ref.1, bf16[64,2880]{1,0:T(8,128)(2,1)} %copy-done.9, f32[2880]{0:T(1024)} %gain_ref.4, bf16[2880,1280]{1,0:T(8,128)(2,1)} %w_ref.3), custom_call_target="tpu_custom_call" | custom-call | flops 943718400 | bytes 7372800 | tf_op jit(solution)/shard_map/project/pallas_call | solution.py:113
  19.5 0.7 copy-done.10
  20.2 6.0 %project.3 = (bf16[256,1024]{1,0:T(8,128)(2,1)}, bf16[256,256]{1,0:T(8,128)(2,1)}) custom-call(s32[4]{0:T(128)} %copy-done.1, s32[4]{0:T(128)} %lengths_ref.9, bf16[64,2880]{1,0:T(8,128)(2,1)} %copy-done.8, bf16[64,2880]{1,0:T(8,128)(2,1)} %copy-done.10, f32[2880]{0:T(1024)} %gain_ref.4, ...), custom_call_target="tpu_custom_call", output_to_operand_aliasing={{0}: (6, {}), {1}: (7, {})} | custom-call | flops 943718400 | bytes 7372800 | tf_op jit(solution)/shard_map/project/pallas_call | solution.py:113
  26.2 0.9 slice.6
  27.1 3.6 %collective-permute-start.4 = (bf16[128,256]{1,0:T(8,128)(2,1)S(1)}, bf16[128,256]{1,0:T(8,128)(2,1)S(1)}, u32[]{:S(2)}, u32[]{:S(2)}) collective-permute-start(bf16[128,256]{1,0:T(8,128)(2,1)S(1)} %slice.6), channel_id=1, source_target_pairs={{0,4},{4,8},{8,12},{12,16},{16,20},{20,24},{24,28},{1,5},{5,9},{9,... | collective-permute-start | bytes 196616 | tf_op jit(solution)/shard_map/ppermute | solution.py:36
  30.7 1.9 %collective-permute-done.4.rim_ref = bf16[128,256]{1,0:T(8,128)(2,1)S(1)} collective-permute-done((bf16[128,256]{1,0:T(8,128)(2,1)S(1)}, bf16[128,256]{1,0:T(8,128)(2,1)S(1)}, u32[]{:S(2)}, u32[]{:S(2)}) %collective-permute-start.4) | collective-permute-done | bytes 65568 | tf_op jit(solution)/shard_map/ppermute | solution.py:36
  32.6 0.6 copy-done.11
  33.3 9.1 %attend.1 = (f32[2,64,2880]{2,1,0:T(8,128)}, bf16[2,64,2880]{2,1,0:T(8,128)(2,1)}) custom-call(s32[4]{0:T(128)} %copy-done.1, s32[4]{0:T(128)} %lengths_ref.9, bf16[256,1024]{1,0:T(8,128)(2,1)} %get-tuple-element.93.q_ref, bf16[128,256]{1,0:T(8,128)(2,1)} %copy-done.11, bf16[256,256]{1,0:T(8,128)(2,1)} %get-tuple-element.98.pair_ref, f32[16]{0:T(128)} %sink_ref.1, ...), custom_call_target="tpu_custom_call" | custom-call | flops 1509949440 | bytes 5898240 | tf_op jit(solution)/shard_map/attend/pallas_call | solution.py:552
  42.3 0.1 select_reduce_fusion.2
  42.7 0.1 select_reduce_fusion.1
  43.1 1.7 collective-permute-done.5
  44.8 1.5 fusion
  46.3 1.6 collective-permute-start.6
  48.0 0.6 gather_fusion
  48.5 13.9 %all_to_all.27 = bf16[8,64,128]{2,1,0:T(8,128)(2,1)S(1)} all-to-all(bf16[8,64,128]{2,1,0:T(8,128)(2,1)S(1)} %bitcast.50), channel_id=1, replica_groups=mesh['tok'=8,'head'=4] {'tok'}, dimensions={0} | all-to-all | bytes 262144 | tf_op jit(solution)/shard_map/all_to_all | solution.py:605
  62.5 0.3 finish_attention.1
  62.8 0.5 collective-permute-start.7
  63.3 17.1 %collective-permute-done.7.moe_ref = bf16[64,2880]{1,0:T(8,128)(2,1)S(1)} collective-permute-done((bf16[64,2880]{1,0:T(8,128)(2,1)S(1)}, bf16[64,2880]{1,0:T(8,128)(2,1)S(1)}, u32[]{:S(2)}, u32[]{:S(2)}) %collective-permute-start.7) | collective-permute-done | bytes 368672 | tf_op jit(solution)/shard_map/ppermute | solution.py:659
  80.3 1.5 pack.2
  81.8 3.6 %all-to-all-start.1 = ((bf16[16,8,3712]{2,1,0:T(8,128)(2,1)}), bf16[16,8,3712]{2,1,0:T(8,128)(2,1)S(1)}, u32[]{:S(2)}, u32[]{:S(2)}) async-start(bf16[16,8,3712]{2,1,0:T(8,128)(2,1)} %bitcast.16), calls=%async_computation.1 | async-start | bytes 1900544 | tf_op jit(solution)/shard_map/all_to_all | solution.py:662
  85.5 1.5 pack.3
  87.0 13.6 %all-to-all-done.1 = bf16[16,8,3712]{2,1,0:T(8,128)(2,1)S(1)} async-done(((bf16[16,8,3712]{2,1,0:T(8,128)(2,1)}), bf16[16,8,3712]{2,1,0:T(8,128)(2,1)S(1)}, u32[]{:S(2)}, u32[]{:S(2)}) %all-to-all-start.1) | async-done | bytes 950304 | tf_op jit(solution)/shard_map/all_to_all | solution.py:662
  100.6 4.5 %all-to-all-start.2 = ((bf16[16,8,3712]{2,1,0:T(8,128)(2,1)}), bf16[16,8,3712]{2,1,0:T(8,128)(2,1)}, u32[]{:S(2)}, u32[]{:S(2)}) async-start(bf16[16,8,3712]{2,1,0:T(8,128)(2,1)} %bitcast.19), calls=%async_computation.2 | async-start | bytes 1900544 | tf_op jit(solution)/shard_map/all_to_all | solution.py:662
  105.1 23.1 %expert.1 = bf16[128,3712]{1,0:T(8,128)(2,1)} custom-call(bf16[128,3712]{1,0:T(8,128)(2,1)} %bitcast.45, bf16[1,2880,5760]{2,1,0:T(8,128)(2,1)} %refs_1_.3, bf16[1,2880,2880]{2,1,0:T(8,128)(2,1)} %w_down_ref), custom_call_target="tpu_custom_call" | custom-call | flops 7962624000 | bytes 49766400 | tf_op jit(solution)/shard_map/expert/pallas_call | solution.py:336
  128.2 4.8 %all-to-all-start.3 = ((bf16[16,8,3712]{2,1,0:T(8,128)(2,1)}), bf16[16,8,3712]{2,1,0:T(8,128)(2,1)S(1)}, u32[]{:S(2)}, u32[]{:S(2)}) async-start(bf16[16,8,3712]{2,1,0:T(8,128)(2,1)} %bitcast.46), calls=%async_computation.3 | async-start | bytes 1900544 | tf_op jit(solution)/shard_map/all_to_all | solution.py:662
  133.0 15.3 %expert_up.1.act_ref = bf16[160,2880]{1,0:T(8,128)(2,1)} custom-call(bf16[128,3712]{1,0:T(8,128)(2,1)} %bitcast.20.refs_0_, bf16[1,2880,5760]{2,1,0:T(8,128)(2,1)} %refs_1_.3), custom_call_target="tpu_custom_call" | custom-call | flops 5308416000 | bytes 33177600 | tf_op jit(solution)/shard_map/expert_up/pallas_call | solution.py:336
  148.3 0.6 combine.2
  148.9 9.5 %expert_down.3 = bf16[128,3712]{1,0:T(8,128)(2,1)} custom-call(bf16[160,2880]{1,0:T(8,128)(2,1)} %expert_up.1.act_ref, bf16[1,2880,2880]{2,1,0:T(8,128)(2,1)} %w_down_ref), custom_call_target="tpu_custom_call" | custom-call | flops 2654208000 | bytes 16588800 | tf_op jit(solution)/shard_map/while/body/expert_down/pallas_call | solution.py:357
  158.4 5.2 %all-to-all-start.4 = ((bf16[16,8,3712]{2,1,0:T(8,128)(2,1)}), bf16[16,8,3712]{2,1,0:T(8,128)(2,1)}, u32[]{:S(2)}, u32[]{:S(2)}) async-start(bf16[16,8,3712]{2,1,0:T(8,128)(2,1)} %bitcast.47), calls=%async_computation.4 | async-start | bytes 1900544 | tf_op jit(solution)/shard_map/while/body/all_to_all | solution.py:662
  163.6 0.9 collective-permute-start.8
  164.6 0.6 gather_fusion.1
  165.2 0.7 copy.22
  165.8 21.0 %all-to-all-done.4 = bf16[16,8,3712]{2,1,0:T(8,128)(2,1)} async-done(((bf16[16,8,3712]{2,1,0:T(8,128)(2,1)}), bf16[16,8,3712]{2,1,0:T(8,128)(2,1)}, u32[]{:S(2)}, u32[]{:S(2)}) %all-to-all-start.4) | async-done | bytes 950304 | tf_op jit(solution)/shard_map/while/body/all_to_all | solution.py:662
  186.8 2.2 %while.12 = (s32[]{:T(128)}, bf16[128,3712]{1,0:T(8,128)(2,1)}, s32[]{:T(128)}, bf16[16,8,3712]{2,1,0:T(8,128)(2,1)}, s32[]{:T(128)}) while((s32[]{:T(128)}, bf16[128,3712]{1,0:T(8,128)(2,1)}, s32[]{:T(128)}, bf16[16,8,3712]{2,1,0:T(8,128)(2,1)}, s32[]{:T(128)}) %tuple.49), condition=%wide.region_3.4_spmd, body=%wide.region_2.3_spmd.sunk | while | flops 2 | bytes 1900605 | solution.py:739
  186.8 2.2 %copy.32 = bf16[128,3712]{1,0:T(8,128)(2,1)} copy(bf16[128,3712]{1,0:T(8,128)(2,1)} %bitcast.40) | data formatting | bytes 1900544 | tf_op jit(solution)/shard_map/while
  189.0 2.5 %combine.3 = bf16[64,2880]{1,0:T(8,128)(2,1)} custom-call(bf16[128,3712]{1,0:T(8,128)(2,1)} %get-tuple-element.111.made_ref, bf16[2,5,64,128]{3,2,1,0:T(8,128)(2,1)S(1)} %get-tuple-element.112.weight_ref, f32[64,2880]{1,0:T(8,128)S(1)} %get-tuple-element.113.resid_ref, bf16[64,2880]{1,0:T(8,128)(2,1)S(1)} %collective-permute-done.8.far_ref), custom_call_target="tpu_custom_call" | custom-call | tf_op jit(solution)/shard_map/combine/pallas_call | solution.py:407
  (47 shorter events, 0.7 us)
Async XLA Ops:
  0.6 12.0 %collective-permute-start = (bf16[64,2880]{1,0:T(8,128)(2,1)}, bf16[64,2880]{1,0:T(8,128)(2,1)S(1)}, u32[]{:S(2)}, u32[]{:S(2)}) collective-permute-start(bf16[64,2880]{1,0:T(8,128)(2,1)} %tokens_ref.1), channel_id=1, source_target_pairs={{0,2},{1,3},{2,0},{3,1},{4,6},{5,7},{6,4},{7,5},{8,10},{9,11},{10,... | collective-permute-start | bytes 1105928 | tf_op jit(solution)/shard_map/ppermute | solution.py:651
  3.7 9.0 %collective-permute-start.3 = (bf16[64,2880]{1,0:T(8,128)(2,1)}, bf16[64,2880]{1,0:T(8,128)(2,1)S(1)}, u32[]{:S(2)}, u32[]{:S(2)}) collective-permute-start(bf16[64,2880]{1,0:T(8,128)(2,1)} %tokens_ref.1), channel_id=1, source_target_pairs={{0,1},{1,0},{2,3},{3,2},{4,5},{5,4},{6,7},{7,6},{8,9},{9,8},{10,11... | collective-permute-start | bytes 1105928 | tf_op jit(solution)/shard_map/ppermute | solution.py:648
  5.0 5.4 %collective-permute-start.1 = (f32[8,64]{1,0:T(8,128)S(1)}, f32[8,64]{1,0:T(8,128)S(1)}, u32[]{:S(2)}, u32[]{:S(2)}) collective-permute-start(f32[8,64]{1,0:T(8,128)S(1)} %pad_maximum_fusion.choice_ref), channel_id=1, source_target_pairs={{0,16},{1,17},{2,18},{3,19},{4,20},{5,21},{6,22},{7,23},{8,24},{9,... | collective-permute-start | bytes 6152 | tf_op jit(solution)/shard_map/ppermute | solution.py:659
  8.8 3.9 %copy-start.1 = (s32[4]{0:T(128)}, s32[4]{0:T(128)S(1)}, u32[]{:S(2)}) copy-start(s32[4]{0:T(128)S(1)} %pad_add_fusion.ids_ref) | copy-start | bytes 52
  8.8 0.7 copy-start.2
  10.5 0.7 copy-start.3
  12.6 6.8 %copy-start.8 = (bf16[64,2880]{1,0:T(8,128)(2,1)}, bf16[64,2880]{1,0:T(8,128)(2,1)S(1)}, u32[]{:S(2)}) copy-start(bf16[64,2880]{1,0:T(8,128)(2,1)S(1)} %collective-permute-done.own_ref) | copy-start | bytes 1105924
  12.6 6.8 %collective-permute-start.2 = (bf16[64,2880]{1,0:T(8,128)(2,1)S(1)}, bf16[64,2880]{1,0:T(8,128)(2,1)S(1)}, u32[]{:S(2)}, u32[]{:S(2)}) collective-permute-start(bf16[64,2880]{1,0:T(8,128)(2,1)S(1)} %collective-permute-done.own_ref), channel_id=1, source_target_pairs={{0,1},{1,0},{2,3},{3,2},{4,5},{5,4},{6,7},{7,6},{8,9},{9,8},{10,11... | collective-permute-start | bytes 1105928 | tf_op jit(solution)/shard_map/ppermute | solution.py:648
  12.7 0.8 copy-start.9
  19.5 0.7 copy-start.10
  26.2 21.7 %copy-start.7 = (bf16[256,256]{1,0:T(8,128)(2,1)S(1)}, bf16[256,256]{1,0:T(8,128)(2,1)}, u32[]{:S(2)}) copy-start(bf16[256,256]{1,0:T(8,128)(2,1)} %get-tuple-element.98.pair_ref) | copy-start | bytes 393220
  26.2 36.3 %copy-start = (bf16[64,2880]{1,0:T(8,128)(2,1)S(1)}, bf16[64,2880]{1,0:T(8,128)(2,1)}, u32[]{:S(2)}) copy-start(bf16[64,2880]{1,0:T(8,128)(2,1)} %tokens_ref.1) | copy-start | bytes 1105924
  26.2 36.3 %copy-start.5 = (f32[2880]{0:T(1024)S(1)}, f32[2880]{0:T(1024)}, u32[]{:S(2)}) copy-start(f32[2880]{0:T(1024)} %gain_ref.5) | copy-start | bytes 34564
  27.1 5.5 %collective-permute-start.4 = (bf16[128,256]{1,0:T(8,128)(2,1)S(1)}, bf16[128,256]{1,0:T(8,128)(2,1)S(1)}, u32[]{:S(2)}, u32[]{:S(2)}) collective-permute-start(bf16[128,256]{1,0:T(8,128)(2,1)S(1)} %slice.6), channel_id=1, source_target_pairs={{0,4},{4,8},{8,12},{12,16},{16,20},{20,24},{24,28},{1,5},{5,9},{9,... | collective-permute-start | bytes 196616 | tf_op jit(solution)/shard_map/ppermute | solution.py:36
  32.6 0.6 copy-start.11
  42.3 2.4 %collective-permute-start.5 = (bf16[2,64,2880]{2,1,0:T(8,128)(2,1)}, bf16[2,64,2880]{2,1,0:T(8,128)(2,1)S(1)}, u32[]{:S(2)}, u32[]{:S(2)}) collective-permute-start(bf16[2,64,2880]{2,1,0:T(8,128)(2,1)} %get-tuple-element.96), channel_id=1, source_target_pairs={{0,1},{1,0},{2,3},{3,2},{4,5},{5,4},{6,7},{7,6},{8,9},{9,8},{10,11... | collective-permute-start | bytes 2211848 | tf_op jit(solution)/shard_map/ppermute | solution.py:648
  46.3 16.2 %collective-permute-start.6 = (bf16[64,2880]{1,0:T(8,128)(2,1)S(1)}, bf16[64,2880]{1,0:T(8,128)(2,1)S(1)}, u32[]{:S(2)}, u32[]{:S(2)}) collective-permute-start(bf16[64,2880]{1,0:T(8,128)(2,1)S(1)} %get-tuple-element.97), channel_id=1, source_target_pairs={{0,2},{1,3},{2,0},{3,1},{4,6},{5,7},{6,4},{7,5},{8,10},{9,11},{10,... | collective-permute-start | bytes 1105928 | tf_op jit(solution)/shard_map/ppermute | solution.py:651
  62.8 17.5 %collective-permute-start.7 = (bf16[64,2880]{1,0:T(8,128)(2,1)S(1)}, bf16[64,2880]{1,0:T(8,128)(2,1)S(1)}, u32[]{:S(2)}, u32[]{:S(2)}) collective-permute-start(bf16[64,2880]{1,0:T(8,128)(2,1)S(1)} %get-tuple-element.100.moe_ref), channel_id=1, source_target_pairs={{0,16},{1,17},{2,18},{3,19},{4,20},{5,21},{6,22},{7,23},{8,24},{9,... | collective-permute-start | bytes 1105928 | tf_op jit(solution)/shard_map/ppermute | solution.py:659
  81.8 18.8 %all-to-all-start.1 = ((bf16[16,8,3712]{2,1,0:T(8,128)(2,1)}), bf16[16,8,3712]{2,1,0:T(8,128)(2,1)S(1)}, u32[]{:S(2)}, u32[]{:S(2)}) async-start(bf16[16,8,3712]{2,1,0:T(8,128)(2,1)} %bitcast.16), calls=%async_computation.1 | async-start | bytes 1900544 | tf_op jit(solution)/shard_map/all_to_all | solution.py:662
  100.6 4.5 %copy-start.6 = (bf16[16,8,3712]{2,1,0:T(8,128)(2,1)}, bf16[16,8,3712]{2,1,0:T(8,128)(2,1)S(1)}, u32[]{:S(2)}) copy-start(bf16[16,8,3712]{2,1,0:T(8,128)(2,1)S(1)} %all-to-all-done.1) | copy-start | bytes 2850820
  100.6 27.6 %all-to-all-start.2 = ((bf16[16,8,3712]{2,1,0:T(8,128)(2,1)}), bf16[16,8,3712]{2,1,0:T(8,128)(2,1)}, u32[]{:S(2)}, u32[]{:S(2)}) async-start(bf16[16,8,3712]{2,1,0:T(8,128)(2,1)} %bitcast.19), calls=%async_computation.2 | async-start | bytes 1900544 | tf_op jit(solution)/shard_map/all_to_all | solution.py:662
  128.2 20.1 %all-to-all-start.3 = ((bf16[16,8,3712]{2,1,0:T(8,128)(2,1)}), bf16[16,8,3712]{2,1,0:T(8,128)(2,1)S(1)}, u32[]{:S(2)}, u32[]{:S(2)}) async-start(bf16[16,8,3712]{2,1,0:T(8,128)(2,1)} %bitcast.46), calls=%async_computation.3 | async-start | bytes 1900544 | tf_op jit(solution)/shard_map/all_to_all | solution.py:662
  148.9 15.6 %copy-start.4 = (s32[4]{0:T(128)S(1)}, s32[4]{0:T(128)}, u32[]{:S(2)}) copy-start(s32[4]{0:T(128)} %lengths_ref.9) | copy-start | bytes 52
  158.4 28.4 %all-to-all-start.4 = ((bf16[16,8,3712]{2,1,0:T(8,128)(2,1)}), bf16[16,8,3712]{2,1,0:T(8,128)(2,1)}, u32[]{:S(2)}, u32[]{:S(2)}) async-start(bf16[16,8,3712]{2,1,0:T(8,128)(2,1)} %bitcast.47), calls=%async_computation.4 | async-start | bytes 1900544 | tf_op jit(solution)/shard_map/while/body/all_to_all | solution.py:662
  163.6 25.5 %collective-permute-start.8 = (bf16[64,2880]{1,0:T(8,128)(2,1)S(1)}, bf16[64,2880]{1,0:T(8,128)(2,1)S(1)}, u32[]{:S(2)}, u32[]{:S(2)}) collective-permute-start(bf16[64,2880]{1,0:T(8,128)(2,1)S(1)} %combine.2), channel_id=1, source_target_pairs={{0,16},{1,17},{2,18},{3,19},{4,20},{5,21},{6,22},{7,23},{8,24},{9,... | collective-permute-start | bytes 1105928 | tf_op jit(solution)/shard_map/ppermute | solution.py:659

commit v2 on v1

--- a/solution.py
+++ b/solution.py
@@ -678,12 +678,10 @@
     extras = capacity > MAIN_SLOTS
     tables = functools.partial(slot_tables, ids, lengths)
     sizes = (half, EXPERTS // 2, shards, extras)
-    slots = tables(choice, False, *sizes), tables(far_choice, True, *sizes)
-
     placed, block = [], tokens
     for k in range(n_y):
         if k:
-            block, slots = lax.optimization_barrier((along_y(tokens, k), slots))
+            block, placed = lax.optimization_barrier((along_y(tokens, k), placed))
         placed = project(
             ids,
             lengths,
@@ -695,9 +693,12 @@
             query_key_value_weight,
             placed,
         )
-    (own_picks, own_weights), (far_picks, far_weights) = slots
+    placed, choice, far_choice = lax.optimization_barrier((placed, choice, far_choice))
     query_rows, key_value_pairs = placed
     rim_rows = passed_along(key_value_pairs[tok_dev - ATTEND_WINDOW :], "tok", 1)
+    slots = tables(choice, False, *sizes), tables(far_choice, True, *sizes)
+    rim_rows, slots = lax.optimization_barrier((rim_rows, slots))
+    (own_picks, own_weights), (far_picks, far_weights) = slots
     kept, sent = attend(
         ids, lengths, query_rows, rim_rows, key_value_pairs, sinks, w_out_attn.T, row_count
     )
@@ -725,23 +726,22 @@
         slots, held = packed.shape
         return in_half(packed.reshape(half, MAIN_SLOTS, held)).reshape(slots, held)
 
-    far_packed = pack(far_moe_in, far_picks, MIB)
-    far_arrived = exchanged(far_packed)
-    far_arrived, own_packed = lax.optimization_barrier((far_arrived, own_packed))
-    own_arrived = exchanged(own_packed)
+    def exchanged_beside(packed):
+        return lax.cond(lengths[0] > 0, exchanged, jnp.zeros_like, packed)
+
+    own_arrived = exchanged_beside(own_packed)
+    far_moe_in, own_arrived = lax.optimization_barrier((far_moe_in, own_arrived))
+    far_arrived = exchanged(pack(far_moe_in, far_picks, MIB))
+    own_act = expert(own_arrived, w_in, w_down, extras, down=False)
+    far_arrived, own_act = lax.optimization_barrier((far_arrived, own_act))
     far_made = expert(far_arrived, w_in, w_down, extras)
-    far_made, own_arrived = lax.optimization_barrier((far_made, own_arrived))
+    far_made, own_act = lax.optimization_barrier((far_made, own_act))
     far_returned = exchanged(far_made)
-    own_act = expert(own_arrived, w_in, w_down, extras, down=False)
-    far_returned, own_act = lax.optimization_barrier((far_returned, own_act))
-    far_part, own_act = lax.optimization_barrier((combine(far_returned, far_weights), own_act))
+    own_made = expert_down(own_act, w_down, *own_packed.shape, extras)
+    far_returned, own_made = lax.optimization_barrier((far_returned, own_made))
+    far_part, own_made = lax.optimization_barrier((combine(far_returned, far_weights), own_made))
     far_sum = across(far_part)
-    own_returned = lax.fori_loop(
-        0,
-        jnp.minimum(lengths[0], 1),
-        lambda _, held: exchanged(expert_down(own_act, w_down, *held.shape, extras)),
-        own_packed,
-    )
+    own_returned = exchanged_beside(own_made)
     hidden_out = combine(own_returned, own_weights, resid, far_sum)
     kv_cache = landed_pages(pages, page_table, tok_id, n_tok, groups)
     return (hidden_out, kv_cache)

time: 193 us -> 182 us (0.943)
  blocking collectives: 13.9 us -> 64.3 us
  waiting for transfers between devices: 55.8 us -> 8.69 us
  starting transfers between devices: 30.3 us -> 20.4 us
  local copies, waits for them, and re-layouts: 9.54 us -> 5.99 us
    all_to_all x0 -> x2, blocking collectives: none -> 52.1 us  [in_half(): lax.all_to_all(array, ('tok', 'head'), split_axis=0, concat_axis=0, tiled...]
    all_to_all x4 -> x2, waiting for transfers between devices: 34.6 us -> 5.66 us  [in_half(): lax.all_to_all(array, ('tok', 'head'), split_axis=0, concat_axis=0, tiled...]
    ppermute x3, waiting for transfers between devices: 17.1 us -> 0.01 us  [across(): lax.ppermute(array, ('tok', 'head'), [(d, d ^ half) for d in range(n_dev)])]
    all_to_all x4 -> x2, starting transfers between devices: 18.1 us -> 9.33 us  [in_half(): lax.all_to_all(array, ('tok', 'head'), split_axis=0, concat_axis=0, tiled...]
    while x1 -> x0, local copies, waits for them, and re-layouts: 2.2 us -> none
    unnamed x25 -> x21, local copies, waits for them, and re-layouts: 4.15 us -> 2.8 us
  transfers between devices with their start and end apart: 13 -> 11, of which waited for: 6 -> 3; matrix products, arithmetic and copies ran while one was open for 4% -> 3% of each run, Pallas kernels for 25% -> 22%
where the time goes in v2:
time: 182 us; the launch traced here: 181 us
  Pallas kernels  75.8 us (42%)
  blocking collectives  64.3 us (35%)
  starting transfers between devices  20.4 us (11%)
  waiting for transfers between devices  8.69 us (5%)
  local copies, waits for them, and re-layouts  5.99 us (3%)
  other arithmetic  5.05 us (3%)
    all_to_all x2, blocking collectives, in_half(): lax.all_to_all(array, ('tok', 'head'), split_axis=0, concat_axis=0, tiled...  52.1 us
    pallas_call x2, Pallas kernels, expert(): pl.pallas_call(functools.partial(expert_kernel, extras, in_tiles, down),...  38 us
    all_to_all x1, blocking collectives, exchanged_pages(): return lax.all_to_all(sent, 'tok', split_axis=0, concat_axis=0, tiled=True)  12.2 us
    pallas_call x2, Pallas kernels, project(): pl.pallas_call(functools.partial(qkv_kernel, step, chips), grid_spec=pltp...  11.9 us
    pallas_call x1, Pallas kernels, expert_down(): pl.pallas_call(functools.partial(down_kernel, extras, width), grid=(PIECE...  9.5 us
    all_to_all x2, starting transfers between devices, in_half(): lax.all_to_all(array, ('tok', 'head'), split_axis=0, concat_axis=0, tiled...  9.33 us
    pallas_call x1, Pallas kernels, attend(): pl.pallas_call(functools.partial(attend_kernel, row_count, chips), grid_s...  9.05 us
    all_to_all x2, waiting for transfers between devices, in_half(): lax.all_to_all(array, ('tok', 'head'), split_axis=0, concat_axis=0, tiled...  5.66 us
  transfers between devices with their start and end apart: 11, of which 3 were waited for; matrix products, arithmetic and copies ran while one was open for 3% of the time, Pallas kernels for 22%

profile of v2, /device:TPU:0, one launch (start us, length us, event | category | flops | bytes accessed | tf_op | source)
XLA Modules:
  0.0 181.2 jit_solution(1741095496695639698)
XLA Ops:
  0.6 0.5 collective-permute-start.1
  1.1 2.6 %collective-permute-start = (bf16[64,2880]{1,0:T(8,128)(2,1)}, bf16[64,2880]{1,0:T(8,128)(2,1)S(1)}, u32[]{:S(2)}, u32[]{:S(2)}) collective-permute-start(bf16[64,2880]{1,0:T(8,128)(2,1)} %tokens_ref.1), channel_id=1, source_target_pairs={{0,2},{1,3},{2,0},{3,1},{4,6},{5,7},{6,4},{7,5},{8,10},{9,11},{10,... | collective-permute-start | bytes 1105928 | tf_op jit(solution)/shard_map/ppermute | solution.py:651
  3.7 0.7 convert_bitcast_fusion
  4.4 0.7 pad_maximum_fusion.choice_ref
  5.1 2.6 %collective-permute-start.3 = (f32[8,64]{1,0:T(8,128)S(1)}, f32[8,64]{1,0:T(8,128)S(1)}, u32[]{:S(2)}, u32[]{:S(2)}) collective-permute-start(f32[8,64]{1,0:T(8,128)S(1)} %pad_maximum_fusion.choice_ref), channel_id=1, source_target_pairs={{0,16},{1,17},{2,18},{3,19},{4,20},{5,21},{6,22},{7,23},{8,24},{9,... | collective-permute-start | bytes 6152 | tf_op jit(solution)/shard_map/ppermute | solution.py:659
  7.7 0.7 pad_add_fusion.ids_ref
  8.4 0.7 reshape.248
  9.2 0.7 copy-done.7
  9.9 6.0 %project.2 = (bf16[256,1024]{1,0:T(8,128)(2,1)}, bf16[256,256]{1,0:T(8,128)(2,1)}) custom-call(s32[4]{0:T(128)} %pad_add_fusion.ids_ref, s32[4]{0:T(128)} %lengths_ref.9, bf16[64,2880]{1,0:T(8,128)(2,1)} %tokens_ref.1, bf16[64,2880]{1,0:T(8,128)(2,1)} %copy-done.7, f32[2880]{0:T(1024)} %gain_ref.4, bf16[2880,1280]{1,0:T(8,128)(2,1)} %w_ref.3), custom_call_target="tpu_custom_call" | custom-call | flops 943718400 | bytes 7372800 | tf_op jit(solution)/shard_map/project/pallas_call | solution.py:113
  16.0 0.3 convert_reduce_fusion
  16.3 1.3 collective-permute-done.2.other_ref
  17.6 0.7 copy-done.8
  18.4 6.0 %project.3 = (bf16[256,1024]{1,0:T(8,128)(2,1)}, bf16[256,256]{1,0:T(8,128)(2,1)}) custom-call(s32[4]{0:T(128)} %pad_add_fusion.ids_ref, s32[4]{0:T(128)} %lengths_ref.9, bf16[64,2880]{1,0:T(8,128)(2,1)} %copy-done.6, bf16[64,2880]{1,0:T(8,128)(2,1)} %copy-done.8, f32[2880]{0:T(1024)} %gain_ref.4, ...), custom_call_target="tpu_custom_call", output_to_operand_aliasing={{0}: (6, {}), {1}: (7, {})} | custom-call | flops 943718400 | bytes 7372800 | tf_op jit(solution)/shard_map/project/pallas_call | solution.py:113
  24.4 0.9 slice.8
  25.3 3.4 %collective-permute-start.4 = (bf16[128,256]{1,0:T(8,128)(2,1)S(1)}, bf16[128,256]{1,0:T(8,128)(2,1)S(1)}, u32[]{:S(2)}, u32[]{:S(2)}) collective-permute-start(bf16[128,256]{1,0:T(8,128)(2,1)S(1)} %slice.8), channel_id=1, source_target_pairs={{0,4},{4,8},{8,12},{12,16},{16,20},{20,24},{24,28},{1,5},{5,9},{9,... | collective-permute-start | bytes 196616 | tf_op jit(solution)/shard_map/ppermute | solution.py:36
  28.7 1.0 slots.2
  29.7 1.0 slots.3
  30.8 0.6 copy-done.9
  31.4 9.0 %attend.1 = (f32[2,64,2880]{2,1,0:T(8,128)}, bf16[2,64,2880]{2,1,0:T(8,128)(2,1)}) custom-call(s32[4]{0:T(128)} %pad_add_fusion.ids_ref, s32[4]{0:T(128)} %lengths_ref.9, bf16[256,1024]{1,0:T(8,128)(2,1)} %get-tuple-element.55.q_ref, bf16[128,256]{1,0:T(8,128)(2,1)} %copy-done.9, bf16[256,256]{1,0:T(8,128)(2,1)} %get-tuple-element.67.pair_ref, f32[16]{0:T(128)} %sink_ref.1, ...), custom_call_target="tpu_custom_call" | custom-call | flops 1509949440 | bytes 5898240 | tf_op jit(solution)/shard_map/attend/pallas_call | solution.py:552
  40.5 0.1 select_reduce_fusion.2
  40.6 0.1 copy.20
  40.8 0.1 select_reduce_fusion.1
  41.0 0.1 copy.21
  41.1 0.1 select_reduce_fusion
  41.3 1.7 collective-permute-done.5
  42.9 2.2 %fusion = (bf16[64,2880]{1,0:T(8,128)(2,1)}, f32[64,2880]{1,0:T(8,128)S(1)}) fusion(f32[2,64,2880]{2,1,0:T(8,128)} %get-tuple-element.64, s32[]{:T(128)S(6)} %select_n.92, bf16[2,64,2880]{2,1,0:T(8,128)(2,1)S(1)} %collective-permute-done.5, s32[]{:T(128)S(6)} %select_n.90), kind=kLoop, calls=%fused_computation.4 | loop fusion | flops 921600 | bytes 3317768 | tf_op jit(solution)/shard_map/convert_element_type | solution.py:713
  45.2 0.5 collective-permute-start.6
  45.8 0.6 gather_fusion
  46.4 12.2 %all_to_all.25 = bf16[8,64,128]{2,1,0:T(8,128)(2,1)S(1)} all-to-all(bf16[8,64,128]{2,1,0:T(8,128)(2,1)S(1)} %bitcast.50), channel_id=1, replica_groups=mesh['tok'=8,'head'=4] {'tok'}, dimensions={0} | all-to-all | bytes 262144 | tf_op jit(solution)/shard_map/all_to_all | solution.py:605
  58.6 0.3 finish_attention.1
  58.9 0.5 collective-permute-start.7
  59.4 1.5 pack.2
  60.9 25.7 %conditional.2 = (bf16[128,3712]{1,0:T(8,128)(2,1)S(1)}) conditional(s32[]{:T(128)} %bitcast.4, () %tuple.36, bf16[128,3712]{1,0:T(8,128)(2,1)} %pack.2), branch_computations={%region_2.3_spmd, %region_3.4_spmd} | conditional | bytes 1900552 | solution.py:730
  60.9 25.7 %all_to_all.23 = bf16[16,8,3712]{2,1,0:T(8,128)(2,1)S(1)} all-to-all(bf16[16,8,3712]{2,1,0:T(8,128)(2,1)} %bitcast.46), channel_id=1, replica_groups={{0,1,2,3,4,5,6,7,8,9,10,11,12,13,14,15},{16,17,18,19,20,21,22,23,24,25,..., dimensions={0} | all-to-all | bytes 1900544 | tf_op jit(solution)/shard_map/cond/branch_1_fun/all_to_all | solution.py:662
  86.5 1.5 pack.3
  88.0 4.5 %all-to-all-start.3 = ((bf16[16,8,3712]{2,1,0:T(8,128)(2,1)}), bf16[16,8,3712]{2,1,0:T(8,128)(2,1)}, u32[]{:S(2)}, u32[]{:S(2)}) async-start(bf16[16,8,3712]{2,1,0:T(8,128)(2,1)} %bitcast.20), calls=%async_computation.3 | async-start | bytes 1900544 | tf_op jit(solution)/shard_map/all_to_all | solution.py:662
  92.5 15.0 %expert_up.1.act_ref = bf16[160,2880]{1,0:T(8,128)(2,1)} custom-call(bf16[128,3712]{1,0:T(8,128)(2,1)S(1)} %get-tuple-element.98.refs_0_, bf16[1,2880,5760]{2,1,0:T(8,128)(2,1)} %refs_1_.3), custom_call_target="tpu_custom_call" | custom-call | flops 5308416000 | bytes 33177600 | tf_op jit(solution)/shard_map/expert_up/pallas_call | solution.py:336
  107.6 22.9 %expert.1 = bf16[128,3712]{1,0:T(8,128)(2,1)} custom-call(bf16[128,3712]{1,0:T(8,128)(2,1)} %bitcast.21.refs_0_, bf16[1,2880,5760]{2,1,0:T(8,128)(2,1)} %refs_1_.3, bf16[1,2880,2880]{2,1,0:T(8,128)(2,1)} %w_down_ref.1), custom_call_target="tpu_custom_call" | custom-call | flops 7962624000 | bytes 49766400 | tf_op jit(solution)/shard_map/expert/pallas_call | solution.py:336
  130.5 4.8 %all-to-all-start.4 = ((bf16[16,8,3712]{2,1,0:T(8,128)(2,1)}), bf16[16,8,3712]{2,1,0:T(8,128)(2,1)S(1)}, u32[]{:S(2)}, u32[]{:S(2)}) async-start(bf16[16,8,3712]{2,1,0:T(8,128)(2,1)} %bitcast.44), calls=%async_computation.4 | async-start | bytes 1900544 | tf_op jit(solution)/shard_map/all_to_all | solution.py:662
  135.3 9.5 %expert_down.1 = bf16[128,3712]{1,0:T(8,128)(2,1)} custom-call(bf16[160,2880]{1,0:T(8,128)(2,1)} %expert_up.1.act_ref, bf16[1,2880,2880]{2,1,0:T(8,128)(2,1)} %w_down_ref.1), custom_call_target="tpu_custom_call" | custom-call | flops 2654208000 | bytes 16588800 | tf_op jit(solution)/shard_map/expert_down/pallas_call | solution.py:357
  144.8 5.7 %all-to-all-done.4 = bf16[16,8,3712]{2,1,0:T(8,128)(2,1)S(1)} async-done(((bf16[16,8,3712]{2,1,0:T(8,128)(2,1)}), bf16[16,8,3712]{2,1,0:T(8,128)(2,1)S(1)}, u32[]{:S(2)}, u32[]{:S(2)}) %all-to-all-start.4) | async-done | bytes 950304 | tf_op jit(solution)/shard_map/all_to_all | solution.py:662
  150.5 0.6 combine.2
  151.1 1.0 collective-permute-start.8
  152.1 0.6 gather_fusion.1
  152.7 0.7 copy.22
  153.4 26.5 %conditional.3 = (bf16[128,3712]{1,0:T(8,128)(2,1)S(1)}) conditional(s32[]{:T(128)} %bitcast.4, () %tuple.30, bf16[128,3712]{1,0:T(8,128)(2,1)} %expert_down.1), branch_computations={%region_4.5_spmd, %region_5.6_spmd} | conditional | bytes 1900552 | solution.py:730
  153.4 26.5 %all_to_all.24 = bf16[16,8,3712]{2,1,0:T(8,128)(2,1)S(1)} all-to-all(bf16[16,8,3712]{2,1,0:T(8,128)(2,1)} %bitcast.47), channel_id=1, replica_groups={{0,1,2,3,4,5,6,7,8,9,10,11,12,13,14,15},{16,17,18,19,20,21,22,23,24,25,..., dimensions={0} | all-to-all | bytes 1900544 | tf_op jit(solution)/shard_map/cond/branch_1_fun/all_to_all | solution.py:662
  179.8 1.4 combine.3
  (41 shorter events, 0.4 us)
Async XLA Ops:
  0.6 8.5 %collective-permute-start.1 = (bf16[64,2880]{1,0:T(8,128)(2,1)}, bf16[64,2880]{1,0:T(8,128)(2,1)S(1)}, u32[]{:S(2)}, u32[]{:S(2)}) collective-permute-start(bf16[64,2880]{1,0:T(8,128)(2,1)} %tokens_ref.1), channel_id=1, source_target_pairs={{0,1},{1,0},{2,3},{3,2},{4,5},{5,4},{6,7},{7,6},{8,9},{9,8},{10,11... | collective-permute-start | bytes 1105928 | tf_op jit(solution)/shard_map/ppermute | solution.py:648
  1.1 14.7 %collective-permute-start = (bf16[64,2880]{1,0:T(8,128)(2,1)}, bf16[64,2880]{1,0:T(8,128)(2,1)S(1)}, u32[]{:S(2)}, u32[]{:S(2)}) collective-permute-start(bf16[64,2880]{1,0:T(8,128)(2,1)} %tokens_ref.1), channel_id=1, source_target_pairs={{0,2},{1,3},{2,0},{3,1},{4,6},{5,7},{6,4},{7,5},{8,10},{9,11},{10,... | collective-permute-start | bytes 1105928 | tf_op jit(solution)/shard_map/ppermute | solution.py:651
  5.1 19.3 %collective-permute-start.3 = (f32[8,64]{1,0:T(8,128)S(1)}, f32[8,64]{1,0:T(8,128)S(1)}, u32[]{:S(2)}, u32[]{:S(2)}) collective-permute-start(f32[8,64]{1,0:T(8,128)S(1)} %pad_maximum_fusion.choice_ref), channel_id=1, source_target_pairs={{0,16},{1,17},{2,18},{3,19},{4,20},{5,21},{6,22},{7,23},{8,24},{9,... | collective-permute-start | bytes 6152 | tf_op jit(solution)/shard_map/ppermute | solution.py:659
  9.1 19.5 %copy-start.1 = (s32[4]{0:T(128)S(1)}, s32[4]{0:T(128)}, u32[]{:S(2)}) copy-start(s32[4]{0:T(128)} %pad_add_fusion.ids_ref) | copy-start | bytes 52
  9.1 19.5 %copy-start.2 = (s32[4]{0:T(128)S(1)}, s32[4]{0:T(128)}, u32[]{:S(2)}) copy-start(s32[4]{0:T(128)} %lengths_ref.9) | copy-start | bytes 52
  9.2 0.7 copy-start.7
  15.9 1.8 copy-start.6
  15.9 1.8 collective-permute-start.2
  17.6 0.7 copy-start.8
  24.3 21.4 %copy-start.5 = (bf16[256,256]{1,0:T(8,128)(2,1)S(1)}, bf16[256,256]{1,0:T(8,128)(2,1)}, u32[]{:S(2)}) copy-start(bf16[256,256]{1,0:T(8,128)(2,1)} %get-tuple-element.67.pair_ref) | copy-start | bytes 393220
  24.3 34.2 %copy-start = (bf16[64,2880]{1,0:T(8,128)(2,1)S(1)}, bf16[64,2880]{1,0:T(8,128)(2,1)}, u32[]{:S(2)}) copy-start(bf16[64,2880]{1,0:T(8,128)(2,1)} %tokens_ref.1) | copy-start | bytes 1105924
  24.3 34.2 %copy-start.4 = (f32[2880]{0:T(1024)S(1)}, f32[2880]{0:T(1024)}, u32[]{:S(2)}) copy-start(f32[2880]{0:T(1024)} %gain_ref.5) | copy-start | bytes 34564
  24.4 35.0 %copy-start.3 = (s32[4]{0:T(128)S(1)}, s32[4]{0:T(128)}, u32[]{:S(2)}) copy-start(s32[4]{0:T(128)} %lengths_ref.9) | copy-start | bytes 52
  25.3 5.5 %collective-permute-start.4 = (bf16[128,256]{1,0:T(8,128)(2,1)S(1)}, bf16[128,256]{1,0:T(8,128)(2,1)S(1)}, u32[]{:S(2)}, u32[]{:S(2)}) collective-permute-start(bf16[128,256]{1,0:T(8,128)(2,1)S(1)} %slice.8), channel_id=1, source_target_pairs={{0,4},{4,8},{8,12},{12,16},{16,20},{20,24},{24,28},{1,5},{5,9},{9,... | collective-permute-start | bytes 196616 | tf_op jit(solution)/shard_map/ppermute | solution.py:36
  30.8 0.6 copy-start.9
  40.5 2.4 %collective-permute-start.5 = (bf16[2,64,2880]{2,1,0:T(8,128)(2,1)}, bf16[2,64,2880]{2,1,0:T(8,128)(2,1)S(1)}, u32[]{:S(2)}, u32[]{:S(2)}) collective-permute-start(bf16[2,64,2880]{2,1,0:T(8,128)(2,1)} %get-tuple-element.65), channel_id=1, source_target_pairs={{0,1},{1,0},{2,3},{3,2},{4,5},{5,4},{6,7},{7,6},{8,9},{9,8},{10,11... | collective-permute-start | bytes 2211848 | tf_op jit(solution)/shard_map/ppermute | solution.py:648
  45.2 13.4 %collective-permute-start.6 = (bf16[64,2880]{1,0:T(8,128)(2,1)}, bf16[64,2880]{1,0:T(8,128)(2,1)S(1)}, u32[]{:S(2)}, u32[]{:S(2)}) collective-permute-start(bf16[64,2880]{1,0:T(8,128)(2,1)} %get-tuple-element.66), channel_id=1, source_target_pairs={{0,2},{1,3},{2,0},{3,1},{4,6},{5,7},{6,4},{7,5},{8,10},{9,11},{10,... | collective-permute-start | bytes 1105928 | tf_op jit(solution)/shard_map/ppermute | solution.py:651
  58.9 27.6 %collective-permute-start.7 = (bf16[64,2880]{1,0:T(8,128)(2,1)S(1)}, bf16[64,2880]{1,0:T(8,128)(2,1)S(1)}, u32[]{:S(2)}, u32[]{:S(2)}) collective-permute-start(bf16[64,2880]{1,0:T(8,128)(2,1)S(1)} %get-tuple-element.69.moe_ref), channel_id=1, source_target_pairs={{0,16},{1,17},{2,18},{3,19},{4,20},{5,21},{6,22},{7,23},{8,24},{9,... | collective-permute-start | bytes 1105928 | tf_op jit(solution)/shard_map/ppermute | solution.py:659
  88.0 19.5 %all-to-all-start.3 = ((bf16[16,8,3712]{2,1,0:T(8,128)(2,1)}), bf16[16,8,3712]{2,1,0:T(8,128)(2,1)}, u32[]{:S(2)}, u32[]{:S(2)}) async-start(bf16[16,8,3712]{2,1,0:T(8,128)(2,1)} %bitcast.20), calls=%async_computation.3 | async-start | bytes 1900544 | tf_op jit(solution)/shard_map/all_to_all | solution.py:662
  130.5 20.0 %all-to-all-start.4 = ((bf16[16,8,3712]{2,1,0:T(8,128)(2,1)}), bf16[16,8,3712]{2,1,0:T(8,128)(2,1)S(1)}, u32[]{:S(2)}, u32[]{:S(2)}) async-start(bf16[16,8,3712]{2,1,0:T(8,128)(2,1)} %bitcast.44), calls=%async_computation.4 | async-start | bytes 1900544 | tf_op jit(solution)/shard_map/all_to_all | solution.py:662
  151.1 28.7 %collective-permute-start.8 = (bf16[64,2880]{1,0:T(8,128)(2,1)S(1)}, bf16[64,2880]{1,0:T(8,128)(2,1)S(1)}, u32[]{:S(2)}, u32[]{:S(2)}) collective-permute-start(bf16[64,2880]{1,0:T(8,128)(2,1)S(1)} %combine.2), channel_id=1, source_target_pairs={{0,16},{1,17},{2,18},{3,19},{4,20},{5,21},{6,22},{7,23},{8,24},{9,... | collective-permute-start | bytes 1105928 | tf_op jit(solution)/shard_map/ppermute | solution.py:659

commit v3 on v2

--- a/solution.py
+++ b/solution.py
@@ -26,7 +26,9 @@
 PIECE = 768
 PIECES = 4
 EXTRA_AT = 2944
-IN_TILE = 1152
+IN_TILE = 1920
+FIRST_COPY = 1
+DOWN_COPIES = 4
 MIB = 1 << 20
 
 
@@ -243,12 +245,18 @@
         ).astype(jnp.bfloat16)
 
 
-def put_piece(piece, act_ref, w_down_ref, out_ref, width, piece_ref):
+def put_piece(piece, made, out_ref, width, piece_ref):
     slots = out_ref.shape[0]
-    made = jnp.dot(act_ref[...], w_down_ref[0], preferred_element_type=jnp.float32)
-    column = lax.broadcasted_iota(jnp.int32, made.shape, 1) + piece * PIECE
-    made = jnp.where(column < width, made, 0.0).astype(jnp.bfloat16)
-    out_ref[:, pl.ds(pl.multiple_of(piece * PIECE, LANES), PIECE)] = made[:slots]
+    extent = made.shape[1]
+    if extent < PIECE:
+        out_ref[:, piece * PIECE + extent : (piece + 1) * PIECE] = jnp.zeros(
+            (slots, PIECE - extent), jnp.bfloat16
+        )
+        out_ref[:, piece * PIECE : piece * PIECE + extent] = made[:slots]
+    else:
+        start = piece * PIECE
+        start = start if isinstance(piece, int) else pl.multiple_of(start, LANES)
+        out_ref[:, pl.ds(start, extent)] = made[:slots]
     if piece_ref is not None:
         further = slots // PIECES
         t = lax.broadcasted_iota(jnp.int32, (slots, further), 1)
@@ -257,6 +265,14 @@
         part = jnp.dot(spread, made[slots:], preferred_element_type=jnp.float32).astype(
             jnp.bfloat16
         )
+        if isinstance(piece, int):
+            if piece == 0:
+                piece_ref[...] = part
+            else:
+                piece_ref[:, :extent] = piece_ref[:, :extent] + part
+            if piece == PIECES - 1:
+                out_ref[:, EXTRA_AT:] = piece_ref[...]
+            return
 
         @pl.when(piece == 0)
         def _():
@@ -277,34 +293,57 @@
     x_ref, gate_up_ref = scratch[:2]
     act_ref = scratch[2] if down else refs[2]
     step = pl.program_id(0)
+    copies = []
+    if down:
+        w_down_ref, out_ref = refs[2:4]
+        held_ref, total_ref, sems = scratch[3:6]
+        piece_ref = scratch[6] if extras else None
+        ffs = held_ref.shape[0]
+        rows = pl.cdiv(ffs, DOWN_COPIES * LANES) * LANES
+        for c in range(pl.cdiv(ffs, rows)):
+            part = pl.ds(c * rows, min(rows, ffs - c * rows))
+            copies.append(
+                pltpu.make_async_copy(w_down_ref.at[0, part], held_ref.at[part], sems.at[c])
+            )
 
     @pl.when(step == 0)
     def _():
         fill_rows(packed_ref, x_ref, extras)
 
-    @pl.when(step < in_tiles)
-    def _():
-        gate_up_ref[:, pl.ds(pl.multiple_of(step * IN_TILE, LANES), IN_TILE)] = jnp.dot(
-            x_ref[...], w_in_ref[0], preferred_element_type=jnp.float32
-        )
-
-    @pl.when(step == (in_tiles if down else in_tiles - 1))
+    for c, copy in enumerate(copies):
+        pl.when(step == min(c + FIRST_COPY, in_tiles - 1))(copy.start)
+
+    tile = w_in_ref.shape[2]
+    made = jnp.dot(x_ref[...], w_in_ref[0], preferred_element_type=jnp.float32)
+    if in_tiles == 1:
+        gate_up_ref[...] = made
+    else:
+        gate_up_ref[:, pl.ds(pl.multiple_of(step * tile, LANES), tile)] = made
+
+    @pl.when(step == in_tiles - 1)
     def _():
         activate(gate_up_ref, act_ref)
-
-    if down:
-        w_down_ref, out_ref = refs[2:4]
-
-        @pl.when(step >= in_tiles)
-        def _():
-            piece_ref = scratch[3] if extras else None
-            put_piece(step - in_tiles, act_ref, w_down_ref, out_ref, x_ref.shape[1], piece_ref)
+        if down:
+            width = x_ref.shape[1]
+            for c, copy in enumerate(copies):
+                copy.wait()
+                part = slice(c * rows, min((c + 1) * rows, ffs))
+                term = jnp.dot(
+                    act_ref[:, part], held_ref[part, :], preferred_element_type=jnp.float32
+                )
+                total_ref[...] = term if c == 0 else total_ref[...] + term
+            for piece in range(PIECES):
+                extent = min(PIECE, width - piece * PIECE)
+                made = total_ref[:, piece * PIECE : piece * PIECE + extent].astype(jnp.bfloat16)
+                put_piece(piece, made, out_ref, width, piece_ref)
 
 
 def down_kernel(extras, width, act_ref, w_down_ref, out_ref, *scratch):
-    put_piece(
-        pl.program_id(0), act_ref, w_down_ref, out_ref, width, scratch[0] if extras else None
-    )
+    piece = pl.program_id(0)
+    made = jnp.dot(act_ref[...], w_down_ref[0], preferred_element_type=jnp.float32)
+    column = lax.broadcasted_iota(jnp.int32, made.shape, 1) + piece * PIECE
+    made = jnp.where(column < width, made, 0.0).astype(jnp.bfloat16)
+    put_piece(piece, made, out_ref, width, scratch[0] if extras else None)
 
 
 def expert(packed, w_in, w_down, extras, down=True):
@@ -312,30 +351,34 @@
     width = w_in.shape[1]
     ffs = w_down.shape[1]
     rows = slots + (slots // PIECES if extras else 0)
-    in_tiles = pl.cdiv(2 * ffs, IN_TILE)
+    tile = min(IN_TILE, 2 * ffs)
+    in_tiles = pl.cdiv(2 * ffs, tile)
     whole = lambda i: (0, 0)
     in_specs = [
         pl.BlockSpec((slots, held), whole),
-        pl.BlockSpec((1, width, IN_TILE), lambda i: (0, 0, jnp.minimum(i, in_tiles - 1))),
+        pl.BlockSpec((1, width, tile), lambda i: (0, 0, i)),
     ]
     scratch = [
         pltpu.VMEM((rows, width), jnp.bfloat16),
-        pltpu.VMEM((rows, in_tiles * IN_TILE), jnp.float32),
+        pltpu.VMEM((rows, in_tiles * tile), jnp.float32),
     ]
     args = (packed, w_in)
     out = (rows, ffs)
     if down:
-        in_specs += [
-            pl.BlockSpec((1, ffs, PIECE), lambda i: (0, 0, jnp.maximum(i - in_tiles, 0)))
+        in_specs += [pl.BlockSpec(memory_space=pl.ANY)]
+        scratch += [
+            pltpu.VMEM((rows, ffs), jnp.bfloat16),
+            pltpu.VMEM((ffs, width), jnp.bfloat16),
+            pltpu.VMEM((rows, width), jnp.float32),
+            pltpu.SemaphoreType.DMA((DOWN_COPIES,)),
         ]
-        scratch += [pltpu.VMEM((rows, ffs), jnp.bfloat16)]
         scratch += [pltpu.VMEM((slots, PIECE), jnp.bfloat16)] if extras else []
         args += (w_down,)
         out = (slots, held)
     parts = 6 if down else 4
     return pl.pallas_call(
         functools.partial(expert_kernel, extras, in_tiles, down),
-        grid=(in_tiles + (PIECES if down else 0),),
+        grid=(in_tiles,),
         in_specs=in_specs,
         out_specs=pl.BlockSpec(out, whole),
         out_shape=jax.ShapeDtypeStruct(out, jnp.bfloat16),
@@ -671,7 +714,6 @@
     flat_id = tok_id * n_head + head_id
     ids = jnp.stack([core, y_id, tok_id, flat_id]).astype(jnp.int32)
     choice = jnp.concatenate([routes.T.astype(jnp.float32), gates.T], axis=0)
-    far_choice = across(choice)
 
     capacity = row_count // 8 + 2
     shards = n_dev // EXPERTS
@@ -681,7 +723,7 @@
     placed, block = [], tokens
     for k in range(n_y):
         if k:
-            block, placed = lax.optimization_barrier((along_y(tokens, k), placed))
+            block, placed, choice = lax.optimization_barrier((along_y(tokens, k), placed, choice))
         placed = project(
             ids,
             lengths,
@@ -693,6 +735,7 @@
             query_key_value_weight,
             placed,
         )
+    far_choice = across(choice)
     placed, choice, far_choice = lax.optimization_barrier((placed, choice, far_choice))
     query_rows, key_value_pairs = placed
     rim_rows = passed_along(key_value_pairs[tok_dev - ATTEND_WINDOW :], "tok", 1)

time: 182 us -> 178 us (0.978)
  Pallas kernels: 75.8 us -> 71.4 us
    pallas_call x2, Pallas kernels: 38 us -> 33.7 us  [expert(): pl.pallas_call(functools.partial(expert_kernel, extras, in_tiles, down),...]
where the time goes in v3:
time: 178 us; the launch traced here: 177 us
  Pallas kernels  71.4 us (40%)
  blocking collectives  64.4 us (36%)
  starting transfers between devices  21.5 us (12%)
  waiting for transfers between devices  7.62 us (4%)
  local copies, waits for them, and re-layouts  5.98 us (3%)
  other arithmetic  5 us (3%)
    all_to_all x2, blocking collectives, in_half(): lax.all_to_all(array, ('tok', 'head'), split_axis=0, concat_axis=0, tiled...  52.1 us
    pallas_call x2, Pallas kernels, expert(): pl.pallas_call(functools.partial(expert_kernel, extras, in_tiles, down),...  33.7 us
    all_to_all x1, blocking collectives, exchanged_pages(): return lax.all_to_all(sent, 'tok', split_axis=0, concat_axis=0, tiled=True)  12.3 us
    pallas_call x2, Pallas kernels, project(): pl.pallas_call(functools.partial(qkv_kernel, step, chips), grid_spec=pltp...  11.9 us
    pallas_call x1, Pallas kernels, expert_down(): pl.pallas_call(functools.partial(down_kernel, extras, width), grid=(PIECE...  9.5 us
    all_to_all x2, starting transfers between devices, in_half(): lax.all_to_all(array, ('tok', 'head'), split_axis=0, concat_axis=0, tiled...  9.09 us
    pallas_call x1, Pallas kernels, attend(): pl.pallas_call(functools.partial(attend_kernel, row_count, chips), grid_s...  9.05 us
    all_to_all x2, waiting for transfers between devices, in_half(): lax.all_to_all(array, ('tok', 'head'), split_axis=0, concat_axis=0, tiled...  5.92 us
  transfers between devices with their start and end apart: 11, of which 3 were waited for; matrix products, arithmetic and copies ran while one was open for 3% of the time, Pallas kernels for 22%

profile of v3, /device:TPU:0, one launch (start us, length us, event | category | flops | bytes accessed | tf_op | source)
XLA Modules:
  0.0 176.9 jit_solution(403891106624157734)
XLA Ops:
  0.6 0.5 collective-permute-start.1
  1.1 2.6 %collective-permute-start = (bf16[64,2880]{1,0:T(8,128)(2,1)}, bf16[64,2880]{1,0:T(8,128)(2,1)S(1)}, u32[]{:S(2)}, u32[]{:S(2)}) collective-permute-start(bf16[64,2880]{1,0:T(8,128)(2,1)} %tokens_ref.1), channel_id=1, source_target_pairs={{0,2},{1,3},{2,0},{3,1},{4,6},{5,7},{6,4},{7,5},{8,10},{9,11},{10,... | collective-permute-start | bytes 1105928 | tf_op jit(solution)/shard_map/ppermute | solution.py:694
  3.7 0.7 convert_bitcast_fusion
  4.4 0.7 pad_maximum_fusion.choice_ref
  5.1 0.7 pad_add_fusion.ids_ref
  5.8 0.7 reshape.248
  6.6 0.7 copy-done.7
  7.3 6.0 %project.2 = (bf16[256,1024]{1,0:T(8,128)(2,1)}, bf16[256,256]{1,0:T(8,128)(2,1)}) custom-call(s32[4]{0:T(128)} %pad_add_fusion.ids_ref, s32[4]{0:T(128)} %lengths_ref.9, bf16[64,2880]{1,0:T(8,128)(2,1)} %tokens_ref.1, bf16[64,2880]{1,0:T(8,128)(2,1)} %copy-done.7, f32[2880]{0:T(1024)} %gain_ref.4, bf16[2880,1280]{1,0:T(8,128)(2,1)} %w_ref.3), custom_call_target="tpu_custom_call" | custom-call | flops 943718400 | bytes 7372800 | tf_op jit(solution)/shard_map/project/pallas_call | solution.py:115
  13.3 0.2 collective-permute-start.2
  13.5 0.3 convert_reduce_fusion
  13.8 2.7 %collective-permute-start.3 = (f32[8,64]{1,0:T(8,128)S(1)}, f32[8,64]{1,0:T(8,128)S(1)}, u32[]{:S(2)}, u32[]{:S(2)}) collective-permute-start(f32[8,64]{1,0:T(8,128)S(1)} %pad_maximum_fusion.choice_ref), channel_id=1, source_target_pairs={{0,16},{1,17},{2,18},{3,19},{4,20},{5,21},{6,22},{7,23},{8,24},{9,... | collective-permute-start | bytes 6152 | tf_op jit(solution)/shard_map/ppermute | solution.py:702
  16.5 0.7 copy-done.8
  17.3 6.0 %project.3 = (bf16[256,1024]{1,0:T(8,128)(2,1)}, bf16[256,256]{1,0:T(8,128)(2,1)}) custom-call(s32[4]{0:T(128)} %pad_add_fusion.ids_ref, s32[4]{0:T(128)} %lengths_ref.9, bf16[64,2880]{1,0:T(8,128)(2,1)} %copy-done.6, bf16[64,2880]{1,0:T(8,128)(2,1)} %copy-done.8, f32[2880]{0:T(1024)} %gain_ref.4, ...), custom_call_target="tpu_custom_call", output_to_operand_aliasing={{0}: (6, {}), {1}: (7, {})} | custom-call | flops 943718400 | bytes 7372800 | tf_op jit(solution)/shard_map/project/pallas_call | solution.py:115
  23.3 0.9 slice.8
  24.2 3.4 %collective-permute-start.4 = (bf16[128,256]{1,0:T(8,128)(2,1)S(1)}, bf16[128,256]{1,0:T(8,128)(2,1)S(1)}, u32[]{:S(2)}, u32[]{:S(2)}) collective-permute-start(bf16[128,256]{1,0:T(8,128)(2,1)S(1)} %slice.8), channel_id=1, source_target_pairs={{0,4},{4,8},{8,12},{12,16},{16,20},{20,24},{24,28},{1,5},{5,9},{9,... | collective-permute-start | bytes 196616 | tf_op jit(solution)/shard_map/ppermute | solution.py:38
  27.6 1.0 slots.2
  28.6 1.0 slots.3
  29.7 0.6 copy-done.9
  30.3 9.1 %attend.1 = (f32[2,64,2880]{2,1,0:T(8,128)}, bf16[2,64,2880]{2,1,0:T(8,128)(2,1)}) custom-call(s32[4]{0:T(128)} %pad_add_fusion.ids_ref, s32[4]{0:T(128)} %lengths_ref.9, bf16[256,1024]{1,0:T(8,128)(2,1)} %get-tuple-element.57.q_ref, bf16[128,256]{1,0:T(8,128)(2,1)} %copy-done.9, bf16[256,256]{1,0:T(8,128)(2,1)} %get-tuple-element.69.pair_ref, f32[16]{0:T(128)} %sink_ref.1, ...), custom_call_target="tpu_custom_call" | custom-call | flops 1509949440 | bytes 5898240 | tf_op jit(solution)/shard_map/attend/pallas_call | solution.py:595
  39.4 0.1 select_reduce_fusion.2
  39.5 0.1 copy.20
  39.7 0.1 select_reduce_fusion.1
  40.0 0.1 select_reduce_fusion
  40.2 1.7 collective-permute-done.5
  41.8 2.2 %fusion = (bf16[64,2880]{1,0:T(8,128)(2,1)}, f32[64,2880]{1,0:T(8,128)S(1)}) fusion(f32[2,64,2880]{2,1,0:T(8,128)} %get-tuple-element.66, s32[]{:T(128)S(6)} %select_n.92, bf16[2,64,2880]{2,1,0:T(8,128)(2,1)S(1)} %collective-permute-done.5, s32[]{:T(128)S(6)} %select_n.90), kind=kLoop, calls=%fused_computation.4 | loop fusion | flops 921600 | bytes 3317768 | tf_op jit(solution)/shard_map/convert_element_type | solution.py:756
  44.0 1.5 collective-permute-start.6
  45.7 0.6 gather_fusion
  46.2 12.3 %all_to_all.25 = bf16[8,64,128]{2,1,0:T(8,128)(2,1)S(1)} all-to-all(bf16[8,64,128]{2,1,0:T(8,128)(2,1)S(1)} %bitcast.50), channel_id=1, replica_groups=mesh['tok'=8,'head'=4] {'tok'}, dimensions={0} | all-to-all | bytes 262144 | tf_op jit(solution)/shard_map/all_to_all | solution.py:648
  58.5 0.3 finish_attention.1
  58.8 0.5 collective-permute-start.7
  59.3 1.5 pack.2
  60.8 25.7 %conditional.2 = (bf16[128,3712]{1,0:T(8,128)(2,1)S(1)}) conditional(s32[]{:T(128)} %bitcast.4, () %tuple.36, bf16[128,3712]{1,0:T(8,128)(2,1)} %pack.2), branch_computations={%region_2.3_spmd, %region_3.4_spmd} | conditional | bytes 1900552 | solution.py:773
  60.8 25.7 %all_to_all.23 = bf16[16,8,3712]{2,1,0:T(8,128)(2,1)S(1)} all-to-all(bf16[16,8,3712]{2,1,0:T(8,128)(2,1)} %bitcast.46), channel_id=1, replica_groups={{0,1,2,3,4,5,6,7,8,9,10,11,12,13,14,15},{16,17,18,19,20,21,22,23,24,25,..., dimensions={0} | all-to-all | bytes 1900544 | tf_op jit(solution)/shard_map/cond/branch_1_fun/all_to_all | solution.py:705
  86.5 1.5 pack.3
  88.0 4.5 %all-to-all-start.3 = ((bf16[16,8,3712]{2,1,0:T(8,128)(2,1)}), bf16[16,8,3712]{2,1,0:T(8,128)(2,1)}, u32[]{:S(2)}, u32[]{:S(2)}) async-start(bf16[16,8,3712]{2,1,0:T(8,128)(2,1)} %bitcast.20), calls=%async_computation.3 | async-start | bytes 1900544 | tf_op jit(solution)/shard_map/all_to_all | solution.py:705
  92.5 14.7 %expert_up.1.act_ref = bf16[160,2880]{1,0:T(8,128)(2,1)} custom-call(bf16[128,3712]{1,0:T(8,128)(2,1)S(1)} %get-tuple-element.100.refs_0_, bf16[1,2880,5760]{2,1,0:T(8,128)(2,1)} %refs_1_.3), custom_call_target="tpu_custom_call" | custom-call | flops 5308416000 | bytes 33177600 | tf_op jit(solution)/shard_map/expert_up/pallas_call | solution.py:379
  107.2 0.3 all-to-all-done.3
  107.5 19.0 %expert.1 = bf16[128,3712]{1,0:T(8,128)(2,1)} custom-call(bf16[128,3712]{1,0:T(8,128)(2,1)} %bitcast.21.refs_0_, bf16[1,2880,5760]{2,1,0:T(8,128)(2,1)} %refs_1_.3, bf16[1,2880,2880]{2,1,0:T(8,128)(2,1)} %w_down_ref.1), custom_call_target="tpu_custom_call" | custom-call | flops 7962624000 | bytes 49766400 | tf_op jit(solution)/shard_map/expert/pallas_call | solution.py:379
  126.5 4.6 %all-to-all-start.4 = ((bf16[16,8,3712]{2,1,0:T(8,128)(2,1)}), bf16[16,8,3712]{2,1,0:T(8,128)(2,1)S(1)}, u32[]{:S(2)}, u32[]{:S(2)}) async-start(bf16[16,8,3712]{2,1,0:T(8,128)(2,1)} %bitcast.44), calls=%async_computation.4 | async-start | bytes 1900544 | tf_op jit(solution)/shard_map/all_to_all | solution.py:705
  131.1 9.5 %expert_down.1 = bf16[128,3712]{1,0:T(8,128)(2,1)} custom-call(bf16[160,2880]{1,0:T(8,128)(2,1)} %expert_up.1.act_ref, bf16[1,2880,2880]{2,1,0:T(8,128)(2,1)} %w_down_ref.1), custom_call_target="tpu_custom_call" | custom-call | flops 2654208000 | bytes 16588800 | tf_op jit(solution)/shard_map/expert_down/pallas_call | solution.py:400
  140.6 5.7 %all-to-all-done.4 = bf16[16,8,3712]{2,1,0:T(8,128)(2,1)S(1)} async-done(((bf16[16,8,3712]{2,1,0:T(8,128)(2,1)}), bf16[16,8,3712]{2,1,0:T(8,128)(2,1)S(1)}, u32[]{:S(2)}, u32[]{:S(2)}) %all-to-all-start.4) | async-done | bytes 950304 | tf_op jit(solution)/shard_map/all_to_all | solution.py:705
  146.2 0.6 combine.2
  146.8 1.0 collective-permute-start.8
  147.8 0.6 gather_fusion.1
  148.4 0.7 copy.22
  149.0 26.5 %conditional.3 = (bf16[128,3712]{1,0:T(8,128)(2,1)S(1)}) conditional(s32[]{:T(128)} %bitcast.4, () %tuple.30, bf16[128,3712]{1,0:T(8,128)(2,1)} %expert_down.1), branch_computations={%region_4.5_spmd, %region_5.6_spmd} | conditional | bytes 1900552 | solution.py:773
  149.0 26.5 %all_to_all.24 = bf16[16,8,3712]{2,1,0:T(8,128)(2,1)S(1)} all-to-all(bf16[16,8,3712]{2,1,0:T(8,128)(2,1)} %bitcast.47), channel_id=1, replica_groups={{0,1,2,3,4,5,6,7,8,9,10,11,12,13,14,15},{16,17,18,19,20,21,22,23,24,25,..., dimensions={0} | all-to-all | bytes 1900544 | tf_op jit(solution)/shard_map/cond/branch_1_fun/all_to_all | solution.py:705
  175.5 1.3 combine.3
  (41 shorter events, 0.5 us)
Async XLA Ops:
  0.6 6.0 %collective-permute-start.1 = (bf16[64,2880]{1,0:T(8,128)(2,1)}, bf16[64,2880]{1,0:T(8,128)(2,1)S(1)}, u32[]{:S(2)}, u32[]{:S(2)}) collective-permute-start(bf16[64,2880]{1,0:T(8,128)(2,1)} %tokens_ref.1), channel_id=1, source_target_pairs={{0,1},{1,0},{2,3},{3,2},{4,5},{5,4},{6,7},{7,6},{8,9},{9,8},{10,11... | collective-permute-start | bytes 1105928 | tf_op jit(solution)/shard_map/ppermute | solution.py:691
  1.1 12.2 %collective-permute-start = (bf16[64,2880]{1,0:T(8,128)(2,1)}, bf16[64,2880]{1,0:T(8,128)(2,1)S(1)}, u32[]{:S(2)}, u32[]{:S(2)}) collective-permute-start(bf16[64,2880]{1,0:T(8,128)(2,1)} %tokens_ref.1), channel_id=1, source_target_pairs={{0,2},{1,3},{2,0},{3,1},{4,6},{5,7},{6,4},{7,5},{8,10},{9,11},{10,... | collective-permute-start | bytes 1105928 | tf_op jit(solution)/shard_map/ppermute | solution.py:694
  6.6 21.0 %copy-start.1 = (s32[4]{0:T(128)S(1)}, s32[4]{0:T(128)}, u32[]{:S(2)}) copy-start(s32[4]{0:T(128)} %pad_add_fusion.ids_ref) | copy-start | bytes 52
  6.6 21.0 %copy-start.2 = (s32[4]{0:T(128)S(1)}, s32[4]{0:T(128)}, u32[]{:S(2)}) copy-start(s32[4]{0:T(128)} %lengths_ref.9) | copy-start | bytes 52
  6.6 0.7 copy-start.7
  13.3 3.2 %copy-start.6 = (bf16[64,2880]{1,0:T(8,128)(2,1)}, bf16[64,2880]{1,0:T(8,128)(2,1)S(1)}, u32[]{:S(2)}) copy-start(bf16[64,2880]{1,0:T(8,128)(2,1)S(1)} %collective-permute-done.own_ref) | copy-start | bytes 1105924
  13.3 3.2 %collective-permute-start.2 = (bf16[64,2880]{1,0:T(8,128)(2,1)S(1)}, bf16[64,2880]{1,0:T(8,128)(2,1)S(1)}, u32[]{:S(2)}, u32[]{:S(2)}) collective-permute-start(bf16[64,2880]{1,0:T(8,128)(2,1)S(1)} %collective-permute-done.own_ref), channel_id=1, source_target_pairs={{0,1},{1,0},{2,3},{3,2},{4,5},{5,4},{6,7},{7,6},{8,9},{9,8},{10,11... | collective-permute-start | bytes 1105928 | tf_op jit(solution)/shard_map/ppermute | solution.py:691
  13.8 9.4 %collective-permute-start.3 = (f32[8,64]{1,0:T(8,128)S(1)}, f32[8,64]{1,0:T(8,128)S(1)}, u32[]{:S(2)}, u32[]{:S(2)}) collective-permute-start(f32[8,64]{1,0:T(8,128)S(1)} %pad_maximum_fusion.choice_ref), channel_id=1, source_target_pairs={{0,16},{1,17},{2,18},{3,19},{4,20},{5,21},{6,22},{7,23},{8,24},{9,... | collective-permute-start | bytes 6152 | tf_op jit(solution)/shard_map/ppermute | solution.py:702
  16.5 0.7 copy-start.8
  23.2 22.3 %copy-start.5 = (bf16[256,256]{1,0:T(8,128)(2,1)S(1)}, bf16[256,256]{1,0:T(8,128)(2,1)}, u32[]{:S(2)}) copy-start(bf16[256,256]{1,0:T(8,128)(2,1)} %get-tuple-element.69.pair_ref) | copy-start | bytes 393220
  23.2 35.3 %copy-start = (bf16[64,2880]{1,0:T(8,128)(2,1)S(1)}, bf16[64,2880]{1,0:T(8,128)(2,1)}, u32[]{:S(2)}) copy-start(bf16[64,2880]{1,0:T(8,128)(2,1)} %tokens_ref.1) | copy-start | bytes 1105924
  23.2 35.3 %copy-start.4 = (f32[2880]{0:T(1024)S(1)}, f32[2880]{0:T(1024)}, u32[]{:S(2)}) copy-start(f32[2880]{0:T(1024)} %gain_ref.5) | copy-start | bytes 34564
  23.3 36.0 %copy-start.3 = (s32[4]{0:T(128)S(1)}, s32[4]{0:T(128)}, u32[]{:S(2)}) copy-start(s32[4]{0:T(128)} %lengths_ref.9) | copy-start | bytes 52
  24.2 5.5 %collective-permute-start.4 = (bf16[128,256]{1,0:T(8,128)(2,1)S(1)}, bf16[128,256]{1,0:T(8,128)(2,1)S(1)}, u32[]{:S(2)}, u32[]{:S(2)}) collective-permute-start(bf16[128,256]{1,0:T(8,128)(2,1)S(1)} %slice.8), channel_id=1, source_target_pairs={{0,4},{4,8},{8,12},{12,16},{16,20},{20,24},{24,28},{1,5},{5,9},{9,... | collective-permute-start | bytes 196616 | tf_op jit(solution)/shard_map/ppermute | solution.py:38
  29.7 0.6 copy-start.9
  39.4 2.4 %collective-permute-start.5 = (bf16[2,64,2880]{2,1,0:T(8,128)(2,1)}, bf16[2,64,2880]{2,1,0:T(8,128)(2,1)S(1)}, u32[]{:S(2)}, u32[]{:S(2)}) collective-permute-start(bf16[2,64,2880]{2,1,0:T(8,128)(2,1)} %get-tuple-element.67), channel_id=1, source_target_pairs={{0,1},{1,0},{2,3},{3,2},{4,5},{5,4},{6,7},{7,6},{8,9},{9,8},{10,11... | collective-permute-start | bytes 2211848 | tf_op jit(solution)/shard_map/ppermute | solution.py:691
  44.0 14.5 %collective-permute-start.6 = (bf16[64,2880]{1,0:T(8,128)(2,1)}, bf16[64,2880]{1,0:T(8,128)(2,1)S(1)}, u32[]{:S(2)}, u32[]{:S(2)}) collective-permute-start(bf16[64,2880]{1,0:T(8,128)(2,1)} %get-tuple-element.68), channel_id=1, source_target_pairs={{0,2},{1,3},{2,0},{3,1},{4,6},{5,7},{6,4},{7,5},{8,10},{9,11},{10,... | collective-permute-start | bytes 1105928 | tf_op jit(solution)/shard_map/ppermute | solution.py:694
  58.8 27.7 %collective-permute-start.7 = (bf16[64,2880]{1,0:T(8,128)(2,1)S(1)}, bf16[64,2880]{1,0:T(8,128)(2,1)S(1)}, u32[]{:S(2)}, u32[]{:S(2)}) collective-permute-start(bf16[64,2880]{1,0:T(8,128)(2,1)S(1)} %get-tuple-element.71.moe_ref), channel_id=1, source_target_pairs={{0,16},{1,17},{2,18},{3,19},{4,20},{5,21},{6,22},{7,23},{8,24},{9,... | collective-permute-start | bytes 1105928 | tf_op jit(solution)/shard_map/ppermute | solution.py:702
  88.0 19.5 %all-to-all-start.3 = ((bf16[16,8,3712]{2,1,0:T(8,128)(2,1)}), bf16[16,8,3712]{2,1,0:T(8,128)(2,1)}, u32[]{:S(2)}, u32[]{:S(2)}) async-start(bf16[16,8,3712]{2,1,0:T(8,128)(2,1)} %bitcast.20), calls=%async_computation.3 | async-start | bytes 1900544 | tf_op jit(solution)/shard_map/all_to_all | solution.py:705
  126.5 19.8 %all-to-all-start.4 = ((bf16[16,8,3712]{2,1,0:T(8,128)(2,1)}), bf16[16,8,3712]{2,1,0:T(8,128)(2,1)S(1)}, u32[]{:S(2)}, u32[]{:S(2)}) async-start(bf16[16,8,3712]{2,1,0:T(8,128)(2,1)} %bitcast.44), calls=%async_computation.4 | async-start | bytes 1900544 | tf_op jit(solution)/shard_map/all_to_all | solution.py:705
  146.8 28.7 %collective-permute-start.8 = (bf16[64,2880]{1,0:T(8,128)(2,1)S(1)}, bf16[64,2880]{1,0:T(8,128)(2,1)S(1)}, u32[]{:S(2)}, u32[]{:S(2)}) collective-permute-start(bf16[64,2880]{1,0:T(8,128)(2,1)S(1)} %combine.2), channel_id=1, source_target_pairs={{0,16},{1,17},{2,18},{3,19},{4,20},{5,21},{6,22},{7,23},{8,24},{9,... | collective-permute-start | bytes 1105928 | tf_op jit(solution)/shard_map/ppermute | solution.py:702

commit v4 on v3

--- a/solution.py
+++ b/solution.py
@@ -589,7 +589,7 @@
     total, columns = queries.shape
     width = w_out.shape[0]
     chips = total // (2 * row_count)
-    tile = PIECE
+    tile = 2 * PIECE
     whole = lambda i, ids: (0, 0)
     smem = pl.BlockSpec(memory_space=pltpu.SMEM)
     return pl.pallas_call(

time: 178 us -> 177 us (level)
  transfers between devices with their start and end apart: 11 -> 11, of which waited for: 3 -> 3; matrix products, arithmetic and copies ran while one was open for 3% -> 3% of each run, Pallas kernels for 22% -> 23%
where the time goes in v4:
time: 177 us; the launch traced here: 176 us
  Pallas kernels  70.6 us (40%)
  blocking collectives  64.4 us (36%)
  starting transfers between devices  21.5 us (12%)
  waiting for transfers between devices  7.62 us (4%)
  local copies, waits for them, and re-layouts  5.98 us (3%)
  other arithmetic  5 us (3%)
    all_to_all x2, blocking collectives, in_half(): lax.all_to_all(array, ('tok', 'head'), split_axis=0, concat_axis=0, tiled...  52.1 us
    pallas_call x2, Pallas kernels, expert(): pl.pallas_call(functools.partial(expert_kernel, extras, in_tiles, down),...  33.7 us
    all_to_all x1, blocking collectives, exchanged_pages(): return lax.all_to_all(sent, 'tok', split_axis=0, concat_axis=0, tiled=True)  12.3 us
    pallas_call x2, Pallas kernels, project(): pl.pallas_call(functools.partial(qkv_kernel, step, chips), grid_spec=pltp...  11.9 us
    pallas_call x1, Pallas kernels, expert_down(): pl.pallas_call(functools.partial(down_kernel, extras, width), grid=(PIECE...  9.5 us
    all_to_all x2, starting transfers between devices, in_half(): lax.all_to_all(array, ('tok', 'head'), split_axis=0, concat_axis=0, tiled...  9.09 us
    pallas_call x1, Pallas kernels, attend(): pl.pallas_call(functools.partial(attend_kernel, row_count, chips), grid_s...  8.26 us
    all_to_all x2, waiting for transfers between devices, in_half(): lax.all_to_all(array, ('tok', 'head'), split_axis=0, concat_axis=0, tiled...  5.92 us
  transfers between devices with their start and end apart: 11, of which 3 were waited for; matrix products, arithmetic and copies ran while one was open for 3% of the time, Pallas kernels for 23%

profile of v4, /device:TPU:0, one launch (start us, length us, event | category | flops | bytes accessed | tf_op | source)
XLA Modules:
  0.0 176.1 jit_solution(17546381669918816215)
XLA Ops:
  0.6 0.5 collective-permute-start.1
  1.1 2.6 %collective-permute-start = (bf16[64,2880]{1,0:T(8,128)(2,1)}, bf16[64,2880]{1,0:T(8,128)(2,1)S(1)}, u32[]{:S(2)}, u32[]{:S(2)}) collective-permute-start(bf16[64,2880]{1,0:T(8,128)(2,1)} %tokens_ref.1), channel_id=1, source_target_pairs={{0,2},{1,3},{2,0},{3,1},{4,6},{5,7},{6,4},{7,5},{8,10},{9,11},{10,... | collective-permute-start | bytes 1105928 | tf_op jit(solution)/shard_map/ppermute | solution.py:694
  3.7 0.7 convert_bitcast_fusion
  4.4 0.7 pad_maximum_fusion.choice_ref
  5.1 0.7 pad_add_fusion.ids_ref
  5.8 0.7 reshape.248
  6.6 0.7 copy-done.7
  7.3 6.0 %project.2 = (bf16[256,1024]{1,0:T(8,128)(2,1)}, bf16[256,256]{1,0:T(8,128)(2,1)}) custom-call(s32[4]{0:T(128)} %pad_add_fusion.ids_ref, s32[4]{0:T(128)} %lengths_ref.9, bf16[64,2880]{1,0:T(8,128)(2,1)} %tokens_ref.1, bf16[64,2880]{1,0:T(8,128)(2,1)} %copy-done.7, f32[2880]{0:T(1024)} %gain_ref.4, bf16[2880,1280]{1,0:T(8,128)(2,1)} %w_ref.3), custom_call_target="tpu_custom_call" | custom-call | flops 943718400 | bytes 7372800 | tf_op jit(solution)/shard_map/project/pallas_call | solution.py:115
  13.3 0.2 collective-permute-start.2
  13.5 0.3 convert_reduce_fusion
  13.8 2.7 %collective-permute-start.3 = (f32[8,64]{1,0:T(8,128)S(1)}, f32[8,64]{1,0:T(8,128)S(1)}, u32[]{:S(2)}, u32[]{:S(2)}) collective-permute-start(f32[8,64]{1,0:T(8,128)S(1)} %pad_maximum_fusion.choice_ref), channel_id=1, source_target_pairs={{0,16},{1,17},{2,18},{3,19},{4,20},{5,21},{6,22},{7,23},{8,24},{9,... | collective-permute-start | bytes 6152 | tf_op jit(solution)/shard_map/ppermute | solution.py:702
  16.5 0.7 copy-done.8
  17.3 6.0 %project.3 = (bf16[256,1024]{1,0:T(8,128)(2,1)}, bf16[256,256]{1,0:T(8,128)(2,1)}) custom-call(s32[4]{0:T(128)} %pad_add_fusion.ids_ref, s32[4]{0:T(128)} %lengths_ref.9, bf16[64,2880]{1,0:T(8,128)(2,1)} %copy-done.6, bf16[64,2880]{1,0:T(8,128)(2,1)} %copy-done.8, f32[2880]{0:T(1024)} %gain_ref.4, ...), custom_call_target="tpu_custom_call", output_to_operand_aliasing={{0}: (6, {}), {1}: (7, {})} | custom-call | flops 943718400 | bytes 7372800 | tf_op jit(solution)/shard_map/project/pallas_call | solution.py:115
  23.3 0.9 slice.8
  24.2 3.4 %collective-permute-start.4 = (bf16[128,256]{1,0:T(8,128)(2,1)S(1)}, bf16[128,256]{1,0:T(8,128)(2,1)S(1)}, u32[]{:S(2)}, u32[]{:S(2)}) collective-permute-start(bf16[128,256]{1,0:T(8,128)(2,1)S(1)} %slice.8), channel_id=1, source_target_pairs={{0,4},{4,8},{8,12},{12,16},{16,20},{20,24},{24,28},{1,5},{5,9},{9,... | collective-permute-start | bytes 196616 | tf_op jit(solution)/shard_map/ppermute | solution.py:38
  27.6 1.0 slots.2
  28.6 1.0 slots.3
  29.7 0.6 copy-done.9
  30.3 8.3 %attend.1 = (f32[2,64,2880]{2,1,0:T(8,128)}, bf16[2,64,2880]{2,1,0:T(8,128)(2,1)}) custom-call(s32[4]{0:T(128)} %pad_add_fusion.ids_ref, s32[4]{0:T(128)} %lengths_ref.9, bf16[256,1024]{1,0:T(8,128)(2,1)} %get-tuple-element.57.q_ref, bf16[128,256]{1,0:T(8,128)(2,1)} %copy-done.9, bf16[256,256]{1,0:T(8,128)(2,1)} %get-tuple-element.69.pair_ref, f32[16]{0:T(128)} %sink_ref.1, ...), custom_call_target="tpu_custom_call" | custom-call | flops 1509949440 | bytes 5898240 | tf_op jit(solution)/shard_map/attend/pallas_call | solution.py:595
  38.6 0.1 select_reduce_fusion.2
  38.8 0.1 copy.20
  38.9 0.1 select_reduce_fusion.1
  39.3 0.1 select_reduce_fusion
  39.4 1.7 collective-permute-done.5
  41.0 2.2 %fusion = (bf16[64,2880]{1,0:T(8,128)(2,1)}, f32[64,2880]{1,0:T(8,128)S(1)}) fusion(f32[2,64,2880]{2,1,0:T(8,128)} %get-tuple-element.66, s32[]{:T(128)S(6)} %select_n.92, bf16[2,64,2880]{2,1,0:T(8,128)(2,1)S(1)} %collective-permute-done.5, s32[]{:T(128)S(6)} %select_n.90), kind=kLoop, calls=%fused_computation.4 | loop fusion | flops 921600 | bytes 3317768 | tf_op jit(solution)/shard_map/convert_element_type | solution.py:756
  43.2 1.5 collective-permute-start.6
  44.9 0.6 gather_fusion
  45.4 12.3 %all_to_all.25 = bf16[8,64,128]{2,1,0:T(8,128)(2,1)S(1)} all-to-all(bf16[8,64,128]{2,1,0:T(8,128)(2,1)S(1)} %bitcast.50), channel_id=1, replica_groups=mesh['tok'=8,'head'=4] {'tok'}, dimensions={0} | all-to-all | bytes 262144 | tf_op jit(solution)/shard_map/all_to_all | solution.py:648
  57.7 0.3 finish_attention.1
  58.0 0.5 collective-permute-start.7
  58.5 1.5 pack.2
  60.0 25.7 %conditional.2 = (bf16[128,3712]{1,0:T(8,128)(2,1)S(1)}) conditional(s32[]{:T(128)} %bitcast.4, () %tuple.36, bf16[128,3712]{1,0:T(8,128)(2,1)} %pack.2), branch_computations={%region_2.3_spmd, %region_3.4_spmd} | conditional | bytes 1900552 | solution.py:773
  60.0 25.7 %all_to_all.23 = bf16[16,8,3712]{2,1,0:T(8,128)(2,1)S(1)} all-to-all(bf16[16,8,3712]{2,1,0:T(8,128)(2,1)} %bitcast.46), channel_id=1, replica_groups={{0,1,2,3,4,5,6,7,8,9,10,11,12,13,14,15},{16,17,18,19,20,21,22,23,24,25,..., dimensions={0} | all-to-all | bytes 1900544 | tf_op jit(solution)/shard_map/cond/branch_1_fun/all_to_all | solution.py:705
  85.7 1.5 pack.3
  87.2 4.5 %all-to-all-start.3 = ((bf16[16,8,3712]{2,1,0:T(8,128)(2,1)}), bf16[16,8,3712]{2,1,0:T(8,128)(2,1)}, u32[]{:S(2)}, u32[]{:S(2)}) async-start(bf16[16,8,3712]{2,1,0:T(8,128)(2,1)} %bitcast.20), calls=%async_computation.3 | async-start | bytes 1900544 | tf_op jit(solution)/shard_map/all_to_all | solution.py:705
  91.7 14.7 %expert_up.1.act_ref = bf16[160,2880]{1,0:T(8,128)(2,1)} custom-call(bf16[128,3712]{1,0:T(8,128)(2,1)S(1)} %get-tuple-element.100.refs_0_, bf16[1,2880,5760]{2,1,0:T(8,128)(2,1)} %refs_1_.3), custom_call_target="tpu_custom_call" | custom-call | flops 5308416000 | bytes 33177600 | tf_op jit(solution)/shard_map/expert_up/pallas_call | solution.py:379
  106.4 0.3 all-to-all-done.3
  106.7 19.0 %expert.1 = bf16[128,3712]{1,0:T(8,128)(2,1)} custom-call(bf16[128,3712]{1,0:T(8,128)(2,1)} %bitcast.21.refs_0_, bf16[1,2880,5760]{2,1,0:T(8,128)(2,1)} %refs_1_.3, bf16[1,2880,2880]{2,1,0:T(8,128)(2,1)} %w_down_ref.1), custom_call_target="tpu_custom_call" | custom-call | flops 7962624000 | bytes 49766400 | tf_op jit(solution)/shard_map/expert/pallas_call | solution.py:379
  125.7 4.6 %all-to-all-start.4 = ((bf16[16,8,3712]{2,1,0:T(8,128)(2,1)}), bf16[16,8,3712]{2,1,0:T(8,128)(2,1)S(1)}, u32[]{:S(2)}, u32[]{:S(2)}) async-start(bf16[16,8,3712]{2,1,0:T(8,128)(2,1)} %bitcast.44), calls=%async_computation.4 | async-start | bytes 1900544 | tf_op jit(solution)/shard_map/all_to_all | solution.py:705
  130.3 9.5 %expert_down.1 = bf16[128,3712]{1,0:T(8,128)(2,1)} custom-call(bf16[160,2880]{1,0:T(8,128)(2,1)} %expert_up.1.act_ref, bf16[1,2880,2880]{2,1,0:T(8,128)(2,1)} %w_down_ref.1), custom_call_target="tpu_custom_call" | custom-call | flops 2654208000 | bytes 16588800 | tf_op jit(solution)/shard_map/expert_down/pallas_call | solution.py:400
  139.8 5.7 %all-to-all-done.4 = bf16[16,8,3712]{2,1,0:T(8,128)(2,1)S(1)} async-done(((bf16[16,8,3712]{2,1,0:T(8,128)(2,1)}), bf16[16,8,3712]{2,1,0:T(8,128)(2,1)S(1)}, u32[]{:S(2)}, u32[]{:S(2)}) %all-to-all-start.4) | async-done | bytes 950304 | tf_op jit(solution)/shard_map/all_to_all | solution.py:705
  145.4 0.6 combine.2
  146.0 1.0 collective-permute-start.8
  147.0 0.6 gather_fusion.1
  147.6 0.7 copy.22
  148.2 26.5 %conditional.3 = (bf16[128,3712]{1,0:T(8,128)(2,1)S(1)}) conditional(s32[]{:T(128)} %bitcast.4, () %tuple.30, bf16[128,3712]{1,0:T(8,128)(2,1)} %expert_down.1), branch_computations={%region_4.5_spmd, %region_5.6_spmd} | conditional | bytes 1900552 | solution.py:773
  148.2 26.5 %all_to_all.24 = bf16[16,8,3712]{2,1,0:T(8,128)(2,1)S(1)} all-to-all(bf16[16,8,3712]{2,1,0:T(8,128)(2,1)} %bitcast.47), channel_id=1, replica_groups={{0,1,2,3,4,5,6,7,8,9,10,11,12,13,14,15},{16,17,18,19,20,21,22,23,24,25,..., dimensions={0} | all-to-all | bytes 1900544 | tf_op jit(solution)/shard_map/cond/branch_1_fun/all_to_all | solution.py:705
  174.7 1.3 combine.3
  (41 shorter events, 0.5 us)
Async XLA Ops:
  0.6 6.0 %collective-permute-start.1 = (bf16[64,2880]{1,0:T(8,128)(2,1)}, bf16[64,2880]{1,0:T(8,128)(2,1)S(1)}, u32[]{:S(2)}, u32[]{:S(2)}) collective-permute-start(bf16[64,2880]{1,0:T(8,128)(2,1)} %tokens_ref.1), channel_id=1, source_target_pairs={{0,1},{1,0},{2,3},{3,2},{4,5},{5,4},{6,7},{7,6},{8,9},{9,8},{10,11... | collective-permute-start | bytes 1105928 | tf_op jit(solution)/shard_map/ppermute | solution.py:691
  1.1 12.2 %collective-permute-start = (bf16[64,2880]{1,0:T(8,128)(2,1)}, bf16[64,2880]{1,0:T(8,128)(2,1)S(1)}, u32[]{:S(2)}, u32[]{:S(2)}) collective-permute-start(bf16[64,2880]{1,0:T(8,128)(2,1)} %tokens_ref.1), channel_id=1, source_target_pairs={{0,2},{1,3},{2,0},{3,1},{4,6},{5,7},{6,4},{7,5},{8,10},{9,11},{10,... | collective-permute-start | bytes 1105928 | tf_op jit(solution)/shard_map/ppermute | solution.py:694
  6.6 21.0 %copy-start.1 = (s32[4]{0:T(128)S(1)}, s32[4]{0:T(128)}, u32[]{:S(2)}) copy-start(s32[4]{0:T(128)} %pad_add_fusion.ids_ref) | copy-start | bytes 52
  6.6 21.0 %copy-start.2 = (s32[4]{0:T(128)S(1)}, s32[4]{0:T(128)}, u32[]{:S(2)}) copy-start(s32[4]{0:T(128)} %lengths_ref.9) | copy-start | bytes 52
  6.6 0.7 copy-start.7
  13.3 3.2 %copy-start.6 = (bf16[64,2880]{1,0:T(8,128)(2,1)}, bf16[64,2880]{1,0:T(8,128)(2,1)S(1)}, u32[]{:S(2)}) copy-start(bf16[64,2880]{1,0:T(8,128)(2,1)S(1)} %collective-permute-done.own_ref) | copy-start | bytes 1105924
  13.3 3.2 %collective-permute-start.2 = (bf16[64,2880]{1,0:T(8,128)(2,1)S(1)}, bf16[64,2880]{1,0:T(8,128)(2,1)S(1)}, u32[]{:S(2)}, u32[]{:S(2)}) collective-permute-start(bf16[64,2880]{1,0:T(8,128)(2,1)S(1)} %collective-permute-done.own_ref), channel_id=1, source_target_pairs={{0,1},{1,0},{2,3},{3,2},{4,5},{5,4},{6,7},{7,6},{8,9},{9,8},{10,11... | collective-permute-start | bytes 1105928 | tf_op jit(solution)/shard_map/ppermute | solution.py:691
  13.8 9.4 %collective-permute-start.3 = (f32[8,64]{1,0:T(8,128)S(1)}, f32[8,64]{1,0:T(8,128)S(1)}, u32[]{:S(2)}, u32[]{:S(2)}) collective-permute-start(f32[8,64]{1,0:T(8,128)S(1)} %pad_maximum_fusion.choice_ref), channel_id=1, source_target_pairs={{0,16},{1,17},{2,18},{3,19},{4,20},{5,21},{6,22},{7,23},{8,24},{9,... | collective-permute-start | bytes 6152 | tf_op jit(solution)/shard_map/ppermute | solution.py:702
  16.5 0.7 copy-start.8
  23.2 21.6 %copy-start.5 = (bf16[256,256]{1,0:T(8,128)(2,1)S(1)}, bf16[256,256]{1,0:T(8,128)(2,1)}, u32[]{:S(2)}) copy-start(bf16[256,256]{1,0:T(8,128)(2,1)} %get-tuple-element.69.pair_ref) | copy-start | bytes 393220
  23.2 34.5 %copy-start = (bf16[64,2880]{1,0:T(8,128)(2,1)S(1)}, bf16[64,2880]{1,0:T(8,128)(2,1)}, u32[]{:S(2)}) copy-start(bf16[64,2880]{1,0:T(8,128)(2,1)} %tokens_ref.1) | copy-start | bytes 1105924
  23.2 34.5 %copy-start.4 = (f32[2880]{0:T(1024)S(1)}, f32[2880]{0:T(1024)}, u32[]{:S(2)}) copy-start(f32[2880]{0:T(1024)} %gain_ref.5) | copy-start | bytes 34564
  23.3 35.2 %copy-start.3 = (s32[4]{0:T(128)S(1)}, s32[4]{0:T(128)}, u32[]{:S(2)}) copy-start(s32[4]{0:T(128)} %lengths_ref.9) | copy-start | bytes 52
  24.2 5.5 %collective-permute-start.4 = (bf16[128,256]{1,0:T(8,128)(2,1)S(1)}, bf16[128,256]{1,0:T(8,128)(2,1)S(1)}, u32[]{:S(2)}, u32[]{:S(2)}) collective-permute-start(bf16[128,256]{1,0:T(8,128)(2,1)S(1)} %slice.8), channel_id=1, source_target_pairs={{0,4},{4,8},{8,12},{12,16},{16,20},{20,24},{24,28},{1,5},{5,9},{9,... | collective-permute-start | bytes 196616 | tf_op jit(solution)/shard_map/ppermute | solution.py:38
  29.7 0.6 copy-start.9
  38.6 2.4 %collective-permute-start.5 = (bf16[2,64,2880]{2,1,0:T(8,128)(2,1)}, bf16[2,64,2880]{2,1,0:T(8,128)(2,1)S(1)}, u32[]{:S(2)}, u32[]{:S(2)}) collective-permute-start(bf16[2,64,2880]{2,1,0:T(8,128)(2,1)} %get-tuple-element.67), channel_id=1, source_target_pairs={{0,1},{1,0},{2,3},{3,2},{4,5},{5,4},{6,7},{7,6},{8,9},{9,8},{10,11... | collective-permute-start | bytes 2211848 | tf_op jit(solution)/shard_map/ppermute | solution.py:691
  43.2 14.5 %collective-permute-start.6 = (bf16[64,2880]{1,0:T(8,128)(2,1)}, bf16[64,2880]{1,0:T(8,128)(2,1)S(1)}, u32[]{:S(2)}, u32[]{:S(2)}) collective-permute-start(bf16[64,2880]{1,0:T(8,128)(2,1)} %get-tuple-element.68), channel_id=1, source_target_pairs={{0,2},{1,3},{2,0},{3,1},{4,6},{5,7},{6,4},{7,5},{8,10},{9,11},{10,... | collective-permute-start | bytes 1105928 | tf_op jit(solution)/shard_map/ppermute | solution.py:694
  58.0 27.7 %collective-permute-start.7 = (bf16[64,2880]{1,0:T(8,128)(2,1)S(1)}, bf16[64,2880]{1,0:T(8,128)(2,1)S(1)}, u32[]{:S(2)}, u32[]{:S(2)}) collective-permute-start(bf16[64,2880]{1,0:T(8,128)(2,1)S(1)} %get-tuple-element.71.moe_ref), channel_id=1, source_target_pairs={{0,16},{1,17},{2,18},{3,19},{4,20},{5,21},{6,22},{7,23},{8,24},{9,... | collective-permute-start | bytes 1105928 | tf_op jit(solution)/shard_map/ppermute | solution.py:702
  87.2 19.5 %all-to-all-start.3 = ((bf16[16,8,3712]{2,1,0:T(8,128)(2,1)}), bf16[16,8,3712]{2,1,0:T(8,128)(2,1)}, u32[]{:S(2)}, u32[]{:S(2)}) async-start(bf16[16,8,3712]{2,1,0:T(8,128)(2,1)} %bitcast.20), calls=%async_computation.3 | async-start | bytes 1900544 | tf_op jit(solution)/shard_map/all_to_all | solution.py:705
  125.7 19.8 %all-to-all-start.4 = ((bf16[16,8,3712]{2,1,0:T(8,128)(2,1)}), bf16[16,8,3712]{2,1,0:T(8,128)(2,1)S(1)}, u32[]{:S(2)}, u32[]{:S(2)}) async-start(bf16[16,8,3712]{2,1,0:T(8,128)(2,1)} %bitcast.44), calls=%async_computation.4 | async-start | bytes 1900544 | tf_op jit(solution)/shard_map/all_to_all | solution.py:705
  146.0 28.7 %collective-permute-start.8 = (bf16[64,2880]{1,0:T(8,128)(2,1)S(1)}, bf16[64,2880]{1,0:T(8,128)(2,1)S(1)}, u32[]{:S(2)}, u32[]{:S(2)}) collective-permute-start(bf16[64,2880]{1,0:T(8,128)(2,1)S(1)} %combine.2), channel_id=1, source_target_pairs={{0,16},{1,17},{2,18},{3,19},{4,20},{5,21},{6,22},{7,23},{8,24},{9,... | collective-permute-start | bytes 1105928 | tf_op jit(solution)/shard_map/ppermute | solution.py:702

commit v5 on v4

--- a/solution.py
+++ b/solution.py
@@ -630,7 +630,7 @@
     return (target, order_rank, page_grid % pages_dev)
 
 
-def exchanged_pages(pairs, page_table, tok_id, n_tok):
+def leaving_pages(pairs, page_table, tok_id, n_tok):
     rows = pairs.shape[0]
     groups = pairs.shape[1] // (2 * HEAD_SIZE)
     pages_dev = rows // PAGE_TOKENS
@@ -644,8 +644,7 @@
         order_rank[tok_id][:, None, None] == share_ids[None, None, :]
     )
     pick_page = jnp.sum(jnp.where(matched, page_ids[:, None, None], 0), axis=0).reshape(-1)
-    sent = paged[pick_page].reshape(n_tok, share_count * groups * PAGE_TOKENS, 2 * HEAD_SIZE)
-    return lax.all_to_all(sent, "tok", split_axis=0, concat_axis=0, tiled=True)
+    return paged[pick_page].reshape(n_tok, share_count * groups * PAGE_TOKENS, 2 * HEAD_SIZE)
 
 
 def landed_pages(arrived, page_table, tok_id, n_tok, groups):
@@ -740,23 +739,24 @@
     query_rows, key_value_pairs = placed
     rim_rows = passed_along(key_value_pairs[tok_dev - ATTEND_WINDOW :], "tok", 1)
     slots = tables(choice, False, *sizes), tables(far_choice, True, *sizes)
-    rim_rows, slots = lax.optimization_barrier((rim_rows, slots))
+    pages = leaving_pages(key_value_pairs, page_table, tok_id, n_tok)
+    rim_rows, slots, pages = lax.optimization_barrier((rim_rows, slots, pages))
     (own_picks, own_weights), (far_picks, far_weights) = slots
     kept, sent = attend(
         ids, lengths, query_rows, rim_rows, key_value_pairs, sinks, w_out_attn.T, row_count
     )
     sent = to_core(sent)
 
-    def chip_sum(chip):
+    def chip_sum(kept, sent, chip):
         here = lax.dynamic_index_in_dim(kept, chip, 0, keepdims=False)
         there = lax.dynamic_index_in_dim(sent, chip, 0, keepdims=False)
         return here + there.astype(jnp.float32)
 
-    own_sum = chip_sum(y_id)
-    leaving = [chip_sum((y_id + k) % n_y).astype(jnp.bfloat16) for k in range(1, n_y)]
-    leaving, key_value_pairs = lax.optimization_barrier((leaving, key_value_pairs))
+    leaving = [chip_sum(kept, sent, (y_id + k) % n_y).astype(jnp.bfloat16) for k in range(1, n_y)]
+    leaving, pages, kept, sent = lax.optimization_barrier((leaving, pages, kept, sent))
     other_sums = jnp.stack([along_y(part, k + 1) for k, part in enumerate(leaving)])
-    pages = exchanged_pages(key_value_pairs, page_table, tok_id, n_tok)
+    pages = lax.all_to_all(pages, "tok", split_axis=0, concat_axis=0, tiled=True)
+    own_sum = chip_sum(kept, sent, y_id)
     other_sums, pages = lax.optimization_barrier((other_sums, pages))
 
     resid, moe_in = finish_attention(

time: 177 us -> 176 us (level)
  blocking collectives: 64.4 us -> 53.2 us
  waiting for transfers between devices: 7.62 us -> 14.5 us
  starting transfers between devices: 21.5 us -> 23.5 us
    all_to_all x1 -> x0, blocking collectives: 12.3 us -> none  [exchanged_pages(): return lax.all_to_all(sent, 'tok', split_axis=0, concat_axis=0, tiled=True)]
    all_to_all x0 -> x1, waiting for transfers between devices: none -> 6.09 us  [per_device(): lax.all_to_all(pages, 'tok', split_axis=0, concat_axis=0, tiled=True)]
    all_to_all x0 -> x1, starting transfers between devices: none -> 3.37 us  [per_device(): lax.all_to_all(pages, 'tok', split_axis=0, concat_axis=0, tiled=True)]
  transfers between devices with their start and end apart: 11 -> 12, of which waited for: 3 -> 4; matrix products, arithmetic and copies ran while one was open for 3% -> 5% of each run, Pallas kernels for 23% -> 23%
where the time goes in v5:
time: 176 us
  Pallas kernels  70.8 us (40%)
  blocking collectives  53.2 us (30%)
  starting transfers between devices  23.5 us (13%)
  waiting for transfers between devices  14.5 us (8%)
  local copies, waits for them, and re-layouts  7.53 us (4%)
  other arithmetic  5.17 us (3%)
    all_to_all x2, blocking collectives, in_half(): lax.all_to_all(array, ('tok', 'head'), split_axis=0, concat_axis=0, tiled...  53.2 us
    pallas_call x2, Pallas kernels, expert(): pl.pallas_call(functools.partial(expert_kernel, extras, in_tiles, down),...  33.7 us
    pallas_call x2, Pallas kernels, project(): pl.pallas_call(functools.partial(qkv_kernel, step, chips), grid_spec=pltp...  11.9 us
    pallas_call x1, Pallas kernels, expert_down(): pl.pallas_call(functools.partial(down_kernel, extras, width), grid=(PIECE...  9.5 us
    all_to_all x2, starting transfers between devices, in_half(): lax.all_to_all(array, ('tok', 'head'), split_axis=0, concat_axis=0, tiled...  9.09 us
    pallas_call x1, Pallas kernels, attend(): pl.pallas_call(functools.partial(attend_kernel, row_count, chips), grid_s...  8.4 us
    all_to_all x1, waiting for transfers between devices, per_device(): lax.all_to_all(pages, 'tok', split_axis=0, concat_axis=0, tiled=True)  6.09 us
    all_to_all x2, waiting for transfers between devices, in_half(): lax.all_to_all(array, ('tok', 'head'), split_axis=0, concat_axis=0, tiled...  5.91 us
  transfers between devices with their start and end apart: 12, of which 4 were waited for; matrix products, arithmetic and copies ran while one was open for 5% of the time, Pallas kernels for 23%

profile of v5, /device:TPU:0, one launch (start us, length us, event | category | flops | bytes accessed | tf_op | source)
XLA Modules:
  0.0 175.6 jit_solution(2219378168359036840)
XLA Ops:
  0.6 0.5 collective-permute-start.1
  1.1 2.6 %collective-permute-start = (bf16[64,2880]{1,0:T(8,128)(2,1)}, bf16[64,2880]{1,0:T(8,128)(2,1)S(1)}, u32[]{:S(2)}, u32[]{:S(2)}) collective-permute-start(bf16[64,2880]{1,0:T(8,128)(2,1)} %tokens_ref.1), channel_id=1, source_target_pairs={{0,2},{1,3},{2,0},{3,1},{4,6},{5,7},{6,4},{7,5},{8,10},{9,11},{10,... | collective-permute-start | bytes 1105928 | tf_op jit(solution)/shard_map/ppermute | solution.py:693
  3.8 0.7 reshape.248
  4.5 0.7 convert_bitcast_fusion
  5.2 0.3 convert_reduce_fusion
  5.5 0.7 pad_maximum_fusion.choice_ref
  6.2 0.1 select_reduce_fusion.1
  6.4 0.7 pad_add_fusion.ids_ref
  7.1 0.7 copy-done.6
  7.8 6.0 %project.2 = (bf16[256,1024]{1,0:T(8,128)(2,1)}, bf16[256,256]{1,0:T(8,128)(2,1)}) custom-call(s32[4]{0:T(128)} %pad_add_fusion.ids_ref, s32[4]{0:T(128)} %lengths_ref.9, bf16[64,2880]{1,0:T(8,128)(2,1)} %tokens_ref.1, bf16[64,2880]{1,0:T(8,128)(2,1)} %copy-done.6, f32[2880]{0:T(1024)} %gain_ref.4, bf16[2880,1280]{1,0:T(8,128)(2,1)} %w_ref.3), custom_call_target="tpu_custom_call" | custom-call | flops 943718400 | bytes 7372800 | tf_op jit(solution)/shard_map/project/pallas_call | solution.py:115
  13.8 0.2 collective-permute-start.2
  14.0 0.1 select_reduce_fusion.2
  14.6 2.7 %collective-permute-start.3 = (f32[8,64]{1,0:T(8,128)S(1)}, f32[8,64]{1,0:T(8,128)S(1)}, u32[]{:S(2)}, u32[]{:S(2)}) collective-permute-start(f32[8,64]{1,0:T(8,128)S(1)} %pad_maximum_fusion.choice_ref), channel_id=1, source_target_pairs={{0,16},{1,17},{2,18},{3,19},{4,20},{5,21},{6,22},{7,23},{8,24},{9,... | collective-permute-start | bytes 6152 | tf_op jit(solution)/shard_map/ppermute | solution.py:701
  17.3 0.7 copy-done.7
  18.0 6.0 %project.3 = (bf16[256,1024]{1,0:T(8,128)(2,1)}, bf16[256,256]{1,0:T(8,128)(2,1)}) custom-call(s32[4]{0:T(128)} %pad_add_fusion.ids_ref, s32[4]{0:T(128)} %lengths_ref.9, bf16[64,2880]{1,0:T(8,128)(2,1)} %copy-done.5, bf16[64,2880]{1,0:T(8,128)(2,1)} %copy-done.7, f32[2880]{0:T(1024)} %gain_ref.4, ...), custom_call_target="tpu_custom_call", output_to_operand_aliasing={{0}: (6, {}), {1}: (7, {})} | custom-call | flops 943718400 | bytes 7372800 | tf_op jit(solution)/shard_map/project/pallas_call | solution.py:115
  24.0 0.9 slice.8
  24.9 3.4 %collective-permute-start.4 = (bf16[128,256]{1,0:T(8,128)(2,1)S(1)}, bf16[128,256]{1,0:T(8,128)(2,1)S(1)}, u32[]{:S(2)}, u32[]{:S(2)}) collective-permute-start(bf16[128,256]{1,0:T(8,128)(2,1)S(1)} %slice.8), channel_id=1, source_target_pairs={{0,4},{4,8},{8,12},{12,16},{16,20},{20,24},{24,28},{1,5},{5,9},{9,... | collective-permute-start | bytes 196616 | tf_op jit(solution)/shard_map/ppermute | solution.py:38
  28.3 0.9 reshape.247
  29.3 1.0 slots.2
  30.3 1.0 slots.3
  31.4 1.2 gather_fusion
  32.6 0.6 copy-done.8
  33.2 8.4 %attend.1 = (f32[2,64,2880]{2,1,0:T(8,128)}, bf16[2,64,2880]{2,1,0:T(8,128)(2,1)}) custom-call(s32[4]{0:T(128)} %pad_add_fusion.ids_ref, s32[4]{0:T(128)} %lengths_ref.9, bf16[256,1024]{1,0:T(8,128)(2,1)} %get-tuple-element.60.q_ref, bf16[128,256]{1,0:T(8,128)(2,1)} %copy-done.8, bf16[256,256]{1,0:T(8,128)(2,1)} %get-tuple-element.61.pair_ref, f32[16]{0:T(128)} %sink_ref.1, ...), custom_call_target="tpu_custom_call" | custom-call | flops 1509949440 | bytes 5898240 | tf_op jit(solution)/shard_map/attend/pallas_call | solution.py:595
  41.6 2.4 %collective-permute-done.5 = bf16[2,64,2880]{2,1,0:T(8,128)(2,1)S(1)} collective-permute-done((bf16[2,64,2880]{2,1,0:T(8,128)(2,1)}, bf16[2,64,2880]{2,1,0:T(8,128)(2,1)S(1)}, u32[]{:S(2)}, u32[]{:S(2)}) %collective-permute-start.5) | collective-permute-done | bytes 737312 | tf_op jit(solution)/shard_map/ppermute | solution.py:690
  44.1 1.2 fusion
  45.3 1.1 collective-permute-start.6
  46.4 3.4 %all-to-all-start.2 = ((bf16[8,64,128]{2,1,0:T(8,128)(2,1)}), bf16[8,64,128]{2,1,0:T(8,128)(2,1)S(1)}, u32[]{:S(2)}, u32[]{:S(2)}) async-start(bf16[8,64,128]{2,1,0:T(8,128)(2,1)} %bitcast.15), calls=%async_computation.2 | async-start | bytes 262144 | tf_op jit(solution)/shard_map/all_to_all | solution.py:758
  49.8 1.2 add_bitcast_fusion.own_ref
  51.0 6.1 %all-to-all-done.2 = bf16[8,64,128]{2,1,0:T(8,128)(2,1)S(1)} async-done(((bf16[8,64,128]{2,1,0:T(8,128)(2,1)}), bf16[8,64,128]{2,1,0:T(8,128)(2,1)S(1)}, u32[]{:S(2)}, u32[]{:S(2)}) %all-to-all-start.2) | async-done | bytes 131104 | tf_op jit(solution)/shard_map/all_to_all | solution.py:758
  57.1 0.3 finish_attention.1
  57.4 0.5 collective-permute-start.7
  57.9 1.5 pack.2
  59.4 26.7 %conditional.2 = (bf16[128,3712]{1,0:T(8,128)(2,1)S(1)}) conditional(s32[]{:T(128)} %bitcast.4, () %tuple.36, bf16[128,3712]{1,0:T(8,128)(2,1)} %pack.2), branch_computations={%region_2.3_spmd, %region_3.4_spmd} | conditional | bytes 1900552 | solution.py:773
  59.4 26.7 %all_to_all.23 = bf16[16,8,3712]{2,1,0:T(8,128)(2,1)S(1)} all-to-all(bf16[16,8,3712]{2,1,0:T(8,128)(2,1)} %bitcast.46), channel_id=1, replica_groups={{0,1,2,3,4,5,6,7,8,9,10,11,12,13,14,15},{16,17,18,19,20,21,22,23,24,25,..., dimensions={0} | all-to-all | bytes 1900544 | tf_op jit(solution)/shard_map/cond/branch_1_fun/all_to_all | solution.py:704
  86.1 1.5 pack.3
  87.6 4.5 %all-to-all-start.3 = ((bf16[16,8,3712]{2,1,0:T(8,128)(2,1)}), bf16[16,8,3712]{2,1,0:T(8,128)(2,1)}, u32[]{:S(2)}, u32[]{:S(2)}) async-start(bf16[16,8,3712]{2,1,0:T(8,128)(2,1)} %bitcast.20), calls=%async_computation.3 | async-start | bytes 1900544 | tf_op jit(solution)/shard_map/all_to_all | solution.py:704
  92.1 14.7 %expert_up.1.act_ref = bf16[160,2880]{1,0:T(8,128)(2,1)} custom-call(bf16[128,3712]{1,0:T(8,128)(2,1)S(1)} %get-tuple-element.104.refs_0_, bf16[1,2880,5760]{2,1,0:T(8,128)(2,1)} %refs_1_.3), custom_call_target="tpu_custom_call" | custom-call | flops 5308416000 | bytes 33177600 | tf_op jit(solution)/shard_map/expert_up/pallas_call | solution.py:379
  106.8 0.3 all-to-all-done.3
  107.1 19.0 %expert.1 = bf16[128,3712]{1,0:T(8,128)(2,1)} custom-call(bf16[128,3712]{1,0:T(8,128)(2,1)} %bitcast.21.refs_0_, bf16[1,2880,5760]{2,1,0:T(8,128)(2,1)} %refs_1_.3, bf16[1,2880,2880]{2,1,0:T(8,128)(2,1)} %w_down_ref.1), custom_call_target="tpu_custom_call" | custom-call | flops 7962624000 | bytes 49766400 | tf_op jit(solution)/shard_map/expert/pallas_call | solution.py:379
  126.1 4.6 %all-to-all-start.4 = ((bf16[16,8,3712]{2,1,0:T(8,128)(2,1)}), bf16[16,8,3712]{2,1,0:T(8,128)(2,1)S(1)}, u32[]{:S(2)}, u32[]{:S(2)}) async-start(bf16[16,8,3712]{2,1,0:T(8,128)(2,1)} %bitcast.44), calls=%async_computation.4 | async-start | bytes 1900544 | tf_op jit(solution)/shard_map/all_to_all | solution.py:704
  130.7 9.5 %expert_down.1 = bf16[128,3712]{1,0:T(8,128)(2,1)} custom-call(bf16[160,2880]{1,0:T(8,128)(2,1)} %expert_up.1.act_ref, bf16[1,2880,2880]{2,1,0:T(8,128)(2,1)} %w_down_ref.1), custom_call_target="tpu_custom_call" | custom-call | flops 2654208000 | bytes 16588800 | tf_op jit(solution)/shard_map/expert_down/pallas_call | solution.py:400
  140.2 5.7 %all-to-all-done.4 = bf16[16,8,3712]{2,1,0:T(8,128)(2,1)S(1)} async-done(((bf16[16,8,3712]{2,1,0:T(8,128)(2,1)}), bf16[16,8,3712]{2,1,0:T(8,128)(2,1)S(1)}, u32[]{:S(2)}, u32[]{:S(2)}) %all-to-all-start.4) | async-done | bytes 950304 | tf_op jit(solution)/shard_map/all_to_all | solution.py:704
  145.8 0.6 combine.2
  146.5 0.6 gather_fusion.1
  147.1 0.7 copy.22
  147.8 26.5 %conditional.3 = (bf16[128,3712]{1,0:T(8,128)(2,1)S(1)}) conditional(s32[]{:T(128)} %bitcast.4, () %tuple.30, bf16[128,3712]{1,0:T(8,128)(2,1)} %expert_down.1), branch_computations={%region_4.5_spmd, %region_5.6_spmd} | conditional | bytes 1900552 | solution.py:773
  147.8 26.5 %all_to_all.24 = bf16[16,8,3712]{2,1,0:T(8,128)(2,1)S(1)} all-to-all(bf16[16,8,3712]{2,1,0:T(8,128)(2,1)} %bitcast.47), channel_id=1, replica_groups={{0,1,2,3,4,5,6,7,8,9,10,11,12,13,14,15},{16,17,18,19,20,21,22,23,24,25,..., dimensions={0} | all-to-all | bytes 1900544 | tf_op jit(solution)/shard_map/cond/branch_1_fun/all_to_all | solution.py:704
  174.2 1.3 combine.3
  (41 shorter events, 0.7 us)
Async XLA Ops:
  0.6 6.4 %collective-permute-start.1 = (bf16[64,2880]{1,0:T(8,128)(2,1)}, bf16[64,2880]{1,0:T(8,128)(2,1)S(1)}, u32[]{:S(2)}, u32[]{:S(2)}) collective-permute-start(bf16[64,2880]{1,0:T(8,128)(2,1)} %tokens_ref.1), channel_id=1, source_target_pairs={{0,1},{1,0},{2,3},{3,2},{4,5},{5,4},{6,7},{7,6},{8,9},{9,8},{10,11... | collective-permute-start | bytes 1105928 | tf_op jit(solution)/shard_map/ppermute | solution.py:690
  1.1 12.6 %collective-permute-start = (bf16[64,2880]{1,0:T(8,128)(2,1)}, bf16[64,2880]{1,0:T(8,128)(2,1)S(1)}, u32[]{:S(2)}, u32[]{:S(2)}) collective-permute-start(bf16[64,2880]{1,0:T(8,128)(2,1)} %tokens_ref.1), channel_id=1, source_target_pairs={{0,2},{1,3},{2,0},{3,1},{4,6},{5,7},{6,4},{7,5},{8,10},{9,11},{10,... | collective-permute-start | bytes 1105928 | tf_op jit(solution)/shard_map/ppermute | solution.py:693
  7.1 0.7 copy-start.6
  13.8 15.5 %copy-start.1 = (s32[4]{0:T(128)S(1)}, s32[4]{0:T(128)}, u32[]{:S(2)}) copy-start(s32[4]{0:T(128)} %pad_add_fusion.ids_ref) | copy-start | bytes 52
  13.8 15.5 %copy-start.2 = (s32[4]{0:T(128)S(1)}, s32[4]{0:T(128)}, u32[]{:S(2)}) copy-start(s32[4]{0:T(128)} %lengths_ref.9) | copy-start | bytes 52
  13.8 3.5 %copy-start.5 = (bf16[64,2880]{1,0:T(8,128)(2,1)}, bf16[64,2880]{1,0:T(8,128)(2,1)S(1)}, u32[]{:S(2)}) copy-start(bf16[64,2880]{1,0:T(8,128)(2,1)S(1)} %collective-permute-done.own_ref) | copy-start | bytes 1105924
  13.8 3.5 %collective-permute-start.2 = (bf16[64,2880]{1,0:T(8,128)(2,1)S(1)}, bf16[64,2880]{1,0:T(8,128)(2,1)S(1)}, u32[]{:S(2)}, u32[]{:S(2)}) collective-permute-start(bf16[64,2880]{1,0:T(8,128)(2,1)S(1)} %collective-permute-done.own_ref), channel_id=1, source_target_pairs={{0,1},{1,0},{2,3},{3,2},{4,5},{5,4},{6,7},{7,6},{8,9},{9,8},{10,11... | collective-permute-start | bytes 1105928 | tf_op jit(solution)/shard_map/ppermute | solution.py:690
  14.6 9.4 %collective-permute-start.3 = (f32[8,64]{1,0:T(8,128)S(1)}, f32[8,64]{1,0:T(8,128)S(1)}, u32[]{:S(2)}, u32[]{:S(2)}) collective-permute-start(f32[8,64]{1,0:T(8,128)S(1)} %pad_maximum_fusion.choice_ref), channel_id=1, source_target_pairs={{0,16},{1,17},{2,18},{3,19},{4,20},{5,21},{6,22},{7,23},{8,24},{9,... | collective-permute-start | bytes 6152 | tf_op jit(solution)/shard_map/ppermute | solution.py:701
  17.3 0.7 copy-start.7
  24.0 33.1 %copy-start = (bf16[64,2880]{1,0:T(8,128)(2,1)S(1)}, bf16[64,2880]{1,0:T(8,128)(2,1)}, u32[]{:S(2)}) copy-start(bf16[64,2880]{1,0:T(8,128)(2,1)} %tokens_ref.1) | copy-start | bytes 1105924
  24.0 33.1 %copy-start.4 = (f32[2880]{0:T(1024)S(1)}, f32[2880]{0:T(1024)}, u32[]{:S(2)}) copy-start(f32[2880]{0:T(1024)} %gain_ref.5) | copy-start | bytes 34564
  24.9 7.7 %collective-permute-start.4 = (bf16[128,256]{1,0:T(8,128)(2,1)S(1)}, bf16[128,256]{1,0:T(8,128)(2,1)S(1)}, u32[]{:S(2)}, u32[]{:S(2)}) collective-permute-start(bf16[128,256]{1,0:T(8,128)(2,1)S(1)} %slice.8), channel_id=1, source_target_pairs={{0,4},{4,8},{8,12},{12,16},{16,20},{20,24},{24,28},{1,5},{5,9},{9,... | collective-permute-start | bytes 196616 | tf_op jit(solution)/shard_map/ppermute | solution.py:38
  32.6 0.6 copy-start.8
  33.2 24.6 %copy-start.3 = (s32[4]{0:T(128)S(1)}, s32[4]{0:T(128)}, u32[]{:S(2)}) copy-start(s32[4]{0:T(128)} %lengths_ref.9) | copy-start | bytes 52
  41.6 2.4 %collective-permute-start.5 = (bf16[2,64,2880]{2,1,0:T(8,128)(2,1)}, bf16[2,64,2880]{2,1,0:T(8,128)(2,1)S(1)}, u32[]{:S(2)}, u32[]{:S(2)}) collective-permute-start(bf16[2,64,2880]{2,1,0:T(8,128)(2,1)} %get-tuple-element.70), channel_id=1, source_target_pairs={{0,1},{1,0},{2,3},{3,2},{4,5},{5,4},{6,7},{7,6},{8,9},{9,8},{10,11... | collective-permute-start | bytes 2211848 | tf_op jit(solution)/shard_map/ppermute | solution.py:690
  45.3 11.8 %collective-permute-start.6 = (bf16[64,2880]{1,0:T(8,128)(2,1)S(1)}, bf16[64,2880]{1,0:T(8,128)(2,1)S(1)}, u32[]{:S(2)}, u32[]{:S(2)}) collective-permute-start(bf16[64,2880]{1,0:T(8,128)(2,1)S(1)} %fusion), channel_id=1, source_target_pairs={{0,2},{1,3},{2,0},{3,1},{4,6},{5,7},{6,4},{7,5},{8,10},{9,11},{10,... | collective-permute-start | bytes 1105928 | tf_op jit(solution)/shard_map/ppermute | solution.py:693
  46.4 10.7 %all-to-all-start.2 = ((bf16[8,64,128]{2,1,0:T(8,128)(2,1)}), bf16[8,64,128]{2,1,0:T(8,128)(2,1)S(1)}, u32[]{:S(2)}, u32[]{:S(2)}) async-start(bf16[8,64,128]{2,1,0:T(8,128)(2,1)} %bitcast.15), calls=%async_computation.2 | async-start | bytes 262144 | tf_op jit(solution)/shard_map/all_to_all | solution.py:758
  57.4 28.7 %collective-permute-start.7 = (bf16[64,2880]{1,0:T(8,128)(2,1)S(1)}, bf16[64,2880]{1,0:T(8,128)(2,1)S(1)}, u32[]{:S(2)}, u32[]{:S(2)}) collective-permute-start(bf16[64,2880]{1,0:T(8,128)(2,1)S(1)} %get-tuple-element.77.moe_ref), channel_id=1, source_target_pairs={{0,16},{1,17},{2,18},{3,19},{4,20},{5,21},{6,22},{7,23},{8,24},{9,... | collective-permute-start | bytes 1105928 | tf_op jit(solution)/shard_map/ppermute | solution.py:701
  87.6 19.5 %all-to-all-start.3 = ((bf16[16,8,3712]{2,1,0:T(8,128)(2,1)}), bf16[16,8,3712]{2,1,0:T(8,128)(2,1)}, u32[]{:S(2)}, u32[]{:S(2)}) async-start(bf16[16,8,3712]{2,1,0:T(8,128)(2,1)} %bitcast.20), calls=%async_computation.3 | async-start | bytes 1900544 | tf_op jit(solution)/shard_map/all_to_all | solution.py:704
  126.1 19.8 %all-to-all-start.4 = ((bf16[16,8,3712]{2,1,0:T(8,128)(2,1)}), bf16[16,8,3712]{2,1,0:T(8,128)(2,1)S(1)}, u32[]{:S(2)}, u32[]{:S(2)}) async-start(bf16[16,8,3712]{2,1,0:T(8,128)(2,1)} %bitcast.44), calls=%async_computation.4 | async-start | bytes 1900544 | tf_op jit(solution)/shard_map/all_to_all | solution.py:704
  146.4 27.8 %collective-permute-start.8 = (bf16[64,2880]{1,0:T(8,128)(2,1)S(1)}, bf16[64,2880]{1,0:T(8,128)(2,1)S(1)}, u32[]{:S(2)}, u32[]{:S(2)}) collective-permute-start(bf16[64,2880]{1,0:T(8,128)(2,1)S(1)} %combine.2), channel_id=1, source_target_pairs={{0,16},{1,17},{2,18},{3,19},{4,20},{5,21},{6,22},{7,23},{8,24},{9,... | collective-permute-start | bytes 1105928 | tf_op jit(solution)/shard_map/ppermute | solution.py:701

commit v6 on v5

--- a/solution.py
+++ b/solution.py
@@ -581,7 +581,7 @@
     )
     for chip in range(chips):
         at, then = chip * row_count, (chips + chip) * row_count
-        kept_ref[chip] = product[at : at + row_count]
+        kept_ref[chip] = product[at : at + row_count].astype(jnp.bfloat16)
         sent_ref[chip] = product[then : then + row_count].astype(jnp.bfloat16)
 
 
@@ -609,7 +609,7 @@
             scratch_shapes=[pltpu.VMEM(queries.shape, jnp.bfloat16)],
         ),
         out_shape=[
-            jax.ShapeDtypeStruct((chips, row_count, width), jnp.float32),
+            jax.ShapeDtypeStruct((chips, row_count, width), jnp.bfloat16),
             jax.ShapeDtypeStruct((chips, row_count, width), jnp.bfloat16),
         ],
         compiler_params=pltpu.CompilerParams(vmem_limit_bytes=60 * MIB),
@@ -750,7 +750,7 @@
     def chip_sum(kept, sent, chip):
         here = lax.dynamic_index_in_dim(kept, chip, 0, keepdims=False)
         there = lax.dynamic_index_in_dim(sent, chip, 0, keepdims=False)
-        return here + there.astype(jnp.float32)
+        return here.astype(jnp.float32) + there.astype(jnp.float32)
 
     leaving = [chip_sum(kept, sent, (y_id + k) % n_y).astype(jnp.bfloat16) for k in range(1, n_y)]
     leaving, pages, kept, sent = lax.optimization_barrier((leaving, pages, kept, sent))

time: 176 us -> 176 us (level)
  no operation moved by 1% of the time
where the time goes in v6:
time: 176 us; the launch traced here: 175 us
  Pallas kernels  70.7 us (40%)
  blocking collectives  53.2 us (30%)
  starting transfers between devices  23.6 us (13%)
  waiting for transfers between devices  14.6 us (8%)
  local copies, waits for them, and re-layouts  7.48 us (4%)
  other arithmetic  4.92 us (3%)
    all_to_all x2, blocking collectives, in_half(): lax.all_to_all(array, ('tok', 'head'), split_axis=0, concat_axis=0, tiled...  53.2 us
    pallas_call x2, Pallas kernels, expert(): pl.pallas_call(functools.partial(expert_kernel, extras, in_tiles, down),...  33.7 us
    pallas_call x2, Pallas kernels, project(): pl.pallas_call(functools.partial(qkv_kernel, step, chips), grid_spec=pltp...  11.9 us
    pallas_call x1, Pallas kernels, expert_down(): pl.pallas_call(functools.partial(down_kernel, extras, width), grid=(PIECE...  9.5 us
    all_to_all x2, starting transfers between devices, in_half(): lax.all_to_all(array, ('tok', 'head'), split_axis=0, concat_axis=0, tiled...  9.09 us
    pallas_call x1, Pallas kernels, attend(): pl.pallas_call(functools.partial(attend_kernel, row_count, chips), grid_s...  8.18 us
    all_to_all x1, waiting for transfers between devices, per_device(): lax.all_to_all(pages, 'tok', split_axis=0, concat_axis=0, tiled=True)  6.2 us
    all_to_all x2, waiting for transfers between devices, in_half(): lax.all_to_all(array, ('tok', 'head'), split_axis=0, concat_axis=0, tiled...  5.92 us
  transfers between devices with their start and end apart: 12, of which 4 were waited for; matrix products, arithmetic and copies ran while one was open for 5% of the time, Pallas kernels for 23%

profile of v6, /device:TPU:0, one launch (start us, length us, event | category | flops | bytes accessed | tf_op | source)
XLA Modules:
  0.0 175.3 jit_solution(18079605898487898557)
XLA Ops:
  0.7 0.5 collective-permute-start.1
  1.2 2.6 %collective-permute-start = (bf16[64,2880]{1,0:T(8,128)(2,1)}, bf16[64,2880]{1,0:T(8,128)(2,1)S(1)}, u32[]{:S(2)}, u32[]{:S(2)}) collective-permute-start(bf16[64,2880]{1,0:T(8,128)(2,1)} %tokens_ref.1), channel_id=1, source_target_pairs={{0,2},{1,3},{2,0},{3,1},{4,6},{5,7},{6,4},{7,5},{8,10},{9,11},{10,... | collective-permute-start | bytes 1105928 | tf_op jit(solution)/shard_map/ppermute | solution.py:693
  3.8 0.7 reshape.250
  4.6 0.7 convert_bitcast_fusion
  5.2 0.3 convert_reduce_fusion
  5.6 0.7 pad_maximum_fusion.choice_ref
  6.3 0.1 select_reduce_fusion.1
  6.4 0.6 pad_add_fusion.ids_ref
  7.1 0.7 copy-done.6
  7.8 6.0 %project.2 = (bf16[256,1024]{1,0:T(8,128)(2,1)}, bf16[256,256]{1,0:T(8,128)(2,1)}) custom-call(s32[4]{0:T(128)} %pad_add_fusion.ids_ref, s32[4]{0:T(128)} %lengths_ref.9, bf16[64,2880]{1,0:T(8,128)(2,1)} %tokens_ref.1, bf16[64,2880]{1,0:T(8,128)(2,1)} %copy-done.6, f32[2880]{0:T(1024)} %gain_ref.4, bf16[2880,1280]{1,0:T(8,128)(2,1)} %w_ref.3), custom_call_target="tpu_custom_call" | custom-call | flops 943718400 | bytes 7372800 | tf_op jit(solution)/shard_map/project/pallas_call | solution.py:115
  13.8 0.2 collective-permute-start.2
  14.0 0.1 select_reduce_fusion.2
  14.6 2.6 %collective-permute-start.3 = (f32[8,64]{1,0:T(8,128)S(1)}, f32[8,64]{1,0:T(8,128)S(1)}, u32[]{:S(2)}, u32[]{:S(2)}) collective-permute-start(f32[8,64]{1,0:T(8,128)S(1)} %pad_maximum_fusion.choice_ref), channel_id=1, source_target_pairs={{0,16},{1,17},{2,18},{3,19},{4,20},{5,21},{6,22},{7,23},{8,24},{9,... | collective-permute-start | bytes 6152 | tf_op jit(solution)/shard_map/ppermute | solution.py:701
  17.3 0.7 copy-done.7
  18.0 6.0 %project.3 = (bf16[256,1024]{1,0:T(8,128)(2,1)}, bf16[256,256]{1,0:T(8,128)(2,1)}) custom-call(s32[4]{0:T(128)} %pad_add_fusion.ids_ref, s32[4]{0:T(128)} %lengths_ref.9, bf16[64,2880]{1,0:T(8,128)(2,1)} %copy-done.5, bf16[64,2880]{1,0:T(8,128)(2,1)} %copy-done.7, f32[2880]{0:T(1024)} %gain_ref.4, ...), custom_call_target="tpu_custom_call", output_to_operand_aliasing={{0}: (6, {}), {1}: (7, {})} | custom-call | flops 943718400 | bytes 7372800 | tf_op jit(solution)/shard_map/project/pallas_call | solution.py:115
  24.0 0.8 slice.8
  24.8 3.4 %collective-permute-start.4 = (bf16[128,256]{1,0:T(8,128)(2,1)S(1)}, bf16[128,256]{1,0:T(8,128)(2,1)S(1)}, u32[]{:S(2)}, u32[]{:S(2)}) collective-permute-start(bf16[128,256]{1,0:T(8,128)(2,1)S(1)} %slice.8), channel_id=1, source_target_pairs={{0,4},{4,8},{8,12},{12,16},{16,20},{20,24},{24,28},{1,5},{5,9},{9,... | collective-permute-start | bytes 196616 | tf_op jit(solution)/shard_map/ppermute | solution.py:38
  28.3 0.9 reshape.249
  29.2 1.0 slots.2
  30.3 1.0 slots.3
  31.3 1.2 gather_fusion
  32.6 0.6 copy-done.8
  33.2 8.2 %attend.1 = (bf16[2,64,2880]{2,1,0:T(8,128)(2,1)}, bf16[2,64,2880]{2,1,0:T(8,128)(2,1)}) custom-call(s32[4]{0:T(128)} %pad_add_fusion.ids_ref, s32[4]{0:T(128)} %lengths_ref.9, bf16[256,1024]{1,0:T(8,128)(2,1)} %get-tuple-element.60.q_ref, bf16[128,256]{1,0:T(8,128)(2,1)} %copy-done.8, bf16[256,256]{1,0:T(8,128)(2,1)} %get-tuple-element.61.pair_ref, ...), custom_call_target="tpu_custom_call" | custom-call | flops 1509949440 | bytes 5898240 | tf_op jit(solution)/shard_map/attend/pallas_call | solution.py:595
  41.4 2.4 %collective-permute-done.5 = bf16[2,64,2880]{2,1,0:T(8,128)(2,1)S(1)} collective-permute-done((bf16[2,64,2880]{2,1,0:T(8,128)(2,1)}, bf16[2,64,2880]{2,1,0:T(8,128)(2,1)S(1)}, u32[]{:S(2)}, u32[]{:S(2)}) %collective-permute-start.5) | collective-permute-done | bytes 737312 | tf_op jit(solution)/shard_map/ppermute | solution.py:690
  43.8 1.1 fusion
  44.9 1.2 collective-permute-start.6
  46.0 3.4 %all-to-all-start.2 = ((bf16[8,64,128]{2,1,0:T(8,128)(2,1)}), bf16[8,64,128]{2,1,0:T(8,128)(2,1)S(1)}, u32[]{:S(2)}, u32[]{:S(2)}) async-start(bf16[8,64,128]{2,1,0:T(8,128)(2,1)} %bitcast.15), calls=%async_computation.2 | async-start | bytes 262144 | tf_op jit(solution)/shard_map/all_to_all | solution.py:758
  49.4 1.1 add_bitcast_fusion.own_ref
  50.5 6.2 %all-to-all-done.2 = bf16[8,64,128]{2,1,0:T(8,128)(2,1)S(1)} async-done(((bf16[8,64,128]{2,1,0:T(8,128)(2,1)}), bf16[8,64,128]{2,1,0:T(8,128)(2,1)S(1)}, u32[]{:S(2)}, u32[]{:S(2)}) %all-to-all-start.2) | async-done | bytes 131104 | tf_op jit(solution)/shard_map/all_to_all | solution.py:758
  56.7 0.3 finish_attention.1
  57.0 0.5 collective-permute-start.7
  57.6 1.5 pack.2
  59.1 26.7 %conditional.2 = (bf16[128,3712]{1,0:T(8,128)(2,1)S(1)}) conditional(s32[]{:T(128)} %bitcast.4, () %tuple.36, bf16[128,3712]{1,0:T(8,128)(2,1)} %pack.2), branch_computations={%region_2.3_spmd, %region_3.4_spmd} | conditional | bytes 1900552 | solution.py:773
  59.1 26.7 %all_to_all.23 = bf16[16,8,3712]{2,1,0:T(8,128)(2,1)S(1)} all-to-all(bf16[16,8,3712]{2,1,0:T(8,128)(2,1)} %bitcast.46), channel_id=1, replica_groups={{0,1,2,3,4,5,6,7,8,9,10,11,12,13,14,15},{16,17,18,19,20,21,22,23,24,25,..., dimensions={0} | all-to-all | bytes 1900544 | tf_op jit(solution)/shard_map/cond/branch_1_fun/all_to_all | solution.py:704
  85.7 1.5 pack.3
  87.3 4.5 %all-to-all-start.3 = ((bf16[16,8,3712]{2,1,0:T(8,128)(2,1)}), bf16[16,8,3712]{2,1,0:T(8,128)(2,1)}, u32[]{:S(2)}, u32[]{:S(2)}) async-start(bf16[16,8,3712]{2,1,0:T(8,128)(2,1)} %bitcast.20), calls=%async_computation.3 | async-start | bytes 1900544 | tf_op jit(solution)/shard_map/all_to_all | solution.py:704
  91.8 14.7 %expert_up.1.act_ref = bf16[160,2880]{1,0:T(8,128)(2,1)} custom-call(bf16[128,3712]{1,0:T(8,128)(2,1)S(1)} %get-tuple-element.104.refs_0_, bf16[1,2880,5760]{2,1,0:T(8,128)(2,1)} %refs_1_.3), custom_call_target="tpu_custom_call" | custom-call | flops 5308416000 | bytes 33177600 | tf_op jit(solution)/shard_map/expert_up/pallas_call | solution.py:379
  106.5 0.3 all-to-all-done.3
  106.8 19.0 %expert.1 = bf16[128,3712]{1,0:T(8,128)(2,1)} custom-call(bf16[128,3712]{1,0:T(8,128)(2,1)} %bitcast.21.refs_0_, bf16[1,2880,5760]{2,1,0:T(8,128)(2,1)} %refs_1_.3, bf16[1,2880,2880]{2,1,0:T(8,128)(2,1)} %w_down_ref.1), custom_call_target="tpu_custom_call" | custom-call | flops 7962624000 | bytes 49766400 | tf_op jit(solution)/shard_map/expert/pallas_call | solution.py:379
  125.7 4.6 %all-to-all-start.4 = ((bf16[16,8,3712]{2,1,0:T(8,128)(2,1)}), bf16[16,8,3712]{2,1,0:T(8,128)(2,1)S(1)}, u32[]{:S(2)}, u32[]{:S(2)}) async-start(bf16[16,8,3712]{2,1,0:T(8,128)(2,1)} %bitcast.44), calls=%async_computation.4 | async-start | bytes 1900544 | tf_op jit(solution)/shard_map/all_to_all | solution.py:704
  130.3 9.5 %expert_down.1 = bf16[128,3712]{1,0:T(8,128)(2,1)} custom-call(bf16[160,2880]{1,0:T(8,128)(2,1)} %expert_up.1.act_ref, bf16[1,2880,2880]{2,1,0:T(8,128)(2,1)} %w_down_ref.1), custom_call_target="tpu_custom_call" | custom-call | flops 2654208000 | bytes 16588800 | tf_op jit(solution)/shard_map/expert_down/pallas_call | solution.py:400
  139.8 5.7 %all-to-all-done.4 = bf16[16,8,3712]{2,1,0:T(8,128)(2,1)S(1)} async-done(((bf16[16,8,3712]{2,1,0:T(8,128)(2,1)}), bf16[16,8,3712]{2,1,0:T(8,128)(2,1)S(1)}, u32[]{:S(2)}, u32[]{:S(2)}) %all-to-all-start.4) | async-done | bytes 950304 | tf_op jit(solution)/shard_map/all_to_all | solution.py:704
  145.5 0.6 combine.2
  146.2 0.6 gather_fusion.1
  146.8 0.7 copy.22
  147.5 26.5 %conditional.3 = (bf16[128,3712]{1,0:T(8,128)(2,1)S(1)}) conditional(s32[]{:T(128)} %bitcast.4, () %tuple.30, bf16[128,3712]{1,0:T(8,128)(2,1)} %expert_down.1), branch_computations={%region_4.5_spmd, %region_5.6_spmd} | conditional | bytes 1900552 | solution.py:773
  147.5 26.5 %all_to_all.24 = bf16[16,8,3712]{2,1,0:T(8,128)(2,1)S(1)} all-to-all(bf16[16,8,3712]{2,1,0:T(8,128)(2,1)} %bitcast.47), channel_id=1, replica_groups={{0,1,2,3,4,5,6,7,8,9,10,11,12,13,14,15},{16,17,18,19,20,21,22,23,24,25,..., dimensions={0} | all-to-all | bytes 1900544 | tf_op jit(solution)/shard_map/cond/branch_1_fun/all_to_all | solution.py:704
  173.9 1.4 combine.3
  (41 shorter events, 0.7 us)
Async XLA Ops:
  0.6 56.1 %copy-start = (bf16[64,2880]{1,0:T(8,128)(2,1)S(1)}, bf16[64,2880]{1,0:T(8,128)(2,1)}, u32[]{:S(2)}) copy-start(bf16[64,2880]{1,0:T(8,128)(2,1)} %tokens_ref.1) | copy-start | bytes 1105924
  0.6 28.6 %copy-start.2 = (s32[4]{0:T(128)S(1)}, s32[4]{0:T(128)}, u32[]{:S(2)}) copy-start(s32[4]{0:T(128)} %lengths_ref.9) | copy-start | bytes 52
  0.7 56.9 %copy-start.3 = (s32[4]{0:T(128)S(1)}, s32[4]{0:T(128)}, u32[]{:S(2)}) copy-start(s32[4]{0:T(128)} %lengths_ref.9) | copy-start | bytes 52
  0.7 56.1 %copy-start.4 = (f32[2880]{0:T(1024)S(1)}, f32[2880]{0:T(1024)}, u32[]{:S(2)}) copy-start(f32[2880]{0:T(1024)} %gain_ref.5) | copy-start | bytes 34564
  0.7 6.4 %collective-permute-start.1 = (bf16[64,2880]{1,0:T(8,128)(2,1)}, bf16[64,2880]{1,0:T(8,128)(2,1)S(1)}, u32[]{:S(2)}, u32[]{:S(2)}) collective-permute-start(bf16[64,2880]{1,0:T(8,128)(2,1)} %tokens_ref.1), channel_id=1, source_target_pairs={{0,1},{1,0},{2,3},{3,2},{4,5},{5,4},{6,7},{7,6},{8,9},{9,8},{10,11... | collective-permute-start | bytes 1105928 | tf_op jit(solution)/shard_map/ppermute | solution.py:690
  1.2 12.6 %collective-permute-start = (bf16[64,2880]{1,0:T(8,128)(2,1)}, bf16[64,2880]{1,0:T(8,128)(2,1)S(1)}, u32[]{:S(2)}, u32[]{:S(2)}) collective-permute-start(bf16[64,2880]{1,0:T(8,128)(2,1)} %tokens_ref.1), channel_id=1, source_target_pairs={{0,2},{1,3},{2,0},{3,1},{4,6},{5,7},{6,4},{7,5},{8,10},{9,11},{10,... | collective-permute-start | bytes 1105928 | tf_op jit(solution)/shard_map/ppermute | solution.py:693
  7.1 22.2 %copy-start.1 = (s32[4]{0:T(128)S(1)}, s32[4]{0:T(128)}, u32[]{:S(2)}) copy-start(s32[4]{0:T(128)} %pad_add_fusion.ids_ref) | copy-start | bytes 52
  7.1 0.7 copy-start.6
  13.8 3.5 %copy-start.5 = (bf16[64,2880]{1,0:T(8,128)(2,1)}, bf16[64,2880]{1,0:T(8,128)(2,1)S(1)}, u32[]{:S(2)}) copy-start(bf16[64,2880]{1,0:T(8,128)(2,1)S(1)} %collective-permute-done.own_ref) | copy-start | bytes 1105924
  13.8 3.5 %collective-permute-start.2 = (bf16[64,2880]{1,0:T(8,128)(2,1)S(1)}, bf16[64,2880]{1,0:T(8,128)(2,1)S(1)}, u32[]{:S(2)}, u32[]{:S(2)}) collective-permute-start(bf16[64,2880]{1,0:T(8,128)(2,1)S(1)} %collective-permute-done.own_ref), channel_id=1, source_target_pairs={{0,1},{1,0},{2,3},{3,2},{4,5},{5,4},{6,7},{7,6},{8,9},{9,8},{10,11... | collective-permute-start | bytes 1105928 | tf_op jit(solution)/shard_map/ppermute | solution.py:690
  14.6 9.4 %collective-permute-start.3 = (f32[8,64]{1,0:T(8,128)S(1)}, f32[8,64]{1,0:T(8,128)S(1)}, u32[]{:S(2)}, u32[]{:S(2)}) collective-permute-start(f32[8,64]{1,0:T(8,128)S(1)} %pad_maximum_fusion.choice_ref), channel_id=1, source_target_pairs={{0,16},{1,17},{2,18},{3,19},{4,20},{5,21},{6,22},{7,23},{8,24},{9,... | collective-permute-start | bytes 6152 | tf_op jit(solution)/shard_map/ppermute | solution.py:701
  17.3 0.7 copy-start.7
  24.8 7.7 %collective-permute-start.4 = (bf16[128,256]{1,0:T(8,128)(2,1)S(1)}, bf16[128,256]{1,0:T(8,128)(2,1)S(1)}, u32[]{:S(2)}, u32[]{:S(2)}) collective-permute-start(bf16[128,256]{1,0:T(8,128)(2,1)S(1)} %slice.8), channel_id=1, source_target_pairs={{0,4},{4,8},{8,12},{12,16},{16,20},{20,24},{24,28},{1,5},{5,9},{9,... | collective-permute-start | bytes 196616 | tf_op jit(solution)/shard_map/ppermute | solution.py:38
  32.6 0.6 copy-start.8
  41.4 2.4 %collective-permute-start.5 = (bf16[2,64,2880]{2,1,0:T(8,128)(2,1)}, bf16[2,64,2880]{2,1,0:T(8,128)(2,1)S(1)}, u32[]{:S(2)}, u32[]{:S(2)}) collective-permute-start(bf16[2,64,2880]{2,1,0:T(8,128)(2,1)} %get-tuple-element.70), channel_id=1, source_target_pairs={{0,1},{1,0},{2,3},{3,2},{4,5},{5,4},{6,7},{7,6},{8,9},{9,8},{10,11... | collective-permute-start | bytes 2211848 | tf_op jit(solution)/shard_map/ppermute | solution.py:690
  44.9 11.8 %collective-permute-start.6 = (bf16[64,2880]{1,0:T(8,128)(2,1)S(1)}, bf16[64,2880]{1,0:T(8,128)(2,1)S(1)}, u32[]{:S(2)}, u32[]{:S(2)}) collective-permute-start(bf16[64,2880]{1,0:T(8,128)(2,1)S(1)} %fusion), channel_id=1, source_target_pairs={{0,2},{1,3},{2,0},{3,1},{4,6},{5,7},{6,4},{7,5},{8,10},{9,11},{10,... | collective-permute-start | bytes 1105928 | tf_op jit(solution)/shard_map/ppermute | solution.py:693
  46.0 10.7 %all-to-all-start.2 = ((bf16[8,64,128]{2,1,0:T(8,128)(2,1)}), bf16[8,64,128]{2,1,0:T(8,128)(2,1)S(1)}, u32[]{:S(2)}, u32[]{:S(2)}) async-start(bf16[8,64,128]{2,1,0:T(8,128)(2,1)} %bitcast.15), calls=%async_computation.2 | async-start | bytes 262144 | tf_op jit(solution)/shard_map/all_to_all | solution.py:758
  57.0 28.7 %collective-permute-start.7 = (bf16[64,2880]{1,0:T(8,128)(2,1)S(1)}, bf16[64,2880]{1,0:T(8,128)(2,1)S(1)}, u32[]{:S(2)}, u32[]{:S(2)}) collective-permute-start(bf16[64,2880]{1,0:T(8,128)(2,1)S(1)} %get-tuple-element.77.moe_ref), channel_id=1, source_target_pairs={{0,16},{1,17},{2,18},{3,19},{4,20},{5,21},{6,22},{7,23},{8,24},{9,... | collective-permute-start | bytes 1105928 | tf_op jit(solution)/shard_map/ppermute | solution.py:701
  87.3 19.5 %all-to-all-start.3 = ((bf16[16,8,3712]{2,1,0:T(8,128)(2,1)}), bf16[16,8,3712]{2,1,0:T(8,128)(2,1)}, u32[]{:S(2)}, u32[]{:S(2)}) async-start(bf16[16,8,3712]{2,1,0:T(8,128)(2,1)} %bitcast.20), calls=%async_computation.3 | async-start | bytes 1900544 | tf_op jit(solution)/shard_map/all_to_all | solution.py:704
  125.7 19.8 %all-to-all-start.4 = ((bf16[16,8,3712]{2,1,0:T(8,128)(2,1)}), bf16[16,8,3712]{2,1,0:T(8,128)(2,1)S(1)}, u32[]{:S(2)}, u32[]{:S(2)}) async-start(bf16[16,8,3712]{2,1,0:T(8,128)(2,1)} %bitcast.44), calls=%async_computation.4 | async-start | bytes 1900544 | tf_op jit(solution)/shard_map/all_to_all | solution.py:704
  146.1 27.8 %collective-permute-start.8 = (bf16[64,2880]{1,0:T(8,128)(2,1)S(1)}, bf16[64,2880]{1,0:T(8,128)(2,1)S(1)}, u32[]{:S(2)}, u32[]{:S(2)}) collective-permute-start(bf16[64,2880]{1,0:T(8,128)(2,1)S(1)} %combine.2), channel_id=1, source_target_pairs={{0,16},{1,17},{2,18},{3,19},{4,20},{5,21},{6,22},{7,23},{8,24},{9,... | collective-permute-start | bytes 1105928 | tf_op jit(solution)/shard_map/ppermute | solution.py:701
